TPU v7x, 32 devices: a whole 2x2x4 slice. The times are simulated.
32 devices in a mesh: doc: 16 (over z, x, core), half: 2 (over y).
Axes of the slice: x: 2, y: 2, z: 4, core: 2. Of those that a mesh axis runs over, the one named last changes fastest.
Arguments:
- hidden_in: bfloat16 [64, 512, 768], P('doc', 'half'), may hold values from -6 to 6
- boxes: int32 [4, 64, 512], P(None, 'doc', 'half'), may hold values from 0 to 1000, as said below
- lengths: int32 [64], P('doc'), may hold values from 128 to 512, as said below
- box_weight: bfloat16 [128, 768], replicated, may hold values from -0.5 to 0.5
- qkv_weight: bfloat16 [768, 2304], replicated, may hold values from -0.21875 to 0.21875
- qv_bias: float32 [2, 768], replicated, may hold values from -3 to 3
- out_weight: bfloat16 [768, 768], replicated, may hold values from -0.875 to 0.875
- out_bias: float32 [768], replicated, may hold values from -3 to 3
- rel_tables: float32 [32, 36], replicated, may hold values from -4 to 4
- norm_one: float32 [2, 768], replicated, may hold values from -0.5 to 1.4, as said below
- ffn_in_weight: bfloat16 [768, 3072], replicated, may hold values from -0.21875 to 0.21875
- ffn_in_bias: float32 [3072], replicated, may hold values from -3 to 3
- ffn_out_weight: bfloat16 [3072, 768], replicated, may hold values from -0.15625 to 0.15625
- ffn_out_bias: float32 [768], replicated, may hold values from -3 to 3
- norm_two: float32 [2, 768], replicated, may hold values from -0.5 to 1.4, as said below
- cotangent: bfloat16 [64, 512, 768], P('doc', 'half'), may hold values from -6 to 6
Outputs:
- layer_out: bfloat16 [64, 512, 768], P('doc', 'half')
- hidden_grad: bfloat16 [64, 512, 768], P('doc', 'half')
- box_weight_grad: float32 [128, 768], P('half')
- qkv_weight_grad: float32 [768, 2304], P('half')
- qv_bias_grad: float32 [2, 768], P('half')
- out_weight_grad: float32 [768, 768], P('half')
- out_bias_grad: float32 [768], P('half')
- rel_tables_grad: float32 [32, 36], P('half')
- norm_one_grad: float32 [2, 768], P('half')
- ffn_in_weight_grad: float32 [768, 3072], P('half')
- ffn_in_bias_grad: float32 [3072], P('half')
- ffn_out_weight_grad: float32 [3072, 768], P('half')
- ffn_out_bias_grad: float32 [768], P('half')
- norm_two_grad: float32 [2, 768], P('half')
Inputs may be any that keep to these rules, and one draw needn't show every extreme that they name: `boxes`: rows hold x0, y0, x1, y1 with x1 > x0 and y1 > y0. `lengths`: tokens at positions at or past a window's length are padding. In every aligned run of 4 windows one window has length 512. `norm_one`: row 0 is a gain, row 1 a shift. `norm_two`: row 0 is a gain, row 1 a shift.
All inputs are finite; a program needn't handle non-finite values.
Results may differ from a plain program's by a relative error of at most 0.019.
Values may be sent and summed in bfloat16 or wider, within the bound.
No kernel may reach another device: no remote copies, remote signals or barrier semaphores. Data moves between devices by JAX's collectives and lax.ppermute only.
A program may use at most 256 MiB of HBM per device.

v0:
```python
from functools import partial
import math

import jax
import jax.numpy as jnp
from jax import lax
from jax.sharding import PartitionSpec as P

H = 12
DH = 64
BOXF = 128
NB = 32


epsilon = 1e-05
highest = lax.Precision.HIGHEST
thresholds = (1, 2, 3, 4, 5, 6, 7, 8, 12, 16, 24, 32, 48, 64, 96)


def bucket_of(offset, step_size):
    magnitude = jnp.abs(offset) // step_size
    counter = jnp.zeros(offset.shape, jnp.int32)
    for bound_value in thresholds:
        counter = counter + (magnitude >= bound_value).astype(jnp.int32)
    return counter + 16 * (offset > 0).astype(jnp.int32)


def box_features(boxes):
    coords = jnp.moveaxis(boxes, 0, -1).astype(jnp.float32)
    freq_count = BOXF // 8
    frequencies = 1000.0 ** (-jnp.arange(freq_count, dtype=jnp.float32) / freq_count)
    angles = coords[..., None] * frequencies
    sin_cos = jnp.stack([jnp.sin(angles), jnp.cos(angles)], axis=-2)
    return sin_cos.reshape(coords.shape[:-1] + (BOXF,))


def exact_gelu(inputs):
    return jax.nn.gelu(inputs, approximate=False)


def norm_forward(summed, params):
    centered = summed - jnp.mean(summed, -1, keepdims=True)
    inverse = lax.rsqrt(jnp.mean(centered * centered, -1, keepdims=True) + epsilon)
    normed = centered * inverse
    return (normed * params[0] + params[1], normed, inverse)


def norm_backward(upstream, normed, inverse, params):
    scaled = upstream * params[0]
    inner_grad = inverse * (
        scaled
        - jnp.mean(scaled, -1, keepdims=True)
        - normed * jnp.mean(scaled * normed, -1, keepdims=True)
    )
    param_grad = jnp.stack([jnp.sum(upstream * normed, 0), jnp.sum(upstream, 0)])
    return (inner_grad, param_grad)


def bucket_maps(query_boxes, key_boxes, first_row, query_count, key_count):
    rows_here = first_row + jnp.arange(query_count, dtype=jnp.int32)
    columns = jnp.arange(key_count, dtype=jnp.int32)
    line_bucket = bucket_of(columns[None, :] - rows_here[:, None], 1)
    across_bucket = bucket_of(key_boxes[0][:, None, :] - query_boxes[0][:, :, None], 4)
    down_bucket = bucket_of(key_boxes[1][:, None, :] - query_boxes[1][:, :, None], 4)
    return (line_bucket, across_bucket, down_bucket)


def one_hot(buckets, dtype):
    return (buckets[..., None] == jnp.arange(NB, dtype=jnp.int32)).astype(dtype)


def scores_of(rel_tables, first_row, queries, keys_all, query_boxes, key_boxes, lengths):
    line_bucket, across_bucket, down_bucket = bucket_maps(
        query_boxes, key_boxes, first_row, queries.shape[1], keys_all.shape[1]
    )
    raw_scores = jnp.einsum(
        "gihd,gjhd->ghij", queries, keys_all, preferred_element_type=jnp.float32
    ) * DH ** (-0.5)
    raw_scores = raw_scores + jnp.einsum(
        "ijb,bh->hij", one_hot(line_bucket, jnp.float32), rel_tables[:, :H], precision=highest
    )
    raw_scores = raw_scores + jnp.einsum(
        "gijb,bh->ghij",
        one_hot(across_bucket, jnp.float32),
        rel_tables[:, H : 2 * H],
        precision=highest,
    )
    raw_scores = raw_scores + jnp.einsum(
        "gijb,bh->ghij",
        one_hot(down_bucket, jnp.float32),
        rel_tables[:, 2 * H :],
        precision=highest,
    )
    columns = jnp.arange(keys_all.shape[1], dtype=jnp.int32)
    key_valid = columns[None, :] < lengths[:, None]
    return (
        jnp.where(key_valid[:, None, None, :], raw_scores, -1000000000.0),
        (line_bucket, across_bucket, down_bucket),
    )


def attend_group(rel_tables, first_row, packed):
    queries, keys_all, values_all, query_boxes, key_boxes, lengths = packed
    scores, unused = scores_of(
        rel_tables, first_row, queries, keys_all, query_boxes, key_boxes, lengths
    )
    row_max = jnp.max(scores, -1, keepdims=True)
    exps = jnp.exp(scores - row_max)
    row_total = jnp.sum(exps, -1, keepdims=True)
    probabilities = (exps / row_total).astype(jnp.bfloat16)
    attended = jnp.einsum(
        "ghij,gjhd->gihd", probabilities, values_all, preferred_element_type=jnp.float32
    )
    return (attended, (row_max + jnp.log(row_total))[..., 0])


def attend_back(rel_tables, first_row, packed):
    queries, keys_all, values_all, query_boxes, key_boxes, lengths, logsum, upstream = packed
    scores, buckets = scores_of(
        rel_tables, first_row, queries, keys_all, query_boxes, key_boxes, lengths
    )
    probabilities = jnp.exp(scores - logsum[..., None])
    dprobs = jnp.einsum("gihd,gjhd->ghij", upstream, values_all, preferred_element_type=jnp.float32)
    dvalues = jnp.einsum(
        "ghij,gihd->gjhd",
        probabilities.astype(jnp.bfloat16),
        upstream,
        preferred_element_type=jnp.float32,
    )
    center = jnp.sum(dprobs * probabilities, -1, keepdims=True)
    dscores = (probabilities * (dprobs - center)).astype(jnp.bfloat16)
    dqueries = jnp.einsum(
        "ghij,gjhd->gihd", dscores, keys_all, preferred_element_type=jnp.float32
    ) * DH ** (-0.5)
    dkey_part = jnp.einsum(
        "ghij,gihd->gjhd", dscores, queries, preferred_element_type=jnp.float32
    ) * DH ** (-0.5)
    line_grad = jnp.einsum(
        "ijb,ghij->bh",
        one_hot(buckets[0], jnp.bfloat16),
        dscores,
        preferred_element_type=jnp.float32,
    )
    across_grad = jnp.einsum(
        "gijb,ghij->bh",
        one_hot(buckets[1], jnp.bfloat16),
        dscores,
        preferred_element_type=jnp.float32,
    )
    down_grad = jnp.einsum(
        "gijb,ghij->bh",
        one_hot(buckets[2], jnp.bfloat16),
        dscores,
        preferred_element_type=jnp.float32,
    )
    table_part = jnp.concatenate([line_grad, across_grad, down_grad], axis=1)
    return (dqueries, dkey_part, dvalues, table_part)


def shards(
    hidden_in,
    boxes,
    lengths,
    box_weight,
    qkv_weight,
    qv_bias,
    out_weight,
    out_bias,
    rel_tables,
    norm_one,
    ffn_in_weight,
    ffn_in_bias,
    ffn_out_weight,
    ffn_out_bias,
    norm_two,
    cotangent,
):
    hidden_here, cotangent_here, boxes_here, lengths_here = (hidden_in, cotangent, boxes, lengths)
    first_row = lax.axis_index("half") * hidden_in.shape[1]
    windows, local_len, width = hidden_here.shape
    features = box_features(boxes_here).astype(jnp.bfloat16).reshape(-1, BOXF)
    token_rows = hidden_here.astype(jnp.float32).reshape(-1, width)
    entry_sum = token_rows + jnp.dot(features, box_weight, preferred_element_type=jnp.float32)
    entry_low = entry_sum.astype(jnp.bfloat16)
    projected = jnp.dot(entry_low, qkv_weight, preferred_element_type=jnp.float32)
    queries = (projected[:, :width] + qv_bias[0]).astype(jnp.bfloat16)
    key_rows = projected[:, width : 2 * width].astype(jnp.bfloat16)
    values = (projected[:, 2 * width :] + qv_bias[1]).astype(jnp.bfloat16)
    key_shape = (windows, local_len, width)
    keys_all, values_all = (
        lax.all_gather(key_rows.reshape(key_shape), "half", axis=1, tiled=True),
        lax.all_gather(values.reshape(key_shape), "half", axis=1, tiled=True),
    )
    key_boxes = lax.all_gather(boxes_here, "half", axis=2, tiled=True)
    seq_len = keys_all.shape[1]
    group_size = math.gcd(windows, max(1, 512 // local_len))
    group_count = windows // group_size
    grouped_queries = queries.reshape(group_count, group_size, local_len, H, DH)
    grouped_keys = keys_all.reshape(group_count, group_size, seq_len, H, DH)
    grouped_values = values_all.reshape(group_count, group_size, seq_len, H, DH)
    grouped_qboxes = jnp.moveaxis(boxes_here.reshape(4, group_count, group_size, local_len), 1, 0)
    grouped_kboxes = jnp.moveaxis(key_boxes.reshape(4, group_count, group_size, seq_len), 1, 0)
    grouped_lengths = lengths_here.reshape(group_count, group_size)
    packed = (
        grouped_queries,
        grouped_keys,
        grouped_values,
        grouped_qboxes,
        grouped_kboxes,
        grouped_lengths,
    )
    attended, logsum = lax.map(partial(attend_group, rel_tables, first_row), packed)
    heads_low = attended.reshape(-1, width).astype(jnp.bfloat16)
    branch = jnp.dot(heads_low, out_weight, preferred_element_type=jnp.float32) + out_bias
    second, normed_one, inverse_one = norm_forward(entry_sum + branch, norm_one)
    second_low = second.astype(jnp.bfloat16)
    inner_pre = jnp.dot(second_low, ffn_in_weight, preferred_element_type=jnp.float32) + ffn_in_bias
    active, gelu_back = jax.vjp(exact_gelu, inner_pre)
    active_low = active.astype(jnp.bfloat16)
    outer_pre = (
        jnp.dot(active_low, ffn_out_weight, preferred_element_type=jnp.float32) + ffn_out_bias
    )
    result, normed_two, inverse_two = norm_forward(second + outer_pre, norm_two)
    layer_here = result.astype(jnp.bfloat16).reshape(hidden_here.shape)
    upstream = cotangent_here.astype(jnp.float32).reshape(-1, width)
    d_sum_two, norm_two_grad = norm_backward(upstream, normed_two, inverse_two, norm_two)
    d_outer = d_sum_two.astype(jnp.bfloat16)
    ffn_out_bias_grad = jnp.sum(d_outer.astype(jnp.float32), 0)
    ffn_out_weight_grad = jnp.dot(active_low.T, d_outer, preferred_element_type=jnp.float32)
    d_active = jnp.dot(d_outer, ffn_out_weight.T, preferred_element_type=jnp.float32)
    d_inner = gelu_back(d_active)[0].astype(jnp.bfloat16)
    ffn_in_bias_grad = jnp.sum(d_inner.astype(jnp.float32), 0)
    ffn_in_weight_grad = jnp.dot(second_low.T, d_inner, preferred_element_type=jnp.float32)
    d_second = d_sum_two + jnp.dot(d_inner, ffn_in_weight.T, preferred_element_type=jnp.float32)
    d_sum_one, norm_one_grad = norm_backward(d_second, normed_one, inverse_one, norm_one)
    d_branch = d_sum_one.astype(jnp.bfloat16)
    out_bias_grad = jnp.sum(d_branch.astype(jnp.float32), 0)
    out_weight_grad = jnp.dot(heads_low.T, d_branch, preferred_element_type=jnp.float32)
    d_heads = jnp.dot(d_branch, out_weight.T, preferred_element_type=jnp.float32).astype(
        jnp.bfloat16
    )
    grouped_upstream = d_heads.reshape(group_count, group_size, local_len, H, DH)

    def back_step(table_sum, packed_back):
        dqueries, dkey_part, dvalues, table_part = attend_back(rel_tables, first_row, packed_back)
        return (table_sum + table_part, (dqueries, dkey_part, dvalues))

    table_start = jnp.zeros((NB, 3 * H), jnp.float32)
    rel_tables_grad, (d_queries, d_keys, d_values) = lax.scan(
        back_step, table_start, packed + (logsum, grouped_upstream)
    )
    full_shape = (windows, seq_len, width)
    key_grad, value_grad = (
        lax.psum_scatter(
            d_keys.reshape(full_shape).astype(jnp.bfloat16), "half", scatter_dimension=1, tiled=True
        ).astype(jnp.float32),
        lax.psum_scatter(
            d_values.reshape(full_shape).astype(jnp.bfloat16),
            "half",
            scatter_dimension=1,
            tiled=True,
        ).astype(jnp.float32),
    )
    query_low = d_queries.reshape(-1, width).astype(jnp.bfloat16)
    key_low = key_grad.reshape(-1, width).astype(jnp.bfloat16)
    value_low = value_grad.reshape(-1, width).astype(jnp.bfloat16)
    qv_bias_grad = jnp.stack(
        [jnp.sum(query_low.astype(jnp.float32), 0), jnp.sum(value_low.astype(jnp.float32), 0)]
    )
    d_projected = jnp.concatenate([query_low, key_low, value_low], axis=1)
    qkv_weight_grad = jnp.dot(entry_low.T, d_projected, preferred_element_type=jnp.float32)
    d_entry = d_sum_one + jnp.dot(d_projected, qkv_weight.T, preferred_element_type=jnp.float32)
    entry_grad_low = d_entry.astype(jnp.bfloat16)
    grad_here = entry_grad_low.reshape(hidden_here.shape)
    box_weight_grad = jnp.dot(features.T, entry_grad_low, preferred_element_type=jnp.float32)
    layer_out, hidden_grad = (layer_here, grad_here)
    shares = (
        lax.psum_scatter(
            box_weight_grad.astype(jnp.bfloat16), "half", scatter_dimension=0, tiled=True
        ).astype(jnp.float32),
        lax.psum_scatter(
            qkv_weight_grad.astype(jnp.bfloat16), "half", scatter_dimension=0, tiled=True
        ).astype(jnp.float32),
        lax.psum_scatter(
            qv_bias_grad.astype(jnp.bfloat16), "half", scatter_dimension=0, tiled=True
        ).astype(jnp.float32),
        lax.psum_scatter(
            out_weight_grad.astype(jnp.bfloat16), "half", scatter_dimension=0, tiled=True
        ).astype(jnp.float32),
        lax.psum_scatter(
            out_bias_grad.astype(jnp.bfloat16), "half", scatter_dimension=0, tiled=True
        ).astype(jnp.float32),
        lax.psum_scatter(
            rel_tables_grad.astype(jnp.bfloat16), "half", scatter_dimension=0, tiled=True
        ).astype(jnp.float32),
        lax.psum_scatter(
            norm_one_grad.astype(jnp.bfloat16), "half", scatter_dimension=0, tiled=True
        ).astype(jnp.float32),
        lax.psum_scatter(
            ffn_in_weight_grad.astype(jnp.bfloat16), "half", scatter_dimension=0, tiled=True
        ).astype(jnp.float32),
        lax.psum_scatter(
            ffn_in_bias_grad.astype(jnp.bfloat16), "half", scatter_dimension=0, tiled=True
        ).astype(jnp.float32),
        lax.psum_scatter(
            ffn_out_weight_grad.astype(jnp.bfloat16), "half", scatter_dimension=0, tiled=True
        ).astype(jnp.float32),
        lax.psum_scatter(
            ffn_out_bias_grad.astype(jnp.bfloat16), "half", scatter_dimension=0, tiled=True
        ).astype(jnp.float32),
        lax.psum_scatter(
            norm_two_grad.astype(jnp.bfloat16), "half", scatter_dimension=0, tiled=True
        ).astype(jnp.float32),
    )
    summed = lax.psum(
        (
            shares[0],
            shares[1],
            shares[2],
            shares[3],
            shares[4],
            shares[5],
            shares[6],
            shares[7],
            shares[8],
            shares[9],
            shares[10],
            shares[11],
        ),
        "doc",
    )
    return (
        layer_out,
        hidden_grad,
        summed[0],
        summed[1],
        summed[2],
        summed[3],
        summed[4],
        summed[5],
        summed[6],
        summed[7],
        summed[8],
        summed[9],
        summed[10],
        summed[11],
    )


def solution(mesh):
    return jax.shard_map(
        shards,
        mesh=mesh,
        in_specs=(
            P("doc", "half", None),
            P(None, "doc", "half"),
            P("doc"),
            P(),
            P(),
            P(),
            P(),
            P(),
            P(),
            P(),
            P(),
            P(),
            P(),
            P(),
            P(),
            P("doc", "half", None),
        ),
        out_specs=(
            P("doc", "half", None),
            P("doc", "half", None),
            P("half", None),
            P("half", None),
            P("half", None),
            P("half", None),
            P("half"),
            P("half", None),
            P("half", None),
            P("half", None),
            P("half"),
            P("half", None),
            P("half"),
            P("half", None),
        ),
        check_vma=False,
    )
```

profile of v0, /device:TPU:1, one launch (start us, length us, event | category | flops | bytes accessed | tf_op | source)
XLA Modules:
  0.0 1346.3 jit_solution(11451168982236275476)
XLA Ops:
  51.7 19.7 %all-gather.3.cloned.1.call-done = bf16[4,512,768]{2,1,0:T(8,128)(2,1)} async-done(((bf16[4,256,768]{2,1,0:T(8,128)(2,1)}), bf16[4,512,768]{2,1,0:T(8,128)(2,1)}) %all-gather.3.cloned.1.call-update) | async-done | bytes 3145744 | tf_op jit(solution)/shard_map/all_gather | solution.py:192
  76.0 42.4 %all-gather.5.cloned.1.call-done = bf16[4,512,768]{2,1,0:T(8,128)(2,1)} async-done(((bf16[4,256,768]{2,1,0:T(8,128)(2,1)}), bf16[4,512,768]{2,1,0:T(8,128)(2,1)}) %all-gather.5.cloned.1.call-update) | async-done | bytes 3145744 | tf_op jit(solution)/shard_map/all_gather | solution.py:191
  124.4 192.6 %while.35 = (s32[]{:T(128)}, bf16[2,2,256,12,64]{2,4,3,1,0:T(8,128)(2,1)}, f32[2,2,12,256]{3,2,1,0:T(8,128)}, bf16[2,2,512,12,64]{2,4,3,1,0:T(8,128)(2,1)}, s32[...) while((s32[]{:T(128)}, ...), condition=%wide.region_3.4_spmd, body=%wide.region_0.3_spmd.sunk | while | flops 3920751872 | bytes 183104288 | solution.py:212
  130.6 15.1 %fusion.246 = f32[2,256,512,12]{2,3,1,0:T(8,128)} fusion(s32[2,256,512]{2,1,0:T(8,128)S(1)} %get-tuple-element.872, f32[32,36]{0,1:T(8,128)} %get-tuple-element.937), kind=kOutput, calls=%fused_computation.3.clone.1 | convolution fusion | flops 1216348160 | bytes 13639680 | tf_op jit(solution)/shard_map/while/body/eval_jaxpr/gijb,bh->ghij/dot_general | solution.py:88
  145.7 14.4 %fusion.247 = f32[2,256,512,12]{2,3,1,0:T(8,128)} fusion(s32[2,256,512]{2,1,0:T(8,128)S(1)} %get-tuple-element.873, f32[32,36]{0,1:T(8,128)S(1)} %copy-done.18), kind=kOutput, calls=%fused_computation.2.clone.1 | convolution fusion | flops 1216348160 | bytes 13639680 | tf_op jit(solution)/shard_map/while/body/eval_jaxpr/gijb,bh->ghij/dot_general | solution.py:82
  173.3 31.6 %fusion.250 = (f32[2,12,256]{2,1,0:T(8,128)}, f32[2,12,256,512]{3,2,1,0:T(8,128)}) fusion(f32[2,256,512,12]{2,3,1,0:T(8,128)} %fusion.246, f32[2,256,512,12]{2,3,1,0:T(8,128)} %fusion.247, f32[12,256,512]{2,1,0:T(8,128)} %copy.177, bf16[2,2,512,12,64]{2,4,3,1,0:T(8,128)(2,1)} %get-tuple-element.935, s32[]{:T(128)} %get-tuple-element.915, ...), kind=kOutput, calls=%fused_computation.304.clone.1 | convolution fusion | flops 421521408 | bytes 54814720 | tf_op jit(solution)/shard_map/while/body/eval_jaxpr/gihd,gjhd->ghij/dot_general | solution.py:76
  225.0 15.3 %fusion.246 = f32[2,256,512,12]{2,3,1,0:T(8,128)} fusion(s32[2,256,512]{2,1,0:T(8,128)S(1)} %get-tuple-element.872, f32[32,36]{0,1:T(8,128)} %get-tuple-element.937), kind=kOutput, calls=%fused_computation.3.clone.1 | convolution fusion | flops 1216348160 | bytes 13639680 | tf_op jit(solution)/shard_map/while/body/eval_jaxpr/gijb,bh->ghij/dot_general | solution.py:88
  240.3 14.2 %fusion.247 = f32[2,256,512,12]{2,3,1,0:T(8,128)} fusion(s32[2,256,512]{2,1,0:T(8,128)S(1)} %get-tuple-element.873, f32[32,36]{0,1:T(8,128)S(1)} %copy-done.18), kind=kOutput, calls=%fused_computation.2.clone.1 | convolution fusion | flops 1216348160 | bytes 13639680 | tf_op jit(solution)/shard_map/while/body/eval_jaxpr/gijb,bh->ghij/dot_general | solution.py:82
  267.5 31.6 %fusion.250 = (f32[2,12,256]{2,1,0:T(8,128)}, f32[2,12,256,512]{3,2,1,0:T(8,128)}) fusion(f32[2,256,512,12]{2,3,1,0:T(8,128)} %fusion.246, f32[2,256,512,12]{2,3,1,0:T(8,128)} %fusion.247, f32[12,256,512]{2,1,0:T(8,128)} %copy.177, bf16[2,2,512,12,64]{2,4,3,1,0:T(8,128)(2,1)} %get-tuple-element.935, s32[]{:T(128)} %get-tuple-element.915, ...), kind=kOutput, calls=%fused_computation.304.clone.1 | convolution fusion | flops 421521408 | bytes 54814720 | tf_op jit(solution)/shard_map/while/body/eval_jaxpr/gihd,gjhd->ghij/dot_general | solution.py:76
  330.7 38.1 %multiply_convert_fusion.1 = (bf16[1024,3072]{1,0:T(8,128)(2,1)S(1)}, f32[1024,3072]{1,0:T(8,128)}, f32[1024,3072]{1,0:T(8,128)}) fusion(f32[3072]{0:T(1024)S(1)} %copy-done.41, bf16[768,3072]{1,0:T(8,128)(2,1)} %param.30, f32[1024,768]{1,0:T(8,128)S(1)} %get-tuple-element.696, f32[768]{0:T(1024)S(1)} %copy-done.38, f32[768]{0:T(1024)S(1)} %copy-done.31, ...), kind=kOutput, calls=%fused_computation.211 | convolution fusion | flops 5043388416 | bytes 39348224 | tf_op jit(solution)/shard_map/dot_general | solution.py:217
  382.0 19.3 %fusion.184 = (bf16[3072]{0:T(1024)(128)(2,1)}, bf16[1024,3072]{1,0:T(8,128)(2,1)}) fusion(f32[1024,3072]{1,0:T(8,128)} %get-tuple-element.671, bf16[3072,768]{1,0:T(8,128)(2,1)} %param.32, f32[1024,768]{1,0:T(8,128)} %get-tuple-element.667, f32[1024,3072]{1,0:T(8,128)} %get-tuple-element.697, f32[3072]{0:T(1024)S(1)} %copy-done.41), kind=kOutput, calls=%fused_computation.307 | convolution fusion | flops 4882953216 | bytes 39340032 | tf_op jit(solution)/shard_map/dot_general | solution.py:230
  426.8 290.0 %while.36 = (s32[]{:T(128)}, f32[32,36]{0,1:T(8,128)}, bf16[2,2,256,12,64]{2,4,3,1,0:T(8,128)(2,1)}, bf16[2,2,512,12,64]{2,4,3,1,0:T(8,128)(2,1)}, bf16[2,2,512,...) while((s32[]{:T(128)}, f32[32,36]{0,1:T(8,128)}, ...), condition=%wide.region_15.16_spmd.clone, body=%wide.region_12.15_spmd.clone.sunk | while | flops 5662047744 | bytes 322347712 | solution.py:249
  433.3 15.1 %fusion.266 = f32[2,256,512,12]{2,3,1,0:T(8,128)} fusion(s32[2,256,512]{2,1,0:T(8,128)S(1)} %get-tuple-element.895, f32[32,36]{0,1:T(8,128)} %get-tuple-element.988), kind=kOutput, calls=%fused_computation.92.clone.1 | convolution fusion | flops 1216348160 | bytes 13639680 | tf_op jit(solution)/shard_map/while/body/eval_jaxpr/gijb,bh->ghij/dot_general | solution.py:88
  448.4 14.2 %fusion.267 = f32[2,256,512,12]{2,3,1,0:T(8,128)} fusion(s32[2,256,512]{2,1,0:T(8,128)S(1)} %get-tuple-element.896, f32[32,36]{0,1:T(8,128)S(1)} %copy-done.19), kind=kOutput, calls=%fused_computation.95.clone.1 | convolution fusion | flops 1216348160 | bytes 13639680 | tf_op jit(solution)/shard_map/while/body/eval_jaxpr/gijb,bh->ghij/dot_general | solution.py:82
  477.9 31.6 %fusion.270 = f32[2,12,256,512]{3,2,1,0:T(8,128)} fusion(f32[2,256,512,12]{2,3,1,0:T(8,128)} %fusion.266, f32[2,256,512,12]{2,3,1,0:T(8,128)} %fusion.267, f32[2,12,256]{2,1,0:T(8,128)} %dynamic-slice_bitcast_fusion.10, f32[12,256,512]{2,1,0:T(8,128)} %copy.185, pred[2,512]{1,0:T(4,128)(4,1)S(1)} %iota_compare_fusion.48, ...), kind=kOutput, calls=%fused_computation.106.clone.1 | convolution fusion | flops 421527552 | bytes 54822912 | tf_op jit(solution)/shard_map/while/body/eval_jaxpr/gihd,gjhd->ghij/dot_general | solution.py:76
  573.9 15.4 %fusion.266 = f32[2,256,512,12]{2,3,1,0:T(8,128)} fusion(s32[2,256,512]{2,1,0:T(8,128)S(1)} %get-tuple-element.895, f32[32,36]{0,1:T(8,128)} %get-tuple-element.988), kind=kOutput, calls=%fused_computation.92.clone.1 | convolution fusion | flops 1216348160 | bytes 13639680 | tf_op jit(solution)/shard_map/while/body/eval_jaxpr/gijb,bh->ghij/dot_general | solution.py:88
  589.3 14.2 %fusion.267 = f32[2,256,512,12]{2,3,1,0:T(8,128)} fusion(s32[2,256,512]{2,1,0:T(8,128)S(1)} %get-tuple-element.896, f32[32,36]{0,1:T(8,128)S(1)} %copy-done.19), kind=kOutput, calls=%fused_computation.95.clone.1 | convolution fusion | flops 1216348160 | bytes 13639680 | tf_op jit(solution)/shard_map/while/body/eval_jaxpr/gijb,bh->ghij/dot_general | solution.py:82
  618.8 31.7 %fusion.270 = f32[2,12,256,512]{3,2,1,0:T(8,128)} fusion(f32[2,256,512,12]{2,3,1,0:T(8,128)} %fusion.266, f32[2,256,512,12]{2,3,1,0:T(8,128)} %fusion.267, f32[2,12,256]{2,1,0:T(8,128)} %dynamic-slice_bitcast_fusion.10, f32[12,256,512]{2,1,0:T(8,128)} %copy.185, pred[2,512]{1,0:T(4,128)(4,1)S(1)} %iota_compare_fusion.48, ...), kind=kOutput, calls=%fused_computation.106.clone.1 | convolution fusion | flops 421527552 | bytes 54822912 | tf_op jit(solution)/shard_map/while/body/eval_jaxpr/gihd,gjhd->ghij/dot_general | solution.py:76
  732.0 28.3 %reduce-scatter.9.cloned.1.call-done = bf16[4,256,768]{1,2,0:T(8,128)(2,1)} async-done(((bf16[4,512,768]{1,2,0:T(8,128)(2,1)}), bf16[4,256,768]{1,2,0:T(8,128)(2,1)}) %reduce-scatter.9.cloned.1.call-update) | async-done | bytes 1572880 | tf_op jit(solution)/shard_map/reduce_scatter | solution.py:254
  765.5 40.4 %reduce-scatter.11.cloned.1.call-done = bf16[4,256,768]{1,2,0:T(8,128)(2,1)} async-done(((bf16[4,512,768]{1,2,0:T(8,128)(2,1)}), bf16[4,256,768]{1,2,0:T(8,128)(2,1)}) %reduce-scatter.11.cloned.1.call-update) | async-done | bytes 1572880 | tf_op jit(solution)/shard_map/reduce_scatter | solution.py:257
  876.1 44.1 %reduce-scatter.23.cloned.1.call-done = bf16[1536,768]{1,0:T(8,128)(2,1)} async-done(((bf16[3072,768]{1,0:T(8,128)(2,1)}), bf16[1536,768]{1,0:T(8,128)(2,1)}) %reduce-scatter.23.cloned.1.call-update) | async-done | bytes 2359312 | tf_op jit(solution)/shard_map/reduce_scatter | solution.py:305
  920.3 62.7 %reduce-scatter.21.cloned.1.call-done = bf16[384,3072]{1,0:T(8,128)(2,1)} async-done(((bf16[768,3072]{1,0:T(8,128)(2,1)}), bf16[384,3072]{1,0:T(8,128)(2,1)}) %reduce-scatter.21.cloned.1.call-update) | async-done | bytes 2359312 | tf_op jit(solution)/shard_map/reduce_scatter | solution.py:299
  983.0 50.5 %reduce-scatter.15.cloned.1.call-done = bf16[384,2304]{1,0:T(8,128)(2,1)} async-done(((bf16[768,2304]{1,0:T(8,128)(2,1)}), bf16[384,2304]{1,0:T(8,128)(2,1)}) %reduce-scatter.15.cloned.1.call-update) | async-done | bytes 1769488 | tf_op jit(solution)/shard_map/reduce_scatter | solution.py:281
  1033.4 305.6 %all-reduce.9 = (f32[64,768]{1,0:T(8,128)}, f32[384,2304]{1,0:T(8,128)}, f32[1,768]{1,0:T(1,128)}, f32[384,768]{1,0:T(8,128)}, f32[384]{0:T(512)}, /*index=5*/f3...) all-reduce(bf16[64,768]{1,0:T(8,128)(2,1)} %reduce-scatter.13.clone, ...), channel_id=1, replica_groups=mesh['doc'=16,'half'=2] {'doc'}, use_global_device_ids=true, to_apply=%region_19.20 | all-reduce | flops 3593280 | bytes 21568896 | tf_op jit(solution)/shard_map/psum | solution.py:315
  (316 shorter events, 420.9 us)
Async XLA Ops:
  7.2 64.1 %all-gather.3.cloned.1.call-start = ((), (), s32[]{:S(2)}) async-start(), calls=%async_computation.8 | async-start | bytes 4718592 | tf_op jit(solution)/shard_map/all_gather | solution.py:192
  23.8 94.6 %all-gather.5.cloned.1.call-start = ((), (), s32[]{:S(2)}) async-start(), calls=%async_computation.9 | async-start | bytes 4718592 | tf_op jit(solution)/shard_map/all_gather | solution.py:191
  27.1 733.3 %reduce-scatter.9.cloned.1.call-start = ((), (), s32[]{:S(2)}) async-start(), calls=%async_computation.10 | async-start | bytes 4718592 | tf_op jit(solution)/shard_map/reduce_scatter | solution.py:254
  130.6 15.1 %copy-start.18 = (f32[32,36]{0,1:T(8,128)S(1)}, f32[32,36]{0,1:T(8,128)}, u32[]{:S(2)}) copy-start(f32[32,36]{0,1:T(8,128)} %get-tuple-element.937) | copy-start | bytes 13828 | tf_op jit(solution)/shard_map/while
  225.0 15.3 %copy-start.18 = (f32[32,36]{0,1:T(8,128)S(1)}, f32[32,36]{0,1:T(8,128)}, u32[]{:S(2)}) copy-start(f32[32,36]{0,1:T(8,128)} %get-tuple-element.937) | copy-start | bytes 13828 | tf_op jit(solution)/shard_map/while
  325.0 43.8 %slice-start.3 = ((s8[4718592]{0:T(1024)(128)(4,1)}), s8[4194304]{0:T(1024)(128)(4,1)S(1)}, s32[]{:S(2)}) async-start(s8[4718592]{0:T(1024)(128)(4,1)} %bitcast.307), calls=%async_computation.21 | async-start | bytes 8388608
  330.1 38.7 %copy-start.14 = (f32[1024,768]{1,0:T(8,128)}, f32[1024,768]{1,0:T(8,128)S(1)}, u32[]{:S(2)}) copy-start(f32[1024,768]{1,0:T(8,128)S(1)} %get-tuple-element.696) | copy-start | bytes 9437188
  330.1 82.9 %copy-start.29 = (f32[1024]{0:T(1024)}, f32[1024]{0:T(1024)S(1)}, u32[]{:S(2)}) copy-start(f32[1024]{0:T(1024)S(1)} %broadcast_multiply_fusion.4) | copy-start | bytes 12292
  330.7 82.3 %copy-start.33 = (f32[1024]{0:T(1024)}, f32[1024]{0:T(1024)S(1)}, u32[]{:S(2)}) copy-start(f32[1024]{0:T(1024)S(1)} %add_rsqrt_fusion.1) | copy-start | bytes 12292
  330.7 38.1 %slice-start.4 = ((s8[4718592]{0:T(1024)(128)(4,1)}), s8[524288]{0:T(1024)(128)(4,1)S(1)}, s32[]{:S(2)}) async-start(s8[4718592]{0:T(1024)(128)(4,1)} %bitcast.307), calls=%async_computation.22 | async-start | bytes 1048576
  330.7 38.1 %copy-start.43 = (f32[768]{0:T(1024)S(1)}, f32[768]{0:T(1024)}, u32[]{:S(2)}) copy-start(f32[768]{0:T(1024)} %param.33) | copy-start | bytes 9220
  433.3 15.1 %copy-start.4 = (s32[2,256,512]{2,1,0:T(8,128)}, s32[2,256,512]{2,1,0:T(8,128)S(1)}, u32[]{:S(2)}) copy-start(s32[2,256,512]{2,1,0:T(8,128)S(1)} %get-tuple-element.895) | copy-start | bytes 3145732 | tf_op jit(solution)/shard_map/while
  433.3 15.1 %copy-start.6 = (s32[2,256,512]{2,1,0:T(8,128)}, s32[2,256,512]{2,1,0:T(8,128)S(1)}, u32[]{:S(2)}) copy-start(s32[2,256,512]{2,1,0:T(8,128)S(1)} %get-tuple-element.896) | copy-start | bytes 3145732 | tf_op jit(solution)/shard_map/while
  433.3 15.1 %copy-start.19 = (f32[32,36]{0,1:T(8,128)S(1)}, f32[32,36]{0,1:T(8,128)}, u32[]{:S(2)}) copy-start(f32[32,36]{0,1:T(8,128)} %get-tuple-element.988) | copy-start | bytes 13828 | tf_op jit(solution)/shard_map/while
  573.9 15.4 %copy-start.4 = (s32[2,256,512]{2,1,0:T(8,128)}, s32[2,256,512]{2,1,0:T(8,128)S(1)}, u32[]{:S(2)}) copy-start(s32[2,256,512]{2,1,0:T(8,128)S(1)} %get-tuple-element.895) | copy-start | bytes 3145732 | tf_op jit(solution)/shard_map/while
  573.9 15.4 %copy-start.6 = (s32[2,256,512]{2,1,0:T(8,128)}, s32[2,256,512]{2,1,0:T(8,128)S(1)}, u32[]{:S(2)}) copy-start(s32[2,256,512]{2,1,0:T(8,128)S(1)} %get-tuple-element.896) | copy-start | bytes 3145732 | tf_op jit(solution)/shard_map/while
  573.9 15.4 %copy-start.19 = (f32[32,36]{0,1:T(8,128)S(1)}, f32[32,36]{0,1:T(8,128)}, u32[]{:S(2)}) copy-start(f32[32,36]{0,1:T(8,128)} %get-tuple-element.988) | copy-start | bytes 13828 | tf_op jit(solution)/shard_map/while
  716.8 89.1 %reduce-scatter.11.cloned.1.call-start = ((), (), s32[]{:S(2)}) async-start(), calls=%async_computation.11 | async-start | bytes 4718592 | tf_op jit(solution)/shard_map/reduce_scatter | solution.py:257
  717.4 142.2 %reduce-scatter.19.cloned.1.call-start = ((), (), s32[]{:S(2)}) async-start(), calls=%async_computation.15 | async-start | bytes 12288 | tf_op jit(solution)/shard_map/reduce_scatter | solution.py:293
  718.9 140.7 %reduce-scatter.17.cloned.1.call-start = ((), (), s32[]{:S(2)}) async-start(), calls=%async_computation.14 | async-start | bytes 1769472 | tf_op jit(solution)/shard_map/reduce_scatter | solution.py:287
  723.7 152.4 %reduce-scatter.13.cloned.1.call-start = ((), (), s32[]{:S(2)}) async-start(), calls=%async_computation.12 | async-start | bytes 294912 | tf_op jit(solution)/shard_map/reduce_scatter | solution.py:278
  820.5 99.7 %reduce-scatter.23.cloned.1.call-start = ((), (), s32[]{:S(2)}) async-start(), calls=%async_computation.17 | async-start | bytes 7077888 | tf_op jit(solution)/shard_map/reduce_scatter | solution.py:305
  830.3 152.7 %reduce-scatter.21.cloned.1.call-start = ((), (), s32[]{:S(2)}) async-start(), calls=%async_computation.16 | async-start | bytes 7077888 | tf_op jit(solution)/shard_map/reduce_scatter | solution.py:299
  841.7 191.7 %reduce-scatter.15.cloned.1.call-start = ((), (), s32[]{:S(2)}) async-start(), calls=%async_computation.13 | async-start | bytes 5308416 | tf_op jit(solution)/shard_map/reduce_scatter | solution.py:281
  (57 other events, 336.9 us)
Sparse Core Ops, SparseCore 0:
  23.9 47.3 all-gather.2
  73.4 44.9 all-gather.4
  716.9 43.3 reduce-scatter.8
  762.5 43.3 reduce-scatter.10
  808.5 9.2 reduce-scatter.18
  820.5 22.2 reduce-scatter.16
  845.6 10.9 reduce-scatter.12
  859.6 60.6 reduce-scatter.22
  923.1 59.7 reduce-scatter.20
  985.7 47.6 reduce-scatter.14
where the time goes:
time: 1350 us
  matrix products  501 us (37%)
  blocking collectives  317 us (23%)
  waiting for transfers between devices  289 us (21%)
  local copies, waits for them, and re-layouts  120 us (9%)
  other arithmetic  89.5 us (7%)
  between operations  16.4 us (1%)
  loops' own time  13.8 us (1%)
    psum x1, blocking collectives, shards(): lax.psum((shares[0], shares[1], shares[2], shares[3], shares[4], shares[5...  306 us
    dot_general x4, matrix products, scores_of(): jnp.einsum('gihd,gjhd->ghij', queries, keys_all, preferred_element_type=j...  126 us
    reduce_scatter x1, waiting for transfers between devices, shards(): lax.psum_scatter(ffn_in_weight_grad.astype(jnp.bfloat16), 'half', scatter...  62.7 us
    dot_general x4, matrix products, scores_of(): jnp.einsum('gijb,bh->ghij', one_hot(down_bucket, jnp.float32), rel_tables...  60.8 us
    dot_general x4, matrix products, scores_of(): jnp.einsum('gijb,bh->ghij', one_hot(across_bucket, jnp.float32), rel_tabl...  57 us
    reduce_scatter x1, waiting for transfers between devices, shards(): lax.psum_scatter(qkv_weight_grad.astype(jnp.bfloat16), 'half', scatter_di...  50.5 us
    reduce_scatter x1, waiting for transfers between devices, shards(): lax.psum_scatter(ffn_out_weight_grad.astype(jnp.bfloat16), 'half', scatte...  44.1 us
    all_gather x1, waiting for transfers between devices, shards(): lax.all_gather(key_rows.reshape(key_shape), 'half', axis=1, tiled=True)  42.4 us
  transfers between devices with their start and end apart: 10, of which 7 were waited for; matrix products, arithmetic and copies ran while one was open for 8% of the time, Pallas kernels for 0%

commit v1 on v0

v1 whole, which is shorter than its diff:
```python
from functools import partial

import jax
import jax.numpy as jnp
import numpy as np
from jax import lax
from jax.experimental import pallas as pl
from jax.experimental.pallas import tpu as pltpu
from jax.sharding import PartitionSpec as P

H = 12
DH = 64
BOXF = 128
NB = 32
EPS = 1e-05
LOG2E = 1.4426950408889634
BF = jnp.bfloat16
F32 = jnp.float32
VMEM = 56 << 20
SHORT = pl.CostEstimate(flops=1, bytes_accessed=1, transcendentals=0)


def dot(a, b, ca=1, cb=0):
    return lax.dot_general(a, b, (((ca,), (cb,)), ((), ())), preferred_element_type=F32)


ROUND = 1.5 * 2.0**23 * 2.0**-8
SMALL = 1.6e-4


def unpack(both):
    first = (both + ROUND) - ROUND
    return first, (both - first) * (1.0 / SMALL)


def bucket_of(offset, shift):
    magnitude = jnp.abs(offset)
    if shift:
        magnitude = magnitude >> shift
    count = jnp.minimum(magnitude, 8)
    for n, bound in enumerate((12, 16, 24, 32, 48, 64, 96)):
        count = jnp.where(magnitude >= bound, 9 + n, count)
    return jnp.where(offset > 0, count + 16, count)


def look_up(table, index):
    return jnp.take_along_axis(table, index, axis=1, mode="promise_in_bounds")


def sine(angle, quarter):
    n = jnp.round(angle * 0.6366197723675814)
    x = ((angle - n * 1.5703125) - n * 4.837512969970703125e-4) - n * 7.549789954891882e-8
    turn = n.astype(jnp.int32) + quarter
    y = x * x
    odd = x + x * y * (-1.6666654611e-1 + y * (8.3321608736e-3 + y * -1.9515295891e-4))
    even = 1.0 - 0.5 * y + y * y * (4.166664568298827e-2 + y * (-1.388731625493765e-3 + y * 2.443315711809948e-5))
    value = jnp.where((turn & 1) == 0, odd, even)
    return jnp.where((turn & 2) == 0, value, -value)


def bias_kernel(len_ref, box_ref, rel_ref, freq_ref, out_ref, map_ref, feat_ref, line, maps, tabs, cols, *, tile, rows):
    length = out_ref.shape[3]
    blocks = length // 128
    span = (2 * blocks - 1) * 128
    w = pl.program_id(0)
    it = pl.program_id(1)

    @pl.when((w == 0) & (it == 0))
    def _():
        cols[...] = jnp.zeros_like(cols)
        cols[0:NB, 0 : 3 * H] = rel_ref[...] * LOG2E
        t = cols[0:128, :].T
        for kind in range(3):
            for hp in range(H // 2):
                n = kind * H + 2 * hp
                first = (t[n : n + 1, :] + ROUND) - ROUND
                tabs[3 * hp + kind : 3 * hp + kind + 1, :] = first + t[n + 1 : n + 2, :] * SMALL

        mpos = lax.broadcasted_iota(jnp.int32, (8, span), 1) - (length - 128)
        ipos = lax.broadcasted_iota(jnp.int32, (8, span), 0)

        def body(g, carry):
            sl = pl.ds(pl.multiple_of(g * 8, 8), 8)
            index = bucket_of(mpos - (ipos + g * 8), 0)
            for hp in range(H // 2):
                table = jnp.broadcast_to(tabs[3 * hp : 3 * hp + 1, :], (8, 128))
                for c in range(0, span, 128):
                    a, b = unpack(look_up(table, index[:, c : c + 128]))
                    line[2 * hp, sl, c : c + 128] = a
                    line[2 * hp + 1, sl, c : c + 128] = b
            return carry

        lax.fori_loop(0, 16, body, 0)

    @pl.when(it == 0)
    def _():
        coords = jnp.concatenate([box_ref[m, pl.ds(w, 1), :] for m in range(4)] * 2, 0).astype(F32)
        by_token = coords.T
        cols[:, 0:8] = by_token
        lane = lax.broadcasted_iota(jnp.int32, (1, BOXF), 1)
        which = lane >> 5
        coord = jnp.where(
            which < 2,
            jnp.where(which == 0, by_token[:, 0:1], by_token[:, 1:2]),
            jnp.where(which == 2, by_token[:, 2:3], by_token[:, 3:4]),
        )
        feat_ref[...] = sine(coord * freq_ref[0:1, :], (lane >> 4) & 1).astype(BF)

    dead = lax.broadcasted_iota(jnp.int32, (1, length), 1) >= len_ref[w]
    first = it * tile
    line_lane = (length - 128) - (first // 128) * 128
    line_row = first % 128
    here = cols[pl.ds(pl.multiple_of(first, tile), tile), 0:8].astype(jnp.int32)
    for t in range(2):
        index = bucket_of(box_ref[t, pl.ds(w, 1), :] - here[:, t : t + 1], 2)
        map_ref[0, t] = index.astype(BF)
        maps[t] = index

    def body(g, carry):
        sl = pl.ds(pl.multiple_of(g * rows, rows), rows)
        ls = pl.ds(pl.multiple_of(line_row + g * rows, rows), rows)
        for hp in range(H // 2):
            ta = jnp.broadcast_to(tabs[3 * hp + 1 : 3 * hp + 2, :], (rows, 128))
            td = jnp.broadcast_to(tabs[3 * hp + 2 : 3 * hp + 3, :], (rows, 128))
            for c in range(0, length, 128):
                cs = slice(c, c + 128)
                lc = pl.ds(pl.multiple_of(line_lane + c, 128), 128)
                a, b = unpack(look_up(ta, maps[0, sl, cs]) + look_up(td, maps[1, sl, cs]))
                a = jnp.where(dead[:, cs], -1e9 * LOG2E, a + line[2 * hp, ls, lc])
                b = jnp.where(dead[:, cs], -1e9 * LOG2E, b + line[2 * hp + 1, ls, lc])
                out_ref[0, 2 * hp, sl, cs] = a.astype(BF)
                out_ref[0, 2 * hp + 1, sl, cs] = b.astype(BF)
        return carry

    lax.fori_loop(0, tile // rows, body, 0)


def score_bias(lengths, boxes, rel_tables):
    _, windows, length = boxes.shape
    tile, rows = 64, 32
    span = (2 * (length // 128) - 1) * 128
    freq_count = BOXF // 8
    freqs = np.float32(1000.0) ** (-np.arange(freq_count, dtype=np.float32) / np.float32(freq_count))
    freqs = jnp.asarray(np.tile(freqs.astype(np.float32), (8, 8)))
    return pl.pallas_call(
        partial(bias_kernel, tile=tile, rows=rows),
        grid=(windows, length // tile),
        in_specs=[
            pl.BlockSpec(memory_space=pltpu.SMEM),
            pl.BlockSpec((4, windows, length), lambda w, i: (0, 0, 0)),
            pl.BlockSpec((NB, 3 * H), lambda w, i: (0, 0)),
            pl.BlockSpec((8, BOXF), lambda w, i: (0, 0)),
        ],
        out_specs=[
            pl.BlockSpec((1, H, tile, length), lambda w, i: (w, 0, i, 0)),
            pl.BlockSpec((1, 2, tile, length), lambda w, i: (w, 0, i, 0)),
            pl.BlockSpec((length, BOXF), lambda w, i: (w, 0)),
        ],
        out_shape=[
            jax.ShapeDtypeStruct((windows, H, length, length), BF),
            jax.ShapeDtypeStruct((windows, 2, length, length), BF),
            jax.ShapeDtypeStruct((windows * length, BOXF), BF),
        ],
        scratch_shapes=[
            pltpu.VMEM((H, 128, span), F32),
            pltpu.VMEM((2, tile, length), jnp.int32),
            pltpu.VMEM((3 * H // 2 + 6, 128), F32),
            pltpu.VMEM((length, 128), F32),
        ],
        compiler_params=pltpu.CompilerParams(vmem_limit_bytes=VMEM),
        cost_estimate=SHORT,
        name="score_bias",
    )(lengths, boxes, rel_tables, freqs)


def attend_kernel(len_ref, q_ref, k_ref, v_ref, b_ref, o_ref, e_ref, r_ref, *, chunk):
    length = q_ref.shape[0]
    lane = lax.broadcasted_iota(jnp.int32, (length, 128), 1)
    live = lax.broadcasted_iota(jnp.int32, (length, 128), 0) < len_ref[pl.program_id(0)]
    zero, one = jnp.zeros((), BF), jnp.ones((), BF)
    q, k, v = q_ref[...], k_ref[...], v_ref[...]
    outs = []
    for h in range(2):
        mine = (lane < DH) if h == 0 else (lane >= DH)
        keys = jnp.where(mine & live, k, zero)
        values = jnp.where(mine, v, jnp.where(lane == (DH if h == 0 else 0), one, zero))
        scores = dot(q, keys, 1, 1)
        for c in range(0, length, chunk):
            t = scores[c : c + chunk] * (LOG2E * DH**-0.5) + b_ref[0, h, c : c + chunk, :].astype(F32)
            e_ref[0, h, c : c + chunk, :] = jnp.exp2(t - jnp.max(t, 1, keepdims=True)).astype(BF)
        outs.append(dot(e_ref[0, h], values))
    r = jnp.where(lane < DH, 1.0 / outs[0][:, DH : DH + 1], 1.0 / outs[1][:, 0:1])
    r_ref[...] = r
    o_ref[...] = (jnp.where(lane < DH, outs[0], outs[1]) * r).astype(BF)


def attend(lengths, qkv, bias):
    windows, _, length, _ = bias.shape
    pairs = H // 2
    col = lambda off: pl.BlockSpec((length, 128), lambda w, h: (w, off + h))
    sq = pl.BlockSpec((1, 2, length, length), lambda w, h: (w, h, 0, 0))
    width = H * DH
    return pl.pallas_call(
        partial(attend_kernel, chunk=64),
        grid=(windows, pairs),
        in_specs=[pl.BlockSpec(memory_space=pltpu.SMEM), col(0), col(pairs), col(2 * pairs), sq],
        out_specs=[col(0), sq, col(0)],
        out_shape=[
            jax.ShapeDtypeStruct((windows * length, width), BF),
            jax.ShapeDtypeStruct((windows, H, length, length), BF),
            jax.ShapeDtypeStruct((windows * length, width), F32),
        ],
        compiler_params=pltpu.CompilerParams(vmem_limit_bytes=VMEM),
        cost_estimate=SHORT,
        name="attend",
    )(lengths, qkv, qkv, qkv, bias)


def attend_back_kernel(q_ref, k_ref, v_ref, e_ref, r_ref, o_ref, do_ref, *refs, chunk):
    d_ref, ds_ref, line_ref, sum_ref = refs[-4:]
    length = q_ref.shape[0]
    blocks = length // 128
    w = pl.program_id(1)
    lane = lax.broadcasted_iota(jnp.int32, (length, 128), 1)
    zero = jnp.zeros((), BF)
    q, k, v = q_ref[...], k_ref[...], v_ref[...]
    up = do_ref[...].astype(F32) * r_ref[...]
    both = up * o_ref[...].astype(F32)
    up = up.astype(BF)
    up_t, q_t = up.T, q.T
    dq, dv_t, dk_t = None, [], []
    for h in range(2):
        mine = (lane < DH) if h == 0 else (lane >= DH)
        center = jnp.sum(jnp.where(mine, both, 0.0), 1, keepdims=True)
        dp = dot(up, jnp.where(mine, v, zero), 1, 1)
        for c in range(0, length, chunk):
            e = e_ref[0, h, c : c + chunk, :].astype(F32)
            ds_ref[0, h, c : c + chunk, :] = (e * (dp[c : c + chunk] - center[c : c + chunk])).astype(BF)
        for d in range(2 * blocks - 1):
            total = None
            for ib in range(blocks):
                jb = d - (blocks - 1) + ib
                if 0 <= jb < blocks:
                    part = ds_ref[0, h, ib * 128 : (ib + 1) * 128, jb * 128 : (jb + 1) * 128].astype(F32)
                    total = part if total is None else total + part

            @pl.when(w == 0)
            def _():
                line_ref[h, :, d * 128 : (d + 1) * 128] = total

            @pl.when(w != 0)
            def _():
                line_ref[h, :, d * 128 : (d + 1) * 128] += total

        ds = ds_ref[0, h]
        part = dot(ds, jnp.where(mine, k, zero))
        dq = part if dq is None else dq + part
        dv_t.append(dot(up_t[h * DH : (h + 1) * DH], e_ref[0, h]))
        dk_t.append(dot(q_t[h * DH : (h + 1) * DH], ds))
    parts = (dq * DH**-0.5, jnp.concatenate(dk_t, 0).T * DH**-0.5, jnp.concatenate(dv_t, 0).T)
    for n, x in enumerate(parts):
        cols = slice(n * 128, (n + 1) * 128)
        x = x.astype(BF)
        d_ref[:, cols] = x
        sums = jnp.broadcast_to(column_sums(x.astype(F32)), (8, 128))
        sum_ref[:, cols] = jnp.where(w == 0, sums, sum_ref[:, cols] + sums)


def attend_back(qkv, e, r, o, do, first, count, total, at, before=None):
    windows, _, length, _ = e.shape
    pairs = H // 2
    col = lambda off: pl.BlockSpec((length, 128), lambda h, w: (w, off + h))
    sq = pl.BlockSpec((1, 2, length, length), lambda h, w: (w, first + h, 0, 0))
    span = (2 * (length // 128) - 1) * 128
    more = [] if before is None else [before]
    return pl.pallas_call(
        partial(attend_back_kernel, chunk=64),
        grid=(count, windows),
        in_specs=[col(first), col(pairs + first), col(2 * pairs + first), sq, col(first), col(first), col(first)]
        + [pl.BlockSpec(memory_space=pl.ANY)] * len(more),
        out_specs=[
            pl.BlockSpec((length, 384), lambda h, w: (w, at + h)),
            pl.BlockSpec((1, 2, length, length), lambda h, w: (w, h, 0, 0)),
            pl.BlockSpec((2, 128, span), lambda h, w: (h, 0, 0)),
            pl.BlockSpec((8, 384), lambda h, w: (0, h)),
        ],
        out_shape=[
            jax.ShapeDtypeStruct((windows * length, total * 384), BF),
            jax.ShapeDtypeStruct((windows, 2 * count, length, length), BF),
            jax.ShapeDtypeStruct((2 * count, 128, span), F32),
            jax.ShapeDtypeStruct((8, count * 384), F32),
        ],
        input_output_aliases={7: 0} if more else {},
        compiler_params=pltpu.CompilerParams(vmem_limit_bytes=VMEM),
        cost_estimate=SHORT,
        name="attend_back",
    )(qkv, qkv, qkv, e, r, o, do, *more)


def spread(refs, rows, stride):
    h = 0
    for ref in refs:
        for n in range(ref.shape[-3]):
            x = (ref[0, n] if len(ref.shape) == 4 else ref[n]).astype(F32)
            for c in range(x.shape[1] // 128):
                rows[c, h * stride : h * stride + x.shape[0], :] = x[:, c * 128 : (c + 1) * 128]
            h += 1


def heads_of(rows, i, stride):
    return [rows[c, pl.ds(i, 16, stride=stride), :].astype(BF) for c in range(rows.shape[0])]


def one_hot(index):
    width = index.shape[1]
    ids = lax.broadcasted_iota(jnp.int32, (NB, width), 0).astype(BF)
    hit = jnp.broadcast_to(index, (NB, width)).astype(BF) == ids
    return jnp.where(hit, jnp.ones((), BF), jnp.zeros((), BF))


def table_kernel(*refs, parts, with_line):
    ds_refs, refs = refs[:parts], refs[parts:]
    line_refs, refs = refs[: parts * with_line], refs[parts * with_line :]
    map_ref, out_ref, rows, maps = refs[0], refs[1], refs[-2], refs[-1]
    tile = map_ref.shape[2]
    step = pl.program_id(0)

    @pl.when(step == 0)
    def _():
        out_ref[...] = jnp.zeros_like(out_ref)
        rows[...] = jnp.zeros_like(rows)

    if with_line:
        line_out, line_rows = refs[2], refs[3]
        share = line_refs[0].shape[1]
        span = line_refs[0].shape[2]

        @pl.when(step == 0)
        def _():
            line_out[...] = jnp.zeros_like(line_out)
            line_rows[...] = jnp.zeros_like(line_rows)

        spread(line_refs, line_rows, share + 8)
        offset = lax.broadcasted_iota(jnp.int32, (8, span), 1) - (span - 128) // 2
        down = lax.broadcasted_iota(jnp.int32, (8, span), 0) + step * share
        lhs, rhs = [], []
        for i in range(share):
            if i % 8 == 0:
                index = bucket_of(offset - (down + i), 0).astype(F32)
            lhs += heads_of(line_rows, i, share + 8)
            rhs.append(one_hot(index[i % 8 : i % 8 + 1, :]))
        line_out[...] += dot(jnp.concatenate(lhs, 1), jnp.concatenate(rhs, 1), 1, 1)

    spread(ds_refs, rows, tile + 8)
    maps[...] = map_ref[0].astype(F32)
    lhs, rhs = [], []
    for i in range(tile):
        lhs += heads_of(rows, i, tile + 8)
        rhs.append(jnp.concatenate([one_hot(maps[t, i : i + 1, :]) for t in range(2)], 0))
    out_ref[...] += dot(jnp.concatenate(lhs, 1), jnp.concatenate(rhs, 1), 1, 1)


def table_grads(ds_parts, lines, maps, w):
    _, _, length, _ = maps.shape
    tile = 64
    parts = len(ds_parts)
    steps = length // tile
    outs, out_shapes = [pl.BlockSpec((16, 2 * NB), lambda i: (0, 0))], [jax.ShapeDtypeStruct((16, 2 * NB), F32)]
    line_specs, line_rows = [], []
    if lines:
        share, span = 128 // steps, lines[0].shape[2]
        line_specs = [pl.BlockSpec((x.shape[0], share, span), lambda i: (0, i, 0)) for x in lines]
        line_rows = [pltpu.VMEM((span // 128, 16 * (share + 8), 128), F32)]
        outs.append(pl.BlockSpec((16, NB), lambda i: (0, 0)))
        out_shapes.append(jax.ShapeDtypeStruct((16, NB), F32))
    return pl.pallas_call(
        partial(table_kernel, parts=parts, with_line=bool(lines)),
        grid=(steps,),
        in_specs=[pl.BlockSpec((1, x.shape[1], tile, length), lambda i: (w, 0, i, 0)) for x in ds_parts]
        + line_specs
        + [pl.BlockSpec((1, 2, tile, length), lambda i: (w, 0, i, 0))],
        out_specs=outs,
        out_shape=out_shapes,
        scratch_shapes=line_rows
        + [pltpu.VMEM((length // 128, 16 * (tile + 8), 128), F32), pltpu.VMEM((2, tile, length), F32)],
        compiler_params=pltpu.CompilerParams(vmem_limit_bytes=VMEM),
        cost_estimate=SHORT,
        name="table_grads",
    )(*ds_parts, *lines, maps)


def gelu_both(x):
    t = 1.0 / (1.0 + (0.3275911 * 0.7071067811865476) * jnp.abs(x))
    e = jnp.exp2((-0.5 * LOG2E) * (x * x))
    poly = t * (
        0.5 * 0.254829592
        + t * (0.5 * -0.284496736 + t * (0.5 * 1.421413741 + t * (0.5 * -1.453152027 + t * (0.5 * 1.061405429))))
    )
    tail = poly * e
    cdf = jnp.where(x >= 0, 1.0 - tail, tail)
    return x * cdf, cdf + x * (e * 0.3989422804014327)


def norm_forward(summed, params):
    centered = summed - jnp.mean(summed, -1, keepdims=True)
    inverse = lax.rsqrt(jnp.mean(centered * centered, -1, keepdims=True) + EPS)
    normed = centered * inverse
    return normed * params[0:1] + params[1:2], normed, inverse


def norm_backward(upstream, normed, inverse, params):
    scaled = upstream * params[0:1]
    return inverse * (
        scaled - jnp.mean(scaled, -1, keepdims=True) - normed * jnp.mean(scaled * normed, -1, keepdims=True)
    )


def column_sums(x):
    return jnp.sum(x, 0, keepdims=True)


def feed_kernel(sec_ref, low_ref, w1_ref, b1_ref, w2_ref, b2_ref, n2_ref, cot_ref, act_ref, slope_ref, out_ref, dsum_ref, dlow_ref, sum_ref, acc, *, chunk):
    step = pl.program_id(0)
    tokens = low_ref.shape[0]

    @pl.when(step == 0)
    def _():
        acc[...] = jnp.zeros_like(acc)

    for c in range(0, tokens, chunk):
        cs = slice(c, c + chunk)
        active, slope = gelu_both(dot(low_ref[cs, :], w1_ref[...]) + b1_ref[...])
        active = active.astype(BF)
        act_ref[cs, :] = active
        slope_ref[cs, :] = slope.astype(BF)
        acc[cs, :] += dot(active, w2_ref[...])

    @pl.when(step == pl.num_programs(0) - 1)
    def _():
        sums = [0.0, 0.0, 0.0]
        for c in range(0, tokens, 128):
            cs = slice(c, c + 128)
            result, normed, inverse = norm_forward(sec_ref[cs, :] + (acc[cs, :] + b2_ref[...]), n2_ref[...])
            out_ref[cs, :] = result.astype(BF)
            up = cot_ref[cs, :].astype(F32)
            grad = norm_backward(up, normed, inverse, n2_ref[...])
            low = grad.astype(BF)
            dsum_ref[cs, :] = grad
            dlow_ref[cs, :] = low
            sums = [sums[0] + column_sums(up * normed), sums[1] + column_sums(up), sums[2] + column_sums(low.astype(F32))]
        sum_ref[...] = jnp.concatenate(sums + [jnp.zeros((5, sums[0].shape[1]), F32)], 0)


def feed(second, second_low, w1, b1, w2, b2, norm_two, cotangent):
    tokens, width = second.shape
    hidden = w1.shape[1]
    tile = 512
    whole = lambda shape: pl.BlockSpec(shape, lambda n: (0, 0))
    return pl.pallas_call(
        partial(feed_kernel, chunk=256),
        grid=(hidden // tile,),
        in_specs=[
            whole((tokens, width)),
            whole((tokens, width)),
            pl.BlockSpec((width, tile), lambda n: (0, n)),
            pl.BlockSpec((1, tile), lambda n: (0, n)),
            pl.BlockSpec((tile, width), lambda n: (n, 0)),
            whole((1, width)),
            whole((2, width)),
            whole((tokens, width)),
        ],
        out_specs=[
            pl.BlockSpec((tokens, tile), lambda n: (0, n)),
            pl.BlockSpec((tokens, tile), lambda n: (0, n)),
            whole((tokens, width)),
            whole((tokens, width)),
            whole((tokens, width)),
            whole((8, width)),
        ],
        out_shape=[
            jax.ShapeDtypeStruct((tokens, hidden), BF),
            jax.ShapeDtypeStruct((tokens, hidden), BF),
            jax.ShapeDtypeStruct((tokens, width), BF),
            jax.ShapeDtypeStruct((tokens, width), F32),
            jax.ShapeDtypeStruct((tokens, width), BF),
            jax.ShapeDtypeStruct((8, width), F32),
        ],
        scratch_shapes=[pltpu.VMEM((tokens, width), F32)],
        compiler_params=pltpu.CompilerParams(vmem_limit_bytes=VMEM),
        cost_estimate=SHORT,
        name="feed",
    )(second, second_low, w1, b1.reshape(1, -1), w2, b2.reshape(1, -1), norm_two, cotangent)


def feed_back_kernel(dlow_ref, dsum_ref, w1_ref, w2_ref, slope_ref, z_ref, n1_ref, din_ref, bias_ref, done_ref, dbr_ref, sum_ref, acc, *, chunk):
    step = pl.program_id(0)
    tokens = dlow_ref.shape[0]

    @pl.when(step == 0)
    def _():
        acc[...] = dsum_ref[...]

    sums = 0.0
    for c in range(0, tokens, chunk):
        cs = slice(c, c + chunk)
        d_inner = (dot(dlow_ref[cs, :], w2_ref[...], 1, 1) * slope_ref[cs, :].astype(F32)).astype(BF)
        din_ref[cs, :] = d_inner
        sums = sums + column_sums(d_inner.astype(F32))
        acc[cs, :] += dot(d_inner, w1_ref[...], 1, 1)
    bias_ref[...] = jnp.concatenate([sums, jnp.zeros((7, sums.shape[1]), F32)], 0)

    @pl.when(step == pl.num_programs(0) - 1)
    def _():
        totals = [0.0, 0.0, 0.0]
        for c in range(0, tokens, 128):
            cs = slice(c, c + 128)
            _, normed, inverse = norm_forward(z_ref[cs, :], n1_ref[...])
            up = acc[cs, :]
            grad = norm_backward(up, normed, inverse, n1_ref[...])
            low = grad.astype(BF)
            done_ref[cs, :] = grad
            dbr_ref[cs, :] = low
            totals = [
                totals[0] + column_sums(up * normed),
                totals[1] + column_sums(up),
                totals[2] + column_sums(low.astype(F32)),
            ]
        sum_ref[...] = jnp.concatenate(totals + [jnp.zeros((5, totals[0].shape[1]), F32)], 0)


def feed_back(d_outer, d_sum_two, w1, w2, slope, z_one, norm_one):
    tokens, width = z_one.shape
    hidden = w1.shape[1]
    tile = 512
    whole = lambda shape: pl.BlockSpec(shape, lambda n: (0, 0))
    return pl.pallas_call(
        partial(feed_back_kernel, chunk=256),
        grid=(hidden // tile,),
        in_specs=[
            whole((tokens, width)),
            whole((tokens, width)),
            pl.BlockSpec((width, tile), lambda n: (0, n)),
            pl.BlockSpec((tile, width), lambda n: (n, 0)),
            pl.BlockSpec((tokens, tile), lambda n: (0, n)),
            whole((tokens, width)),
            whole((2, width)),
        ],
        out_specs=[
            pl.BlockSpec((tokens, tile), lambda n: (0, n)),
            pl.BlockSpec((8, tile), lambda n: (0, n)),
            whole((tokens, width)),
            whole((tokens, width)),
            whole((8, width)),
        ],
        out_shape=[
            jax.ShapeDtypeStruct((tokens, hidden), BF),
            jax.ShapeDtypeStruct((8, hidden), F32),
            jax.ShapeDtypeStruct((tokens, width), F32),
            jax.ShapeDtypeStruct((tokens, width), BF),
            jax.ShapeDtypeStruct((8, width), F32),
        ],
        scratch_shapes=[pltpu.VMEM((tokens, width), F32)],
        compiler_params=pltpu.CompilerParams(vmem_limit_bytes=VMEM),
        cost_estimate=SHORT,
        name="feed_back",
    )(d_outer, d_sum_two, w1, w2, slope, z_one, norm_one)


UNIT = 384
PIECES = 2


def halves(full, place_ref):
    rows = full.shape[0] // 2
    upper = place_ref[1] == 0
    low, high = full[:rows], full[rows:]
    return jnp.where(upper, high, low).astype(BF), jnp.where(upper, low, high).astype(BF)


def wide_grads_kernel(place_ref, *refs, counts):
    step = pl.program_id(0)
    pairs = len(counts)
    outs, turned = refs[3 * pairs : -1], refs[-1]
    at = 0
    for n, count in enumerate(counts):

        @pl.when(step == at)
        def _():
            turned[...] = refs[3 * n][...].T

        @pl.when((step >= at) & (step < at + count))
        def _():
            full = dot(turned[...], jnp.concatenate([refs[3 * n + 1][...], refs[3 * n + 2][...]], 1))
            both = halves(full, place_ref)
            for m, x in enumerate(both):
                side = x.shape[0] // 2
                for k in range(2):
                    outs[2 * m + k][...] = x[k * side : (k + 1) * side, :UNIT].reshape(outs[2 * m + k].shape)
                outs[4 + m][...] = x[:, UNIT:].reshape(outs[4 + m].shape)

        at += count


def wide_grads(place, pairs):
    tokens, rows = pairs[0][0].shape
    counts = [right.shape[1] // (2 * UNIT) for _, right in pairs]
    specs, at = [], 0
    for (left, right), count in zip(pairs, counts):

        def block(i, p, send, at=at, count=count):
            owner = 1 - p[0] if send else p[0]
            return (0, owner * count + jnp.clip(i - at, 0, count - 1))

        specs += [
            pl.BlockSpec(left.shape, lambda i, p: (0, 0)),
            pl.BlockSpec((tokens, UNIT), partial(block, send=True)),
            pl.BlockSpec((tokens, UNIT), partial(block, send=False)),
        ]
        at += count
    piece = pl.BlockSpec((1, 1, rows // 4, UNIT), lambda i, p: (0, i, 0, 0))
    out = pl.BlockSpec((2, 1, rows // 4, UNIT), lambda i, p: (0, i, 0, 0))
    outs = pl.pallas_call(
        partial(wide_grads_kernel, counts=counts),
        grid_spec=pltpu.PrefetchScalarGridSpec(
            num_scalar_prefetch=1,
            grid=(at,),
            in_specs=specs,
            out_specs=[piece] * 4 + [out] * 2,
            scratch_shapes=[pltpu.VMEM((rows, tokens), BF)],
        ),
        out_shape=[jax.ShapeDtypeStruct((n, at, rows // 4, UNIT), BF) for n in (1, 1, 1, 1, 2, 2)],
        compiler_params=pltpu.CompilerParams(vmem_limit_bytes=VMEM),
        cost_estimate=SHORT,
        name="wide_grads",
    )(place, *[x for left, right in pairs for x in (left, right, right)])
    return [x.reshape(-1, UNIT) for x in outs]


def long_grads_kernel(place_ref, left_ref, send_ref, keep_ref, *outs):
    full = dot(left_ref[...], jnp.concatenate([send_ref[...], keep_ref[...]], 1), 0, 0).astype(BF)
    for n in range(4):

        @pl.when(pl.program_id(0) == n)
        def _():
            outs[n][...] = full[:, :UNIT]
            outs[4 + n // 2][...] = full[:, UNIT:]


def long_grads(place, left, right):
    tokens, rows = left.shape
    tile = rows // 4

    def quarter(i, p):
        owner = jnp.where(i < 2, 1 - p[1], p[1])
        return (0, owner * 2 + lax.rem(i, 2))

    piece = pl.BlockSpec((tile, UNIT), lambda i, p: (0, 0))
    other = pl.BlockSpec((tile, UNIT), lambda i, p: (jnp.minimum(i, 1), 0))
    own = pl.BlockSpec((tile, UNIT), lambda i, p: (jnp.maximum(i - 2, 0), 0))
    return pl.pallas_call(
        long_grads_kernel,
        grid_spec=pltpu.PrefetchScalarGridSpec(
            num_scalar_prefetch=1,
            grid=(4,),
            in_specs=[
                pl.BlockSpec((tokens, tile), quarter),
                pl.BlockSpec((tokens, UNIT), lambda i, p: (0, 1 - p[0])),
                pl.BlockSpec((tokens, UNIT), lambda i, p: (0, p[0])),
            ],
            out_specs=[piece] * 4 + [other, own],
        ),
        out_shape=[jax.ShapeDtypeStruct((n * tile, UNIT), BF) for n in (1, 1, 1, 1, 2, 2)],
        compiler_params=pltpu.CompilerParams(vmem_limit_bytes=VMEM),
        cost_estimate=SHORT,
        name="long_grads",
    )(place, left, right, right)


E_ROWS = 16


def last_kernel(place_ref, x_ref, dx_ref, f_ref, df_ref, two_ref, one_ref, in_ref, *refs):
    qv_refs, (line_ref, small0_ref, small1_ref), outs = refs[:3], refs[3:6], refs[6:]
    mine = place_ref[0] == 0
    upper = place_ref[1] == 0
    width = x_ref.shape[1]
    middle = width // 2
    x = dot(x_ref[...], dx_ref[...], 0, 0).astype(BF)
    box = dot(f_ref[...], df_ref[...], 0, 0).astype(BF)
    tables = jnp.concatenate([line_ref[...], small0_ref[...] + small1_ref[...], jnp.zeros((16, NB), F32)], 1).T
    blocks = [ref[0:1, p : p + UNIT] for ref in qv_refs for p in range(0, ref.shape[1], UNIT)]
    qv = [jnp.concatenate([y[:, at : at + 128] for y in blocks], 1) for at in (0, 256)]
    halves_of = []
    for n in range(2):
        cols = slice(n * middle, (n + 1) * middle)
        inner = in_ref[0:1, n * 2 * width : (n + 1) * 2 * width]
        sums = [
            two_ref[n : n + 1, :],
            one_ref[n : n + 1, :],
            qv[n],
            jnp.concatenate([one_ref[2:3, cols], two_ref[2:3, cols]], 1),
            inner[:, :width],
            inner[:, width:],
            jnp.zeros((E_ROWS - 6, width), F32),
        ]
        share = [tables[m * NB + n * NB // 2 : m * NB + (n + 1) * NB // 2, :] for m in range(3)]
        share = [jnp.pad(t, ((0, 0), (0, 128 - t.shape[1]))) for t in share]
        sides = [jnp.concatenate(sums, 0), jnp.concatenate(share + [jnp.zeros((E_ROWS, width - 3 * 128), F32)], 1)]
        q, h = x.shape[0] // 4, box.shape[0] // 4
        halves_of.append(
            jnp.concatenate(
                [
                    y
                    for m in range(2)
                    for y in (
                        x[(2 * n + m) * q : (2 * n + m + 1) * q],
                        box[(2 * n + m) * h : (2 * n + m + 1) * h],
                        sides[m].astype(BF),
                    )
                ],
                0,
            )
        )
    for m in range(2):
        rows = jnp.where(upper, halves_of[1 - m], halves_of[m])
        send = jnp.where(mine, rows[:, middle:], rows[:, :middle])
        side = send.shape[0] // 2
        outs[2 * m][...] = send[:side]
        outs[2 * m + 1][...] = send[side:]
        outs[4 + m][...] = jnp.where(mine, rows[:, :middle], rows[:, middle:])


def last_grads(place, x, dx, f, df, *sums):
    rows = (x.shape[1] + f.shape[1]) // 4 + E_ROWS
    vmem = pl.BlockSpec(memory_space=pltpu.VMEM)
    return pl.pallas_call(
        last_kernel,
        in_specs=[pl.BlockSpec(memory_space=pltpu.SMEM)] + [vmem] * (4 + len(sums)),
        out_specs=[vmem] * 6,
        out_shape=[jax.ShapeDtypeStruct((n * rows, UNIT), BF) for n in (1, 1, 1, 1, 2, 2)],
        compiler_params=pltpu.CompilerParams(vmem_limit_bytes=VMEM),
        cost_estimate=SHORT,
        name="last_grads",
    )(place, x, dx, f, df, *sums)


def lay_kernel(place_ref, *refs, kind, rows):
    pieces, outs = refs[:4], refs[4:]
    core, side = place_ref[0], place_ref[2]
    step = pl.program_id(0)

    def lay_piece(ref, owner):
        blocks = ref.shape[0] // rows
        for n in range(ref.shape[0] // rows if kind != "heads" else 3):
            x = ref[n * rows : (n + 1) * rows, :].astype(F32)
            if kind == "long":
                outs[0][n * rows : (n + 1) * rows, owner * UNIT : (owner + 1) * UNIT] = x
            elif kind == "wide":
                at = (owner * blocks + n) * UNIT
                outs[0][:, at : at + UNIT] = x
            elif n == 0:
                outs[0][:, owner * UNIT : (owner + 1) * UNIT] = x
            else:
                lay_pair(x, owner * 2 + n - 1)
        if kind == "heads":
            lay_pair(ref[3 * rows : 4 * rows, :].astype(F32), 4 + owner)
            at = 4 * rows
            box = BOXF // 4
            cols = slice(owner * UNIT, (owner + 1) * UNIT)
            outs[2][:, cols] = ref[at : at + box, :].astype(F32)
            small = ref[at + box : at + box + E_ROWS, :].astype(F32)

            @pl.when(step == 0)
            def _():
                for n in range(3):
                    outs[3 + n][:, cols] = small[n : n + 1]
                outs[6 + owner][...] = small[3:4]
                for n in range(2):
                    at = n * 2 * UNIT + owner * UNIT
                    outs[8][:, at : at + UNIT] = small[4 + n : 5 + n]

            if owner == 0:

                @pl.when(step == 1)
                def _():
                    outs[9][...] = jnp.concatenate([small[:, n * 128 : n * 128 + H] for n in range(3)], 1)

    def lay_pair(x, pair):
        for m in range(3):
            at = (m * (H // 2) + pair) * 128
            outs[1][:, at : at + 128] = x[:, m * 128 : (m + 1) * 128]

    for other_side in range(2):
        for owner in range(2):
            for other_core in range(2):

                @pl.when(((step == side) == (other_side == 0)) & (core == (owner ^ other_core)))
                def _():
                    lay_piece(pieces[2 * other_side + other_core], owner)


def lay(place, pieces, kind, rows):
    blocks = pieces[0].shape[0] // rows
    whole = None
    if kind == "long":
        shapes = [(2 * blocks * rows, 2 * UNIT)]
    elif kind == "wide":
        shapes = [(2 * rows, 2 * blocks * UNIT)]
    else:
        width = 2 * UNIT
        shapes = [(2 * rows, width), (2 * rows, 3 * width), (BOXF // 2, width)]
        whole = [(1, width)] * 3 + [(1, UNIT)] * 2 + [(1, 2 * width), (NB // 2, 3 * H)]
    return pl.pallas_call(
        partial(lay_kernel, kind=kind, rows=rows),
        grid=(2,),
        in_specs=[pl.BlockSpec(memory_space=pltpu.SMEM)] + [pl.BlockSpec(x.shape, lambda i: (0, 0)) for x in pieces],
        out_specs=[pl.BlockSpec((m // 2, n), lambda i: (i, 0)) for m, n in shapes]
        + [pl.BlockSpec(shape, lambda i: (0, 0)) for shape in whole or []],
        out_shape=[jax.ShapeDtypeStruct(shape, F32) for shape in shapes + (whole or [])],
        compiler_params=pltpu.CompilerParams(vmem_limit_bytes=VMEM),
        cost_estimate=SHORT,
        name="lay",
    )(place, *pieces)


def entry_kernel(a_ref, b_ref, w_ref, sum_ref, out_ref):
    pairs = H // 2
    weight = jnp.concatenate([w_ref[:, (m * pairs + n) * 128 : (m * pairs + n + 1) * 128] for n in range(pairs) for m in range(3)], 1)
    both = jnp.concatenate([a_ref[...], b_ref[...]], 1)
    out_ref[...] = (sum_ref[...] + dot(both, weight, 1, 1)).astype(BF)


def entry_grad(first, last, weight, base):
    tokens, width = base.shape
    tile = tokens // 2
    row = lambda x: pl.BlockSpec((tile, x.shape[1]), lambda i: (i, 0))
    return pl.pallas_call(
        entry_kernel,
        grid=(tokens // tile,),
        in_specs=[row(first), row(last), pl.BlockSpec(weight.shape, lambda i: (0, 0)), row(base)],
        out_specs=row(base),
        out_shape=jax.ShapeDtypeStruct((tokens, width), BF),
        compiler_params=pltpu.CompilerParams(vmem_limit_bytes=VMEM),
        cost_estimate=SHORT,
        name="entry_grad",
    )(first, last, weight, base)


def shards(
    docs,
    hidden_in,
    boxes,
    lengths,
    box_weight,
    qkv_weight,
    qv_bias,
    out_weight,
    out_bias,
    rel_tables,
    norm_one,
    ffn_in_weight,
    ffn_in_bias,
    ffn_out_weight,
    ffn_out_bias,
    norm_two,
    cotangent,
):
    half = lax.axis_index("half")
    doc = lax.axis_index("doc")
    core, side = doc & 1, (doc >> 1) & 1
    own, local_len, width = hidden_in.shape
    windows = own // 2
    length = 2 * local_len
    tokens = windows * length

    def swap_half(x):
        return lax.ppermute(x, "half", [(0, 1), (1, 0)])

    def swap_doc(x, bit):
        return lax.ppermute(x, "doc", [(i, i ^ (1 << bit)) for i in range(docs)])

    def part(x, index, axis):
        if isinstance(x, tuple):
            return jnp.where(index == 0, *x)
        size = x.shape[axis] // 2
        return lax.dynamic_slice_in_dim(x, index * size, size, axis)

    def ordered(index, mine, other, axis):
        return jnp.where(index == 0, jnp.concatenate([mine, other], axis), jnp.concatenate([other, mine], axis))

    def whole_windows(x, axis):
        return ordered(half, part(x, half, axis), swap_half(part(x, 1 - half, axis)), axis + 1)

    def half_positions(x):
        return ordered(half, part(x, half, 1), swap_half(part(x, 1 - half, 1)), 0)

    def add(x, y):
        return (x.astype(F32) + y.astype(F32)).astype(BF)

    def tie(x, *others):
        return lax.optimization_barrier((x,) + others)[0]

    box_part = swap_half(part(boxes, 1 - half, 1))
    my_boxes = ordered(half, part(boxes, half, 1), box_part, 2)
    my_lengths = part(lengths, half, 0)
    hidden_send = part(tie(hidden_in, box_part), 1 - half, 0)
    hidden = ordered(half, part(hidden_in, half, 0), swap_half(hidden_send), 1).reshape(tokens, width)
    upstream = whole_windows(tie(cotangent, hidden_send), 0).reshape(tokens, width)

    bias, maps, features = score_bias(my_lengths, my_boxes, rel_tables)
    entry = hidden.astype(F32) + dot(features, box_weight)
    entry_low = entry.astype(BF)
    qkv_shift = jnp.concatenate([qv_bias[0], jnp.zeros_like(qv_bias[0]), qv_bias[1]])
    qkv = (dot(entry_low, qkv_weight) + qkv_shift).astype(BF)

    attended, e, r = attend(my_lengths, qkv, bias)
    z_one = entry + (dot(attended, out_weight) + out_bias)
    second = norm_forward(z_one, norm_one)[0]
    second_low = second.astype(BF)
    active, slope, result, d_sum_two, d_outer, sums_two = feed(
        second, second_low, ffn_in_weight, ffn_in_bias, ffn_out_weight, ffn_out_bias, norm_two, upstream
    )
    pairs, early = H // 2, H // 3
    late_pairs = pairs - early
    step = early // 2
    more = list(range(2, docs.bit_length() - 1))
    place = jnp.stack([core, half, side]).astype(jnp.int32)
    last = [None]

    def now(x):
        return x if last[0] is None else tie(x, last[0])

    def then(x):
        last[0] = x
        return x

    def total(*xs):
        out = xs[0].astype(F32)
        for x in xs[1:]:
            out = out + x.astype(F32)
        return out.astype(BF)

    class Chain:
        def core(self, *parts):
            send, send_own, keep, keep_own = parts[:PIECES], parts[PIECES:-2], parts[-2], parts[-1]
            then(keep_own)
            self.keep, self.come = keep, jnp.concatenate([swap_doc(x, 0) for x in send], 0)
            self.own = [keep_own, tuple(swap_doc(x, 0) for x in send_own)]

        def half(self):
            send = then(total(now(self.keep), self.come))
            self.own.append(swap_half(send))

        def split(self, bit):
            b = (doc >> bit) & 1
            own = [now(self.own[0])] + self.own[1:]
            send = then(total(*[part(x, 1 - b, 0) for x in own]))
            keep = total(*[part(x, b, 0) for x in own])
            self.own = [keep, swap_doc(send, bit)]

        def double(self, bits):
            x = then(total(now(self.own[0]), *self.own[1:]))
            for bit in bits[:-1]:
                x = total(x, swap_doc(x, bit))
            self.own = [x, swap_doc(x, bits[-1])]

        def gather(self):
            x = then(total(now(self.own[0]), *self.own[1:]))
            self.mine, self.across = x, swap_doc(x, 1)
            self.beside = swap_doc(x, 0)

        def pieces(self):
            return [now(self.mine), self.beside, self.across, swap_doc(self.across, 0)]

    def back(first, count, total_pairs, at, before):
        out = attend_back(qkv, e, r, attended, now(d_attended), first, count, total_pairs, at, before)
        then(out[0])
        return out

    a, b, c, d = Chain(), Chain(), Chain(), Chain()
    block_rows = width // 4
    then(d_outer)
    a.core(*long_grads(place, active, now(d_outer)))
    a.half()
    d_inner, sums_in, d_sum_one, d_branch, sums_one = feed_back(
        now(d_outer), d_sum_two, ffn_in_weight, ffn_out_weight, slope, z_one, norm_one
    )
    then(d_branch)
    a.split(1)
    b.core(*wide_grads(place, [(second_low, now(d_inner))]))
    d_attended = then(dot(now(d_branch), out_weight, 1, 1).astype(BF))
    a.double(more[:1])
    b.half()
    first_right, ds_0, line_0, qv_0 = back(0, step, early, 0, None)
    a.double(more[1:])
    first_right, ds_1, line_1, qv_1 = back(step, early - step, early, step, first_right)
    c.core(*wide_grads(place, [(attended, d_branch), (entry_low, now(first_right))]))
    b.split(1)
    c.half()
    result = result.reshape(windows, length, width)
    out_send = then(part(now(result), 1 - half, 1))
    out_mine, out_other = part(result, half, 1), swap_half(out_send)
    last_right, ds_2, line_2, qv_2 = back(early, late_pairs, late_pairs, 0, None)
    b.double(more[:1])
    small_0, line_grad = table_grads([ds_0, ds_1, now(ds_2)], [line_0, line_1, line_2], maps, 0)
    then(small_0)
    a.gather()
    c.split(1)
    b.double(more[1:])
    layer_out = then(ordered(half, now(out_mine), out_other, 0))
    small_1 = table_grads([ds_0, ds_1, now(ds_2)], [], maps, 1)[0]
    for w in range(2, windows):
        small_1 = small_1 + table_grads([ds_0, ds_1, ds_2], [], maps, w)[0]
    then(small_1)
    c.double(more[:1])
    d_entry_low = then(entry_grad(first_right, now(last_right), qkv_weight, d_sum_one))
    d.core(
        *last_grads(
            place, entry_low, last_right, features, now(d_entry_low), sums_two, sums_one, sums_in, qv_0, qv_1, qv_2, line_grad, small_0, small_1
        )
    )
    b.gather()
    c.double(more[1:])
    d.half()
    d_entry = d_entry_low.reshape(windows, length, width)
    grad_send = then(part(now(d_entry), 1 - half, 1))
    grad_mine, grad_other = part(d_entry, half, 1), swap_half(grad_send)
    (ffn_out_grad,) = lay(place, a.pieces(), "long", block_rows)
    then(ffn_out_grad)
    d.split(1)
    (ffn_in_grad,) = lay(place, b.pieces(), "wide", block_rows)
    then(ffn_in_grad)
    d.double(more[:1])
    hidden_grad = then(ordered(half, now(grad_mine), grad_other, 0))
    d.double(more[1:])
    parts = [total(now(c.own[0]), c.own[1]), total(d.own[0], d.own[1])]
    c.own = [then(jnp.concatenate(parts, 0))]
    c.gather()
    out_grad, qkv_grad, box, two, one, qv, out_sum, ffn_out_sum, ffn_in_sum, table = lay(
        place, c.pieces(), "heads", block_rows
    )
    return (
        layer_out,
        hidden_grad,
        box,
        qkv_grad,
        qv,
        out_grad,
        out_sum.reshape(-1),
        table,
        one,
        ffn_in_grad,
        ffn_in_sum.reshape(-1),
        ffn_out_grad,
        ffn_out_sum.reshape(-1),
        two,
    )


def solution(mesh):
    rep = P()
    rows = P("half", None)
    return jax.shard_map(
        partial(shards, mesh.shape["doc"]),
        mesh=mesh,
        in_specs=(P("doc", "half", None), P(None, "doc", "half"), P("doc")) + (rep,) * 12 + (P("doc", "half", None),),
        out_specs=(
            P("doc", "half", None),
            P("doc", "half", None),
            rows,
            rows,
            rows,
            rows,
            P("half"),
            rows,
            rows,
            rows,
            P("half"),
            rows,
            P("half"),
            rows,
        ),
        check_vma=False,
    )
```

time: 1350 us -> 385 us (0.29)
  matrix products: 501 us -> 11.9 us
  blocking collectives: 317 us -> 0 us
  waiting for transfers between devices: 289 us -> 68.8 us
  Pallas kernels: 0 us -> 219 us
  local copies, waits for them, and re-layouts: 120 us -> 9.48 us
  other arithmetic: 89.5 us -> 25.7 us
  starting transfers between devices: 0.41 us -> 41.7 us
  between operations: 16.4 us -> 1.64 us
  loops' own time: 13.8 us -> 0 us
    dot_general x46 -> x4, matrix products: 501 us -> 11.9 us  [dot(): lax.dot_general(a, b, (((ca,), (cb,)), ((), ())), preferred_element_type=...]
    psum x1 -> x0, blocking collectives: 306 us -> none  [shards(): lax.psum((shares[0], shares[1], shares[2], shares[3], shares[4], shares[5...]
    reduce_scatter x8 -> x0, waiting for transfers between devices: 226 us -> none  [the longest x1 62.7 us: shards(): lax.psum_scatter(ffn_in_weight_grad.astype(jnp.bfloat16), 'half', scatter...]
    pallas_call x0 -> x17, Pallas kernels: none -> 219 us  [the longest x1 31.6 us: score_bias(): pl.pallas_call(partial(bias_kernel, tile=tile, rows=rows), grid=(windows,...]
    ppermute x0 -> x46, waiting for transfers between devices: none -> 68.8 us  [the longest x37 56 us: swap_doc(): return lax.ppermute(x, 'doc', [(i, i ^ 1 << bit) for i in range(docs)])]
    all_gather x2 -> x0, waiting for transfers between devices: 62.1 us -> none  [the longest x1 42.4 us: shards(): lax.all_gather(key_rows.reshape(key_shape), 'half', axis=1, tiled=True)]
    reduce_sum x13 -> x1, other arithmetic: 48.1 us -> 0.48 us  [norm_forward(): inverse = lax.rsqrt(jnp.mean(centered * centered, -1, keepdims=True) + EPS)]
    ppermute x0 -> x46, starting transfers between devices: none -> 41.7 us  [the longest x37 30.8 us: swap_doc(): return lax.ppermute(x, 'doc', [(i, i ^ 1 << bit) for i in range(docs)])]
  transfers between devices with their start and end apart: 10 -> 46, of which waited for: 7 -> 16; matrix products, arithmetic and copies ran while one was open for 8% -> 5% of each run, Pallas kernels for 0% -> 41%
where the time goes in v1:
time: 385 us; the launch traced here: 378 us
  Pallas kernels  219 us (57%)
  waiting for transfers between devices  68.8 us (18%)
  starting transfers between devices  41.7 us (11%)
  other arithmetic  25.7 us (7%)
  matrix products  11.9 us (3%)
  local copies, waits for them, and re-layouts  9.48 us (2%)
    ppermute x37, waiting for transfers between devices, swap_doc(): return lax.ppermute(x, 'doc', [(i, i ^ 1 << bit) for i in range(docs)])  56 us
    pallas_call x1, Pallas kernels, score_bias(): pl.pallas_call(partial(bias_kernel, tile=tile, rows=rows), grid=(windows,...  31.6 us
    pallas_call x3, Pallas kernels, attend_back(): pl.pallas_call(partial(attend_back_kernel, chunk=64), grid=(count, window...  31.5 us
    ppermute x37, starting transfers between devices, swap_doc(): return lax.ppermute(x, 'doc', [(i, i ^ 1 << bit) for i in range(docs)])  30.8 us
    pallas_call x1, Pallas kernels, feed(): pl.pallas_call(partial(feed_kernel, chunk=256), grid=(hidden // tile,), i...  30.2 us
    pallas_call x2, Pallas kernels, table_grads(): pl.pallas_call(partial(table_kernel, parts=parts, with_line=bool(lines)),...  26.4 us
    pallas_call x1, Pallas kernels, feed_back(): pl.pallas_call(partial(feed_back_kernel, chunk=256), grid=(hidden // tile...  22.9 us
    pallas_call x2, Pallas kernels, wide_grads(): pl.pallas_call(partial(wide_grads_kernel, counts=counts), grid_spec=pltpu...  20.4 us
  transfers between devices with their start and end apart: 46, of which 16 were waited for; matrix products, arithmetic and copies ran while one was open for 5% of the time, Pallas kernels for 41%

profile of v1, /device:TPU:1, one launch (start us, length us, event | category | flops | bytes accessed | tf_op | source)
XLA Modules:
  0.0 377.9 jit_solution(4972099334746000142)
XLA Ops:
  10.8 31.6 %score_bias.1 = (bf16[2,12,512,512]{3,2,1,0:T(8,128)(2,1)}, bf16[2,2,512,512]{3,2,1,0:T(8,128)(2,1)}, bf16[1024,128]{1,0:T(8,128)(2,1)}) custom-call(s32[2]{0:T(128)} %dynamic_slice.84.len_ref, s32[4,2,512]{2,1,0:T(2,128)} %add_select_fusion.box_ref, f32[32,36]{1,0:T(8,128)} %rel_ref.1, f32[8,128]{1,0:T(8,128)} %constant.43.clone.freq_ref), custom_call_target="tpu_custom_call" | custom-call | flops 1 | bytes 1 | tf_op jit(solution)/shard_map/score_bias/pallas_call | solution.py:145
  48.0 5.4 %add_convert_fusion.q_ref.k_ref.v_ref = bf16[1024,2304]{1,0:T(8,128)(2,1)} fusion(bf16[1024,768]{1,0:T(8,128)(2,1)S(1)} %get-tuple-element.242.refs_3_.x_ref, bf16[768,2304]{1,0:T(8,128)(2,1)S(1)} %copy-done.6, f32[2304]{0:T(1024)S(1)} %pad_maximum_fusion.1), kind=kOutput, calls=%fused_computation | convolution fusion | flops 3628597248 | bytes 9839616 | tf_op jit(solution)/shard_map/dot_general | solution.py:24
  53.4 18.8 %attend.1 = (bf16[1024,768]{1,0:T(8,128)(2,1)}, bf16[2,12,512,512]{3,2,1,0:T(8,128)(2,1)}, f32[1024,768]{1,0:T(8,128)}) custom-call(s32[2]{0:T(128)} %dynamic_slice.84.len_ref, bf16[1024,2304]{1,0:T(8,128)(2,1)} %add_convert_fusion.q_ref.k_ref.v_ref, bf16[1024,2304]{1,0:T(8,128)(2,1)} %add_convert_fusion.q_ref.k_ref.v_ref, ...), custom_call_target="tpu_custom_call" | custom-call | flops 1 | bytes 1 | tf_op jit(solution)/shard_map/attend/pallas_call | solution.py:203
  80.1 30.2 %feed.1 = (bf16[1024,3072]{1,0:T(8,128)(2,1)}, bf16[1024,3072]{1,0:T(8,128)(2,1)}, bf16[1024,768]{1,0:T(8,128)(2,1)}, f32[1024,768]{1,0:T(8,128)}, bf16[1024,768]{1,0:T(8,128)(2,1)}, /*index=5*/f32[8,768]{1,0:T(8,128)}) custom-call(f32[1024,768]{1,0:T(8,128)} %get-tuple-element.229.sec_ref, bf16[1024,768]{1,0:T(8,128)(2,1)} %get-tuple-element.228.low_ref.refs_0_, ...), custom_call_target="tpu_custom_call" | custom-call | flops 1 | bytes 1 | tf_op jit(solution)/shard_map/feed/pallas_call | solution.py:459
  110.3 10.9 %long_grads.1 = (bf16[768,384]{1,0:T(8,128)(2,1)}, bf16[768,384]{1,0:T(8,128)(2,1)}, bf16[768,384]{1,0:T(8,128)(2,1)}, bf16[768,384]{1,0:T(8,128)(2,1)}, bf16[15...) custom-call(s32[3]{0:T(128)} %pad_add_fusion.place_ref, bf16[1024,3072]{1,0:T(8,128)(2,1)} %get-tuple-element.126.left_ref, ...), custom_call_target="tpu_custom_call" | custom-call | flops 1 | bytes 1 | tf_op jit(solution)/shard_map/long_grads/pallas_call | solution.py:660
  129.9 22.9 %feed_back.1 = (bf16[1024,3072]{1,0:T(8,128)(2,1)}, f32[8,3072]{1,0:T(8,128)}, f32[1024,768]{1,0:T(8,128)}, bf16[1024,768]{1,0:T(8,128)(2,1)}, f32[8,768]{1,0:T(8,128)}) custom-call(bf16[1024,768]{1,0:T(8,128)(2,1)} %get-tuple-element.133.send_ref.keep_ref.dlow_ref, f32[1024,768]{1,0:T(8,128)} %get-tuple-element.134.dsum_ref, bf16[768,3072]{1,0:T(8,128)(2,1)} %w1_ref.3, ...), custom_call_target="tpu_custom_call" | custom-call | flops 1 | bytes 1 | tf_op jit(solution)/shard_map/feed_back/pallas_call | solution.py:536
  157.0 10.4 %wide_grads.2 = (bf16[1,4,192,384]{3,2,1,0:T(8,128)(2,1)}, bf16[1,4,192,384]{3,2,1,0:T(8,128)(2,1)}, bf16[1,4,192,384]{3,2,1,0:T(8,128)(2,1)}, bf16[1,4,192,384]...) custom-call(s32[3]{0:T(128)} %pad_add_fusion.place_ref, ...), custom_call_target="tpu_custom_call" | custom-call | flops 1 | bytes 1 | tf_op jit(solution)/shard_map/wide_grads/pallas_call | solution.py:622
  176.8 10.4 %attend_back.3 = (bf16[1024,1536]{1,0:T(8,128)(2,1)}, bf16[2,4,512,512]{3,2,1,0:T(8,128)(2,1)}, f32[4,128,896]{2,1,0:T(8,128)}, f32[8,768]{1,0:T(8,128)}) custom-call(bf16[1024,2304]{1,0:T(8,128)(2,1)} %add_convert_fusion.q_ref.k_ref.v_ref, bf16[1024,2304]{1,0:T(8,128)(2,1)} %add_convert_fusion.q_ref.k_ref.v_ref, ...), custom_call_target="tpu_custom_call" | custom-call | flops 1 | bytes 1 | tf_op jit(solution)/shard_map/attend_back/pallas_call | solution.py:276
  188.8 10.7 %attend_back.4 = (bf16[1024,1536]{1,0:T(8,128)(2,1)}, bf16[2,4,512,512]{3,2,1,0:T(8,128)(2,1)}, f32[4,128,896]{2,1,0:T(8,128)}, f32[8,768]{1,0:T(8,128)}) custom-call(bf16[1024,2304]{1,0:T(8,128)(2,1)} %add_convert_fusion.q_ref.k_ref.v_ref, bf16[1024,2304]{1,0:T(8,128)(2,1)} %add_convert_fusion.q_ref.k_ref.v_ref, ...), custom_call_target="tpu_custom_call", output_to_operand_aliasing={{0}: (7, {})} | custom-call | flops 1 | bytes 1 | tf_op jit(solution)/shard_map/attend_back/pallas_call | solution.py:276
  199.5 10.1 %wide_grads.3 = (bf16[1,3,192,384]{3,2,1,0:T(8,128)(2,1)}, bf16[1,3,192,384]{3,2,1,0:T(8,128)(2,1)}, bf16[1,3,192,384]{3,2,1,0:T(8,128)(2,1)}, bf16[1,3,192,384]...) custom-call(s32[3]{0:T(128)} %pad_add_fusion.place_ref, ...), custom_call_target="tpu_custom_call" | custom-call | flops 1 | bytes 1 | tf_op jit(solution)/shard_map/wide_grads/pallas_call | solution.py:622
  218.1 10.4 %attend_back.5 = (bf16[1024,768]{1,0:T(8,128)(2,1)}, bf16[2,4,512,512]{3,2,1,0:T(8,128)(2,1)}, f32[4,128,896]{2,1,0:T(8,128)}, f32[8,768]{1,0:T(8,128)}) custom-call(bf16[1024,2304]{1,0:T(8,128)(2,1)} %add_convert_fusion.q_ref.k_ref.v_ref, bf16[1024,2304]{1,0:T(8,128)(2,1)} %add_convert_fusion.q_ref.k_ref.v_ref, ...), custom_call_target="tpu_custom_call" | custom-call | flops 1 | bytes 1 | tf_op jit(solution)/shard_map/attend_back/pallas_call | solution.py:276
  231.0 14.4 %table_grads.2 = (f32[16,64]{1,0:T(8,128)}, f32[16,32]{1,0:T(8,128)}) custom-call(bf16[2,4,512,512]{3,2,1,0:T(8,128)(2,1)} %get-tuple-element.169.refs_0_, bf16[2,4,512,512]{3,2,1,0:T(8,128)(2,1)} %get-tuple-element.170.refs_1_, bf16[2,4,512,512]{3,2,1,0:T(8,128)(2,1)} %get-tuple-element.184.refs_2_, f32[4,128,896]{2,1,0:T(8,128)} %get-tuple-element.173.refs_3_, ...), custom_call_target="tpu_custom_call" | custom-call | flops 1 | bytes 1 | tf_op jit(solution)/shard_map/table_grads/pallas_call | solution.py:376
  251.5 8.1 %collective-permute-done.22 = bf16[768,384]{1,0:T(8,128)(2,1)S(1)} collective-permute-done((bf16[768,384]{1,0:T(8,128)(2,1)S(1)}, bf16[768,384]{1,0:T(8,128)(2,1)S(1)}, u32[]{:S(2)}, u32[]{:S(2)}) %collective-permute-start.22) | collective-permute-done | bytes 589856 | tf_op jit(solution)/shard_map/ppermute | solution.py:880
  261.6 12.0 %table_grads.3.refs_5_ = f32[16,64]{1,0:T(8,128)} custom-call(bf16[2,4,512,512]{3,2,1,0:T(8,128)(2,1)} %get-tuple-element.169.refs_0_, bf16[2,4,512,512]{3,2,1,0:T(8,128)(2,1)} %get-tuple-element.170.refs_1_, bf16[2,4,512,512]{3,2,1,0:T(8,128)(2,1)} %get-tuple-element.184.refs_2_, bf16[2,2,512,512]{3,2,1,0:T(8,128)(2,1)} %get-tuple-element.176.refs_6_.refs_3_), custom_call_target="tpu_custom_call" | custom-call | flops 1 | bytes 1 | tf_op jit(solution)/shard_map/table_grads/pallas_call | solution.py:376
  277.4 8.5 %entry_grad.1.df_ref = bf16[1024,768]{1,0:T(8,128)(2,1)} custom-call(bf16[1024,1536]{1,0:T(8,128)(2,1)} %get-tuple-element.156.refs_4_.refs_5_.a_ref, bf16[1024,768]{1,0:T(8,128)(2,1)} %get-tuple-element.186.b_ref.dx_ref, bf16[768,2304]{1,0:T(8,128)(2,1)} %w_ref.1, f32[1024,768]{1,0:T(8,128)} %get-tuple-element.187.sum_ref), custom_call_target="tpu_custom_call" | custom-call | flops 1 | bytes 1 | tf_op jit(solution)/shard_map/entry_grad/pallas_call | solution.py:837
  285.9 5.3 %last_grads.1 = (bf16[240,384]{1,0:T(8,128)(2,1)}, bf16[240,384]{1,0:T(8,128)(2,1)}, bf16[240,384]{1,0:T(8,128)(2,1)}, bf16[240,384]{1,0:T(8,128)(2,1)}, bf16[48...) custom-call(s32[3]{0:T(128)} %pad_add_fusion.place_ref, bf16[1024,768]{1,0:T(8,128)(2,1)} %copy-done.4, ...), custom_call_target="tpu_custom_call" | custom-call | flops 1 | bytes 1 | tf_op jit(solution)/shard_map/last_grads/pallas_call | solution.py:736
  292.0 5.0 %collective-permute-done.26 = bf16[576,384]{1,0:T(8,128)(2,1)S(1)} collective-permute-done((bf16[576,384]{1,0:T(8,128)(2,1)S(1)}, bf16[576,384]{1,0:T(8,128)(2,1)S(1)}, u32[]{:S(2)}, u32[]{:S(2)}) %collective-permute-start.26) | collective-permute-done | bytes 442400 | tf_op jit(solution)/shard_map/ppermute | solution.py:880
  301.1 9.7 %collective-permute-done.36.refs_2_ = bf16[768,384]{1,0:T(8,128)(2,1)} collective-permute-done((bf16[768,384]{1,0:T(8,128)(2,1)S(1)}, bf16[768,384]{1,0:T(8,128)(2,1)}, u32[]{:S(2)}, u32[]{:S(2)}) %collective-permute-start.36) | collective-permute-done | bytes 589856 | tf_op jit(solution)/shard_map/ppermute | solution.py:880
  312.9 4.0 %lay.3 = f32[1536,768]{1,0:T(8,128)} custom-call(s32[3]{0:T(128)} %pad_add_fusion.place_ref, bf16[768,384]{1,0:T(8,128)(2,1)} %copy-done.8, bf16[768,384]{1,0:T(8,128)(2,1)} %copy-done.23, bf16[768,384]{1,0:T(8,128)(2,1)} %copy-done.22, bf16[768,384]{1,0:T(8,128)(2,1)} %copy-done.24), custom_call_target="tpu_custom_call" | custom-call | flops 1 | bytes 1 | tf_op jit(solution)/shard_map/lay/pallas_call | solution.py:813
  326.8 9.3 %collective-permute-done.39 = bf16[2,256,768]{2,1,0:T(8,128)(2,1)S(1)} collective-permute-done((bf16[2,256,768]{2,1,0:T(8,128)(2,1)S(1)}, bf16[2,256,768]{2,1,0:T(8,128)(2,1)S(1)}, u32[]{:S(2)}, u32[]{:S(2)}) %collective-permute-start.39) | collective-permute-done | bytes 786464 | tf_op jit(solution)/shard_map/ppermute | solution.py:877
  338.1 6.2 %collective-permute-done.41 = bf16[576,384]{1,0:T(8,128)(2,1)S(1)} collective-permute-done((bf16[576,384]{1,0:T(8,128)(2,1)S(1)}, bf16[576,384]{1,0:T(8,128)(2,1)S(1)}, u32[]{:S(2)}, u32[]{:S(2)}) %collective-permute-start.41) | collective-permute-done | bytes 442400 | tf_op jit(solution)/shard_map/ppermute | solution.py:880
  344.4 5.8 %collective-permute-done.42 = bf16[240,384]{1,0:T(8,128)(2,1)S(1)} collective-permute-done((bf16[240,384]{1,0:T(8,128)(2,1)S(1)}, bf16[240,384]{1,0:T(8,128)(2,1)S(1)}, u32[]{:S(2)}, u32[]{:S(2)}) %collective-permute-start.42) | collective-permute-done | bytes 184352 | tf_op jit(solution)/shard_map/ppermute | solution.py:880
  352.4 13.0 %collective-permute-done.44.refs_2_ = bf16[816,384]{1,0:T(8,128)(2,1)S(1)} collective-permute-done((bf16[816,384]{1,0:T(8,128)(2,1)S(1)}, bf16[816,384]{1,0:T(8,128)(2,1)S(1)}, u32[]{:S(2)}, u32[]{:S(2)}) %collective-permute-start.44) | collective-permute-done | bytes 626720 | tf_op jit(solution)/shard_map/ppermute | solution.py:880
  369.5 4.1 %lay.5 = (f32[384,768]{1,0:T(8,128)}, f32[384,2304]{1,0:T(8,128)}, f32[64,768]{1,0:T(8,128)}, f32[1,768]{1,0:T(1,128)}, f32[1,768]{1,0:T(1,128)}, /*index=5*/f32...) custom-call(s32[3]{0:T(128)} %pad_add_fusion.place_ref, ...), custom_call_target="tpu_custom_call" | custom-call | flops 1 | bytes 1 | tf_op jit(solution)/shard_map/lay/pallas_call | solution.py:813
  (208 shorter events, 99.0 us)
Async XLA Ops:
  5.7 36.7 %collective-permute-start.1 = (bf16[2,256,768]{2,1,0:T(8,128)(2,1)}, bf16[2,256,768]{2,1,0:T(8,128)(2,1)S(1)}, u32[]{:S(2)}, u32[]{:S(2)}) collective-permute-start(bf16[2,256,768]{2,1,0:T(8,128)(2,1)} %constant_dynamic-slice_fusion.7), channel_id=1, source_target_pairs={{0,1},{1,0},{2,3},{3,2},{4,5},{5,4},{6,7},{7,6},{8,9},{9,8},{10,11... | collective-permute-start | bytes 2359304 | tf_op jit(solution)/shard_map/ppermute | solution.py:877
  8.2 34.2 %collective-permute-start.2 = (bf16[2,256,768]{2,1,0:T(8,128)(2,1)}, bf16[2,256,768]{2,1,0:T(8,128)(2,1)}, u32[]{:S(2)}, u32[]{:S(2)}) collective-permute-start(bf16[2,256,768]{2,1,0:T(8,128)(2,1)} %get-tuple-element.237), channel_id=1, source_target_pairs={{0,1},{1,0},{2,3},{3,2},{4,5},{5,4},{6,7},{7,6},{8,9},{9,8},{10,11... | collective-permute-start | bytes 2359304 | tf_op jit(solution)/shard_map/ppermute | solution.py:877
  127.5 27.8 %collective-permute-start.7 = (bf16[1536,384]{1,0:T(8,128)(2,1)S(1)}, bf16[1536,384]{1,0:T(8,128)(2,1)S(1)}, u32[]{:S(2)}, u32[]{:S(2)}) collective-permute-start(bf16[1536,384]{1,0:T(8,128)(2,1)S(1)} %add_convert_fusion.2), channel_id=1, source_target_pairs={{0,1},{1,0},{2,3},{3,2},{4,5},{5,4},{6,7},{7,6},{8,9},{9,8},{10,11... | collective-permute-start | bytes 3538952 | tf_op jit(solution)/shard_map/ppermute | solution.py:877
  129.3 23.6 %collective-permute-start.5 = (bf16[768,384]{1,0:T(8,128)(2,1)}, bf16[768,384]{1,0:T(8,128)(2,1)S(1)}, u32[]{:S(2)}, u32[]{:S(2)}) collective-permute-start(bf16[768,384]{1,0:T(8,128)(2,1)} %get-tuple-element.139), channel_id=1, source_target_pairs={{0,2},{2,0},{4,6},{6,4},{8,10},{10,8},{12,14},{14,12},{16,18},{18,... | collective-permute-start | bytes 1769480 | tf_op jit(solution)/shard_map/ppermute | solution.py:880
  129.9 22.9 %collective-permute-start.6 = (bf16[768,384]{1,0:T(8,128)(2,1)}, bf16[768,384]{1,0:T(8,128)(2,1)S(1)}, u32[]{:S(2)}, u32[]{:S(2)}) collective-permute-start(bf16[768,384]{1,0:T(8,128)(2,1)} %get-tuple-element.140), channel_id=1, source_target_pairs={{0,2},{2,0},{4,6},{6,4},{8,10},{10,8},{12,14},{14,12},{16,18},{18,... | collective-permute-start | bytes 1769480 | tf_op jit(solution)/shard_map/ppermute | solution.py:880
  173.2 38.1 %collective-permute-start.14 = (bf16[1536,384]{1,0:T(8,128)(2,1)S(1)}, bf16[1536,384]{1,0:T(8,128)(2,1)S(1)}, u32[]{:S(2)}, u32[]{:S(2)}) collective-permute-start(bf16[1536,384]{1,0:T(8,128)(2,1)S(1)} %add_convert_fusion.1), channel_id=1, source_target_pairs={{0,1},{1,0},{2,3},{3,2},{4,5},{5,4},{6,7},{7,6},{8,9},{9,8},{10,11... | collective-permute-start | bytes 3538952 | tf_op jit(solution)/shard_map/ppermute | solution.py:877
  175.8 35.5 %collective-permute-start.12 = (bf16[768,384]{1,0:T(8,128)(2,1)S(1)}, bf16[768,384]{1,0:T(8,128)(2,1)S(1)}, u32[]{:S(2)}, u32[]{:S(2)}) collective-permute-start(bf16[768,384]{1,0:T(8,128)(2,1)S(1)} %bitcast.42), channel_id=1, source_target_pairs={{0,2},{2,0},{4,6},{6,4},{8,10},{10,8},{12,14},{14,12},{16,18},{18,... | collective-permute-start | bytes 1769480 | tf_op jit(solution)/shard_map/ppermute | solution.py:880
  176.8 34.5 %collective-permute-start.13 = (bf16[768,384]{1,0:T(8,128)(2,1)S(1)}, bf16[768,384]{1,0:T(8,128)(2,1)S(1)}, u32[]{:S(2)}, u32[]{:S(2)}) collective-permute-start(bf16[768,384]{1,0:T(8,128)(2,1)S(1)} %bitcast.41), channel_id=1, source_target_pairs={{0,2},{2,0},{4,6},{6,4},{8,10},{10,8},{12,14},{14,12},{16,18},{18,... | collective-permute-start | bytes 1769480 | tf_op jit(solution)/shard_map/ppermute | solution.py:880
  214.6 33.5 %collective-permute-start.21 = (bf16[1152,384]{1,0:T(8,128)(2,1)}, bf16[1152,384]{1,0:T(8,128)(2,1)}, u32[]{:S(2)}, u32[]{:S(2)}) collective-permute-start(bf16[1152,384]{1,0:T(8,128)(2,1)} %add_convert_fusion.3), channel_id=1, source_target_pairs={{0,1},{1,0},{2,3},{3,2},{4,5},{5,4},{6,7},{7,6},{8,9},{9,8},{10,11... | collective-permute-start | bytes 2654216 | tf_op jit(solution)/shard_map/ppermute | solution.py:877
  214.8 30.6 %collective-permute-start.18 = (bf16[768,384]{1,0:T(8,128)(2,1)S(1)}, bf16[768,384]{1,0:T(8,128)(2,1)}, u32[]{:S(2)}, u32[]{:S(2)}) collective-permute-start(bf16[768,384]{1,0:T(8,128)(2,1)S(1)} %add_convert_fusion.10), channel_id=1, source_target_pairs={{0,16},{2,18},{4,20},{6,22},{8,24},{10,26},{12,28},{14,30},{16,0},... | collective-permute-start | bytes 1769480 | tf_op jit(solution)/shard_map/ppermute | solution.py:880
  217.1 30.9 %collective-permute-start.19 = (bf16[576,384]{1,0:T(8,128)(2,1)}, bf16[576,384]{1,0:T(8,128)(2,1)S(1)}, u32[]{:S(2)}, u32[]{:S(2)}) collective-permute-start(bf16[576,384]{1,0:T(8,128)(2,1)} %bitcast.46), channel_id=1, source_target_pairs={{0,2},{2,0},{4,6},{6,4},{8,10},{10,8},{12,14},{14,12},{16,18},{18,... | collective-permute-start | bytes 1327112 | tf_op jit(solution)/shard_map/ppermute | solution.py:880
  218.0 30.0 %collective-permute-start.20 = (bf16[576,384]{1,0:T(8,128)(2,1)}, bf16[576,384]{1,0:T(8,128)(2,1)S(1)}, u32[]{:S(2)}, u32[]{:S(2)}) collective-permute-start(bf16[576,384]{1,0:T(8,128)(2,1)} %bitcast.45), channel_id=1, source_target_pairs={{0,2},{2,0},{4,6},{6,4},{8,10},{10,8},{12,14},{14,12},{16,18},{18,... | collective-permute-start | bytes 1327112 | tf_op jit(solution)/shard_map/ppermute | solution.py:880
  228.5 31.7 %collective-permute-start.23 = (bf16[2,256,768]{2,1,0:T(8,128)(2,1)S(1)}, bf16[2,256,768]{2,1,0:T(8,128)(2,1)S(1)}, u32[]{:S(2)}, u32[]{:S(2)}) collective-permute-start(bf16[2,256,768]{2,1,0:T(8,128)(2,1)S(1)} %constant_dynamic-slice_fusion.2), channel_id=1, source_target_pairs={{0,1},{1,0},{2,3},{3,2},{4,5},{5,4},{6,7},{7,6},{8,9},{9,8},{10,11... | collective-permute-start | bytes 2359304 | tf_op jit(solution)/shard_map/ppermute | solution.py:877
  249.9 23.7 %collective-permute-start.24 = (bf16[576,384]{1,0:T(8,128)(2,1)S(1)}, bf16[576,384]{1,0:T(8,128)(2,1)S(1)}, u32[]{:S(2)}, u32[]{:S(2)}) collective-permute-start(bf16[576,384]{1,0:T(8,128)(2,1)S(1)} %get-tuple-element.235), channel_id=1, source_target_pairs={{0,4},{2,6},{4,0},{6,2},{8,12},{10,14},{12,8},{14,10},{16,20},{18,... | collective-permute-start | bytes 1327112 | tf_op jit(solution)/shard_map/ppermute | solution.py:880
  250.2 27.1 %collective-permute-start.30 = (bf16[768,384]{1,0:T(8,128)(2,1)S(1)}, bf16[768,384]{1,0:T(8,128)(2,1)S(1)}, u32[]{:S(2)}, u32[]{:S(2)}) collective-permute-start(bf16[768,384]{1,0:T(8,128)(2,1)S(1)} %add_convert_fusion.6.refs_0_), channel_id=1, source_target_pairs={{0,4},{2,6},{4,0},{6,2},{8,12},{10,14},{12,8},{14,10},{16,20},{18,... | collective-permute-start | bytes 1769480 | tf_op jit(solution)/shard_map/ppermute | solution.py:880
  259.7 31.9 %collective-permute-start.25 = (bf16[768,384]{1,0:T(8,128)(2,1)S(1)}, bf16[768,384]{1,0:T(8,128)(2,1)S(1)}, u32[]{:S(2)}, u32[]{:S(2)}) collective-permute-start(bf16[768,384]{1,0:T(8,128)(2,1)S(1)} %add_convert_fusion.5), channel_id=1, source_target_pairs={{0,16},{2,18},{4,20},{6,22},{8,24},{10,26},{12,28},{14,30},{16,0},... | collective-permute-start | bytes 1769480 | tf_op jit(solution)/shard_map/ppermute | solution.py:880
  273.7 23.3 %collective-permute-start.26 = (bf16[576,384]{1,0:T(8,128)(2,1)S(1)}, bf16[576,384]{1,0:T(8,128)(2,1)S(1)}, u32[]{:S(2)}, u32[]{:S(2)}) collective-permute-start(bf16[576,384]{1,0:T(8,128)(2,1)S(1)} %add_convert_fusion.16), channel_id=1, source_target_pairs={{0,8},{2,10},{4,12},{6,14},{8,0},{10,2},{12,4},{14,6},{16,24},{18,... | collective-permute-start | bytes 1327112 | tf_op jit(solution)/shard_map/ppermute | solution.py:880
  275.4 25.2 %collective-permute-start.29 = (bf16[768,384]{1,0:T(8,128)(2,1)S(1)}, bf16[768,384]{1,0:T(8,128)(2,1)S(1)}, u32[]{:S(2)}, u32[]{:S(2)}) collective-permute-start(bf16[768,384]{1,0:T(8,128)(2,1)S(1)} %add_convert_fusion.6.refs_0_), channel_id=1, source_target_pairs={{0,2},{2,0},{4,6},{6,4},{8,10},{10,8},{12,14},{14,12},{16,18},{18,... | collective-permute-start | bytes 1769480 | tf_op jit(solution)/shard_map/ppermute | solution.py:880
  277.3 23.4 %collective-permute-start.31 = (bf16[768,384]{1,0:T(8,128)(2,1)S(1)}, bf16[768,384]{1,0:T(8,128)(2,1)S(1)}, u32[]{:S(2)}, u32[]{:S(2)}) collective-permute-start(bf16[768,384]{1,0:T(8,128)(2,1)S(1)} %collective-permute-done.30.refs_2_), channel_id=1, source_target_pairs={{0,2},{2,0},{4,6},{6,4},{8,10},{10,8},{12,14},{14,12},{16,18},{18,... | collective-permute-start | bytes 1769480 | tf_op jit(solution)/shard_map/ppermute | solution.py:880
  298.2 20.0 %collective-permute-start.34 = (bf16[480,384]{1,0:T(8,128)(2,1)}, bf16[480,384]{1,0:T(8,128)(2,1)}, u32[]{:S(2)}, u32[]{:S(2)}) collective-permute-start(bf16[480,384]{1,0:T(8,128)(2,1)} %add_convert_fusion.19), channel_id=1, source_target_pairs={{0,1},{1,0},{2,3},{3,2},{4,5},{5,4},{6,7},{7,6},{8,9},{9,8},{10,11... | collective-permute-start | bytes 1105928 | tf_op jit(solution)/shard_map/ppermute | solution.py:877
  300.6 17.7 %collective-permute-start.33 = (bf16[240,384]{1,0:T(8,128)(2,1)}, bf16[240,384]{1,0:T(8,128)(2,1)}, u32[]{:S(2)}, u32[]{:S(2)}) collective-permute-start(bf16[240,384]{1,0:T(8,128)(2,1)} %get-tuple-element.207), channel_id=1, source_target_pairs={{0,2},{2,0},{4,6},{6,4},{8,10},{10,8},{12,14},{14,12},{16,18},{18,... | collective-permute-start | bytes 552968 | tf_op jit(solution)/shard_map/ppermute | solution.py:880
  300.7 19.8 %collective-permute-start.35 = (bf16[768,384]{1,0:T(8,128)(2,1)S(1)}, bf16[768,384]{1,0:T(8,128)(2,1)}, u32[]{:S(2)}, u32[]{:S(2)}) collective-permute-start(bf16[768,384]{1,0:T(8,128)(2,1)S(1)} %add_convert_fusion.4.refs_0_), channel_id=1, source_target_pairs={{0,2},{2,0},{4,6},{6,4},{8,10},{10,8},{12,14},{14,12},{16,18},{18,... | collective-permute-start | bytes 1769480 | tf_op jit(solution)/shard_map/ppermute | solution.py:880
  317.0 19.2 %collective-permute-start.39 = (bf16[2,256,768]{2,1,0:T(8,128)(2,1)S(1)}, bf16[2,256,768]{2,1,0:T(8,128)(2,1)S(1)}, u32[]{:S(2)}, u32[]{:S(2)}) collective-permute-start(bf16[2,256,768]{2,1,0:T(8,128)(2,1)S(1)} %constant_dynamic-slice_fusion), channel_id=1, source_target_pairs={{0,1},{1,0},{2,3},{3,2},{4,5},{5,4},{6,7},{7,6},{8,9},{9,8},{10,11... | collective-permute-start | bytes 2359304 | tf_op jit(solution)/shard_map/ppermute | solution.py:877
  319.9 24.4 %collective-permute-start.41 = (bf16[576,384]{1,0:T(8,128)(2,1)S(1)}, bf16[576,384]{1,0:T(8,128)(2,1)S(1)}, u32[]{:S(2)}, u32[]{:S(2)}) collective-permute-start(bf16[576,384]{1,0:T(8,128)(2,1)S(1)} %add_convert_fusion.15), channel_id=1, source_target_pairs={{0,16},{2,18},{4,20},{6,22},{8,24},{10,26},{12,28},{14,30},{16,0},... | collective-permute-start | bytes 1327112 | tf_op jit(solution)/shard_map/ppermute | solution.py:880
  (58 other events, 507.6 us)

commit v2 on v1

--- a/solution.py
+++ b/solution.py
@@ -44,7 +44,16 @@
 
 
 def look_up(table, index):
-    return jnp.take_along_axis(table, index, axis=1, mode="promise_in_bounds")
+    dims = lax.GatherDimensionNumbers(
+        offset_dims=(),
+        collapsed_slice_dims=(1,),
+        start_index_map=(1,),
+        operand_batching_dims=(0,),
+        start_indices_batching_dims=(0,),
+    )
+    return lax.gather(
+        table, index[..., None], dims, slice_sizes=(1, 1), mode=lax.GatherScatterMode.PROMISE_IN_BOUNDS
+    )
 
 
 def sine(angle, quarter):
@@ -419,13 +428,56 @@
     return jnp.sum(x, 0, keepdims=True)
 
 
-def feed_kernel(sec_ref, low_ref, w1_ref, b1_ref, w2_ref, b2_ref, n2_ref, cot_ref, act_ref, slope_ref, out_ref, dsum_ref, dlow_ref, sum_ref, acc, *, chunk):
+def front_kernel(hid_ref, f_ref, box_ref, w_ref, qv_ref, low_ref, out_ref):
+    step = pl.program_id(0)
+    third = pl.num_programs(0) // 3
+
+    @pl.when(step == 0)
+    def _():
+        low_ref[...] = (hid_ref[...].astype(F32) + dot(f_ref[...], box_ref[...])).astype(BF)
+
+    wide = out_ref.shape[1]
+    cols = pl.ds(pl.multiple_of(lax.rem(step, third) * wide, wide), wide)
+    shift = jnp.where(step < third, qv_ref[0:1, cols], jnp.where(step < 2 * third, 0.0, qv_ref[1:2, cols]))
+    out_ref[...] = (dot(low_ref[...], w_ref[...]) + shift).astype(BF)
+
+
+def front(hidden, features, box_weight, qkv_weight, qv_bias):
+    tokens, width = hidden.shape
+    cols = qkv_weight.shape[1]
+    whole = lambda x: pl.BlockSpec(x.shape, lambda n: (0, 0))
+    return pl.pallas_call(
+        front_kernel,
+        grid=(cols // width,),
+        in_specs=[
+            whole(hidden),
+            whole(features),
+            whole(box_weight),
+            pl.BlockSpec((width, width), lambda n: (0, n)),
+            whole(qv_bias),
+        ],
+        out_specs=[whole(hidden), pl.BlockSpec((tokens, width), lambda n: (0, n))],
+        out_shape=[jax.ShapeDtypeStruct((tokens, width), BF), jax.ShapeDtypeStruct((tokens, cols), BF)],
+        compiler_params=pltpu.CompilerParams(vmem_limit_bytes=VMEM),
+        cost_estimate=SHORT,
+        name="front",
+    )(hidden, features, box_weight, qkv_weight, qv_bias)
+
+
+def feed_kernel(hid_ref, f_ref, box_ref, att_ref, wo_ref, bo_ref, n1_ref, w1_ref, b1_ref, w2_ref, b2_ref, n2_ref, cot_ref, z_ref, low_ref, act_ref, slope_ref, out_ref, dlow_ref, sum_ref, acc, *, chunk):
     step = pl.program_id(0)
     tokens = low_ref.shape[0]
 
     @pl.when(step == 0)
     def _():
-        acc[...] = jnp.zeros_like(acc)
+        for c in range(0, tokens, chunk):
+            cs = slice(c, c + chunk)
+            entry = hid_ref[cs, :].astype(F32) + dot(f_ref[cs, :], box_ref[...])
+            z = entry + (dot(att_ref[cs, :], wo_ref[...]) + bo_ref[...])
+            second = norm_forward(z, n1_ref[...])[0]
+            z_ref[cs, :] = z.astype(BF)
+            low_ref[cs, :] = second.astype(BF)
+            acc[cs, :] = second
 
     for c in range(0, tokens, chunk):
         cs = slice(c, c + chunk)
@@ -440,48 +492,47 @@
         sums = [0.0, 0.0, 0.0]
         for c in range(0, tokens, 128):
             cs = slice(c, c + 128)
-            result, normed, inverse = norm_forward(sec_ref[cs, :] + (acc[cs, :] + b2_ref[...]), n2_ref[...])
+            result, normed, inverse = norm_forward(acc[cs, :] + b2_ref[...], n2_ref[...])
             out_ref[cs, :] = result.astype(BF)
             up = cot_ref[cs, :].astype(F32)
-            grad = norm_backward(up, normed, inverse, n2_ref[...])
-            low = grad.astype(BF)
-            dsum_ref[cs, :] = grad
+            low = norm_backward(up, normed, inverse, n2_ref[...]).astype(BF)
             dlow_ref[cs, :] = low
             sums = [sums[0] + column_sums(up * normed), sums[1] + column_sums(up), sums[2] + column_sums(low.astype(F32))]
         sum_ref[...] = jnp.concatenate(sums + [jnp.zeros((5, sums[0].shape[1]), F32)], 0)
 
 
-def feed(second, second_low, w1, b1, w2, b2, norm_two, cotangent):
-    tokens, width = second.shape
-    hidden = w1.shape[1]
+def feed(hidden, features, box_weight, attended, out_weight, out_bias, norm_one, w1, b1, w2, b2, norm_two, cotangent):
+    tokens, width = hidden.shape
+    inner = w1.shape[1]
     tile = 512
     whole = lambda shape: pl.BlockSpec(shape, lambda n: (0, 0))
+    full = whole((tokens, width))
+    part = pl.BlockSpec((tokens, tile), lambda n: (0, n))
     return pl.pallas_call(
         partial(feed_kernel, chunk=256),
-        grid=(hidden // tile,),
+        grid=(inner // tile,),
         in_specs=[
-            whole((tokens, width)),
-            whole((tokens, width)),
+            full,
+            whole(features.shape),
+            whole(box_weight.shape),
+            full,
+            whole(out_weight.shape),
+            whole((1, width)),
+            whole((2, width)),
             pl.BlockSpec((width, tile), lambda n: (0, n)),
             pl.BlockSpec((1, tile), lambda n: (0, n)),
             pl.BlockSpec((tile, width), lambda n: (n, 0)),
             whole((1, width)),
             whole((2, width)),
-            whole((tokens, width)),
-        ],
-        out_specs=[
-            pl.BlockSpec((tokens, tile), lambda n: (0, n)),
-            pl.BlockSpec((tokens, tile), lambda n: (0, n)),
-            whole((tokens, width)),
-            whole((tokens, width)),
-            whole((tokens, width)),
-            whole((8, width)),
-        ],
+            full,
+        ],
+        out_specs=[full, full, part, part, full, full, whole((8, width))],
         out_shape=[
-            jax.ShapeDtypeStruct((tokens, hidden), BF),
-            jax.ShapeDtypeStruct((tokens, hidden), BF),
             jax.ShapeDtypeStruct((tokens, width), BF),
-            jax.ShapeDtypeStruct((tokens, width), F32),
+            jax.ShapeDtypeStruct((tokens, width), BF),
+            jax.ShapeDtypeStruct((tokens, inner), BF),
+            jax.ShapeDtypeStruct((tokens, inner), BF),
+            jax.ShapeDtypeStruct((tokens, width), BF),
             jax.ShapeDtypeStruct((tokens, width), BF),
             jax.ShapeDtypeStruct((8, width), F32),
         ],
@@ -489,16 +540,19 @@
         compiler_params=pltpu.CompilerParams(vmem_limit_bytes=VMEM),
         cost_estimate=SHORT,
         name="feed",
-    )(second, second_low, w1, b1.reshape(1, -1), w2, b2.reshape(1, -1), norm_two, cotangent)
-
-
-def feed_back_kernel(dlow_ref, dsum_ref, w1_ref, w2_ref, slope_ref, z_ref, n1_ref, din_ref, bias_ref, done_ref, dbr_ref, sum_ref, acc, *, chunk):
+    )(
+        hidden, features, box_weight, attended, out_weight, out_bias.reshape(1, -1), norm_one,
+        w1, b1.reshape(1, -1), w2, b2.reshape(1, -1), norm_two, cotangent,
+    )
+
+
+def feed_back_kernel(dlow_ref, w1_ref, w2_ref, slope_ref, z_ref, n1_ref, wo_ref, din_ref, bias_ref, dbr_ref, datt_ref, sum_ref, acc, *, chunk):
     step = pl.program_id(0)
     tokens = dlow_ref.shape[0]
 
     @pl.when(step == 0)
     def _():
-        acc[...] = dsum_ref[...]
+        acc[...] = dlow_ref[...].astype(F32)
 
     sums = 0.0
     for c in range(0, tokens, chunk):
@@ -514,11 +568,9 @@
         totals = [0.0, 0.0, 0.0]
         for c in range(0, tokens, 128):
             cs = slice(c, c + 128)
-            _, normed, inverse = norm_forward(z_ref[cs, :], n1_ref[...])
+            _, normed, inverse = norm_forward(z_ref[cs, :].astype(F32), n1_ref[...])
             up = acc[cs, :]
-            grad = norm_backward(up, normed, inverse, n1_ref[...])
-            low = grad.astype(BF)
-            done_ref[cs, :] = grad
+            low = norm_backward(up, normed, inverse, n1_ref[...]).astype(BF)
             dbr_ref[cs, :] = low
             totals = [
                 totals[0] + column_sums(up * normed),
@@ -526,36 +578,38 @@
                 totals[2] + column_sums(low.astype(F32)),
             ]
         sum_ref[...] = jnp.concatenate(totals + [jnp.zeros((5, totals[0].shape[1]), F32)], 0)
-
-
-def feed_back(d_outer, d_sum_two, w1, w2, slope, z_one, norm_one):
+        datt_ref[...] = dot(dbr_ref[...], wo_ref[...], 1, 1).astype(BF)
+
+
+def feed_back(d_outer, w1, w2, slope, z_one, norm_one, out_weight):
     tokens, width = z_one.shape
-    hidden = w1.shape[1]
+    inner = w1.shape[1]
     tile = 512
     whole = lambda shape: pl.BlockSpec(shape, lambda n: (0, 0))
+    full = whole((tokens, width))
     return pl.pallas_call(
         partial(feed_back_kernel, chunk=256),
-        grid=(hidden // tile,),
+        grid=(inner // tile,),
         in_specs=[
-            whole((tokens, width)),
-            whole((tokens, width)),
+            full,
             pl.BlockSpec((width, tile), lambda n: (0, n)),
             pl.BlockSpec((tile, width), lambda n: (n, 0)),
             pl.BlockSpec((tokens, tile), lambda n: (0, n)),
-            whole((tokens, width)),
+            full,
             whole((2, width)),
+            whole((width, width)),
         ],
         out_specs=[
             pl.BlockSpec((tokens, tile), lambda n: (0, n)),
             pl.BlockSpec((8, tile), lambda n: (0, n)),
-            whole((tokens, width)),
-            whole((tokens, width)),
+            full,
+            full,
             whole((8, width)),
         ],
         out_shape=[
-            jax.ShapeDtypeStruct((tokens, hidden), BF),
-            jax.ShapeDtypeStruct((8, hidden), F32),
-            jax.ShapeDtypeStruct((tokens, width), F32),
+            jax.ShapeDtypeStruct((tokens, inner), BF),
+            jax.ShapeDtypeStruct((8, inner), F32),
+            jax.ShapeDtypeStruct((tokens, width), BF),
             jax.ShapeDtypeStruct((tokens, width), BF),
             jax.ShapeDtypeStruct((8, width), F32),
         ],
@@ -563,7 +617,7 @@
         compiler_params=pltpu.CompilerParams(vmem_limit_bytes=VMEM),
         cost_estimate=SHORT,
         name="feed_back",
-    )(d_outer, d_sum_two, w1, w2, slope, z_one, norm_one)
+    )(d_outer, w1, w2, slope, z_one, norm_one, out_weight)
 
 
 UNIT = 384
@@ -723,11 +777,8 @@
         )
     for m in range(2):
         rows = jnp.where(upper, halves_of[1 - m], halves_of[m])
-        send = jnp.where(mine, rows[:, middle:], rows[:, :middle])
-        side = send.shape[0] // 2
-        outs[2 * m][...] = send[:side]
-        outs[2 * m + 1][...] = send[side:]
-        outs[4 + m][...] = jnp.where(mine, rows[:, :middle], rows[:, middle:])
+        outs[m][...] = jnp.where(mine, rows[:, middle:], rows[:, :middle])
+        outs[2 + m][...] = jnp.where(mine, rows[:, :middle], rows[:, middle:])
 
 
 def last_grads(place, x, dx, f, df, *sums):
@@ -736,8 +787,8 @@
     return pl.pallas_call(
         last_kernel,
         in_specs=[pl.BlockSpec(memory_space=pltpu.SMEM)] + [vmem] * (4 + len(sums)),
-        out_specs=[vmem] * 6,
-        out_shape=[jax.ShapeDtypeStruct((n * rows, UNIT), BF) for n in (1, 1, 1, 1, 2, 2)],
+        out_specs=[vmem] * 4,
+        out_shape=[jax.ShapeDtypeStruct((2 * rows, UNIT), BF)] * 4,
         compiler_params=pltpu.CompilerParams(vmem_limit_bytes=VMEM),
         cost_estimate=SHORT,
         name="last_grads",
@@ -745,13 +796,13 @@
 
 
 def lay_kernel(place_ref, *refs, kind, rows):
-    pieces, outs = refs[:4], refs[4:]
-    core, side = place_ref[0], place_ref[2]
-    step = pl.program_id(0)
+    last = refs[4:8] if kind == "heads" else refs[:4]
+    pieces, outs = refs[:4], refs[8 if kind == "heads" else 4 :]
+    core, step = place_ref[0], pl.program_id(0)
 
     def lay_piece(ref, owner):
         blocks = ref.shape[0] // rows
-        for n in range(ref.shape[0] // rows if kind != "heads" else 3):
+        for n in range(blocks):
             x = ref[n * rows : (n + 1) * rows, :].astype(F32)
             if kind == "long":
                 outs[0][n * rows : (n + 1) * rows, owner * UNIT : (owner + 1) * UNIT] = x
@@ -762,41 +813,46 @@
                 outs[0][:, owner * UNIT : (owner + 1) * UNIT] = x
             else:
                 lay_pair(x, owner * 2 + n - 1)
-        if kind == "heads":
-            lay_pair(ref[3 * rows : 4 * rows, :].astype(F32), 4 + owner)
-            at = 4 * rows
-            box = BOXF // 4
-            cols = slice(owner * UNIT, (owner + 1) * UNIT)
-            outs[2][:, cols] = ref[at : at + box, :].astype(F32)
-            small = ref[at + box : at + box + E_ROWS, :].astype(F32)
-
-            @pl.when(step == 0)
+
+    def lay_last(ref, owner):
+        lay_pair(ref[:rows, :].astype(F32), 4 + owner)
+        box = BOXF // 4
+        cols = slice(owner * UNIT, (owner + 1) * UNIT)
+        outs[2][:, cols] = ref[rows : rows + box, :].astype(F32)
+        small = ref[rows + box : rows + box + E_ROWS, :].astype(F32)
+
+        @pl.when(step == 0)
+        def _():
+            for n in range(3):
+                outs[3 + n][:, cols] = small[n : n + 1]
+            outs[6 + owner][...] = small[3]
+            for n in range(2):
+                at = n * 2 * UNIT + owner * UNIT
+                outs[8][at : at + UNIT] = small[4 + n]
+
+        if owner == 0:
+
+            @pl.when(step == 1)
             def _():
-                for n in range(3):
-                    outs[3 + n][:, cols] = small[n : n + 1]
-                outs[6 + owner][...] = small[3:4]
-                for n in range(2):
-                    at = n * 2 * UNIT + owner * UNIT
-                    outs[8][:, at : at + UNIT] = small[4 + n : 5 + n]
-
-            if owner == 0:
-
-                @pl.when(step == 1)
-                def _():
-                    outs[9][...] = jnp.concatenate([small[:, n * 128 : n * 128 + H] for n in range(3)], 1)
+                outs[9][...] = jnp.concatenate([small[:, n * 128 : n * 128 + H] for n in range(3)], 1)
 
     def lay_pair(x, pair):
         for m in range(3):
             at = (m * (H // 2) + pair) * 128
             outs[1][:, at : at + 128] = x[:, m * 128 : (m + 1) * 128]
 
-    for other_side in range(2):
-        for owner in range(2):
-            for other_core in range(2):
-
-                @pl.when(((step == side) == (other_side == 0)) & (core == (owner ^ other_core)))
-                def _():
-                    lay_piece(pieces[2 * other_side + other_core], owner)
+    def choose(refs, side, lay_one):
+        for other_side in range(2):
+            for owner in range(2):
+                for other_core in range(2):
+
+                    @pl.when(((step == side) == (other_side == 0)) & (core == (owner ^ other_core)))
+                    def _():
+                        lay_one(refs[2 * other_side + other_core], owner)
+
+    choose(pieces, place_ref[2], lay_piece)
+    if kind == "heads":
+        choose(last, place_ref[3], lay_last)
 
 
 def lay(place, pieces, kind, rows):
@@ -809,13 +865,13 @@
     else:
         width = 2 * UNIT
         shapes = [(2 * rows, width), (2 * rows, 3 * width), (BOXF // 2, width)]
-        whole = [(1, width)] * 3 + [(1, UNIT)] * 2 + [(1, 2 * width), (NB // 2, 3 * H)]
+        whole = [(1, width)] * 3 + [(UNIT,)] * 2 + [(2 * width,), (NB // 2, 3 * H)]
     return pl.pallas_call(
         partial(lay_kernel, kind=kind, rows=rows),
         grid=(2,),
         in_specs=[pl.BlockSpec(memory_space=pltpu.SMEM)] + [pl.BlockSpec(x.shape, lambda i: (0, 0)) for x in pieces],
         out_specs=[pl.BlockSpec((m // 2, n), lambda i: (i, 0)) for m, n in shapes]
-        + [pl.BlockSpec(shape, lambda i: (0, 0)) for shape in whole or []],
+        + [pl.BlockSpec(shape, lambda i, n=len(shape): (0,) * n) for shape in whole or []],
         out_shape=[jax.ShapeDtypeStruct(shape, F32) for shape in shapes + (whole or [])],
         compiler_params=pltpu.CompilerParams(vmem_limit_bytes=VMEM),
         cost_estimate=SHORT,
@@ -827,7 +883,7 @@
     pairs = H // 2
     weight = jnp.concatenate([w_ref[:, (m * pairs + n) * 128 : (m * pairs + n + 1) * 128] for n in range(pairs) for m in range(3)], 1)
     both = jnp.concatenate([a_ref[...], b_ref[...]], 1)
-    out_ref[...] = (sum_ref[...] + dot(both, weight, 1, 1)).astype(BF)
+    out_ref[...] = (sum_ref[...].astype(F32) + dot(both, weight, 1, 1)).astype(BF)
 
 
 def entry_grad(first, last, weight, base):
@@ -880,8 +936,6 @@
         return lax.ppermute(x, "doc", [(i, i ^ (1 << bit)) for i in range(docs)])
 
     def part(x, index, axis):
-        if isinstance(x, tuple):
-            return jnp.where(index == 0, *x)
         size = x.shape[axis] // 2
         return lax.dynamic_slice_in_dim(x, index * size, size, axis)
 
@@ -905,34 +959,43 @@
     my_lengths = part(lengths, half, 0)
     hidden_send = part(tie(hidden_in, box_part), 1 - half, 0)
     hidden = ordered(half, part(hidden_in, half, 0), swap_half(hidden_send), 1).reshape(tokens, width)
-    upstream = whole_windows(tie(cotangent, hidden_send), 0).reshape(tokens, width)
 
     bias, maps, features = score_bias(my_lengths, my_boxes, rel_tables)
-    entry = hidden.astype(F32) + dot(features, box_weight)
-    entry_low = entry.astype(BF)
-    qkv_shift = jnp.concatenate([qv_bias[0], jnp.zeros_like(qv_bias[0]), qv_bias[1]])
-    qkv = (dot(entry_low, qkv_weight) + qkv_shift).astype(BF)
-
+    upstream = whole_windows(tie(cotangent, maps), 0).reshape(tokens, width)
+    entry_low, qkv = front(hidden, features, box_weight, qkv_weight, qv_bias)
     attended, e, r = attend(my_lengths, qkv, bias)
-    z_one = entry + (dot(attended, out_weight) + out_bias)
-    second = norm_forward(z_one, norm_one)[0]
-    second_low = second.astype(BF)
-    active, slope, result, d_sum_two, d_outer, sums_two = feed(
-        second, second_low, ffn_in_weight, ffn_in_bias, ffn_out_weight, ffn_out_bias, norm_two, upstream
+    z_one, second_low, active, slope, result, d_outer, sums_two = feed(
+        hidden,
+        features,
+        box_weight,
+        attended,
+        out_weight,
+        out_bias,
+        norm_one,
+        ffn_in_weight,
+        ffn_in_bias,
+        ffn_out_weight,
+        ffn_out_bias,
+        norm_two,
+        upstream,
     )
+
     pairs, early = H // 2, H // 3
     late_pairs = pairs - early
     step = early // 2
     more = list(range(2, docs.bit_length() - 1))
-    place = jnp.stack([core, half, side]).astype(jnp.int32)
+    place = jnp.stack([core, half, side, (doc >> 2) & 1]).astype(jnp.int32)
     last = [None]
 
     def now(x):
-        return x if last[0] is None else tie(x, last[0])
-
-    def then(x):
-        last[0] = x
+        return x if last[0] is None else tie(x, *last[0])
+
+    def then(x, *more):
+        last[0] = (x,) + more
         return x
+
+    def joined(pieces):
+        return jnp.concatenate(pieces, 0) if len(pieces) > 1 else pieces[0]
 
     def total(*xs):
         out = xs[0].astype(F32)
@@ -942,14 +1005,18 @@
 
     class Chain:
         def core(self, *parts):
-            send, send_own, keep, keep_own = parts[:PIECES], parts[PIECES:-2], parts[-2], parts[-1]
+            pieces, keep, keep_own = parts[:-2], parts[-2], parts[-1]
+            count = len(pieces) // 2
             then(keep_own)
-            self.keep, self.come = keep, jnp.concatenate([swap_doc(x, 0) for x in send], 0)
-            self.own = [keep_own, tuple(swap_doc(x, 0) for x in send_own)]
+            pieces = [swap_doc(x, 0) for x in pieces]
+            self.own = [keep, pieces[:count], keep_own, pieces[count:]]
 
         def half(self):
-            send = then(total(now(self.keep), self.come))
-            self.own.append(swap_half(send))
+            keep, come, keep_own, come_own = self.own
+            keep, keep_own = lax.optimization_barrier((keep, keep_own) + last[0])[:2]
+            send, own = total(keep, joined(come)), total(keep_own, joined(come_own))
+            then(send, own)
+            self.own = [own, swap_half(send)]
 
         def split(self, bit):
             b = (doc >> bit) & 1
@@ -964,13 +1031,23 @@
                 x = total(x, swap_doc(x, bit))
             self.own = [x, swap_doc(x, bits[-1])]
 
-        def gather(self):
+        def back(self, bit):
             x = then(total(now(self.own[0]), *self.own[1:]))
-            self.mine, self.across = x, swap_doc(x, 1)
+            self.parted, self.own = bit, [x, swap_doc(x, bit)]
+
+        def gather(self, bit=1):
+            if hasattr(self, "parted"):
+                x = then(ordered((doc >> self.parted) & 1, now(self.own[0]), self.own[1], 0))
+            else:
+                x = then(total(now(self.own[0]), *self.own[1:]))
+            self.mine, self.across = x, swap_doc(x, bit)
             self.beside = swap_doc(x, 0)
 
+        def settle(self, *others):
+            then(*last[0], self.beside, *others)
+
         def pieces(self):
-            return [now(self.mine), self.beside, self.across, swap_doc(self.across, 0)]
+            return [now(self.mine), self.beside, self.across, swap_doc(now(self.across), 0)]
 
     def back(first, count, total_pairs, at, before):
         out = attend_back(qkv, e, r, attended, now(d_attended), first, count, total_pairs, at, before)
@@ -982,63 +1059,69 @@
     then(d_outer)
     a.core(*long_grads(place, active, now(d_outer)))
     a.half()
-    d_inner, sums_in, d_sum_one, d_branch, sums_one = feed_back(
-        now(d_outer), d_sum_two, ffn_in_weight, ffn_out_weight, slope, z_one, norm_one
+    d_inner, sums_in, d_branch, d_attended, sums_one = feed_back(
+        now(d_outer), ffn_in_weight, ffn_out_weight, slope, z_one, norm_one, out_weight
     )
     then(d_branch)
     a.split(1)
     b.core(*wide_grads(place, [(second_low, now(d_inner))]))
-    d_attended = then(dot(now(d_branch), out_weight, 1, 1).astype(BF))
-    a.double(more[:1])
+    a.split(more[0])
     b.half()
     first_right, ds_0, line_0, qv_0 = back(0, step, early, 0, None)
     a.double(more[1:])
     first_right, ds_1, line_1, qv_1 = back(step, early - step, early, step, first_right)
+    a.back(more[0])
+    b.split(1)
     c.core(*wide_grads(place, [(attended, d_branch), (entry_low, now(first_right))]))
-    b.split(1)
     c.half()
-    result = result.reshape(windows, length, width)
-    out_send = then(part(now(result), 1 - half, 1))
-    out_mine, out_other = part(result, half, 1), swap_half(out_send)
     last_right, ds_2, line_2, qv_2 = back(early, late_pairs, late_pairs, 0, None)
-    b.double(more[:1])
+    a.gather()
+    b.split(more[0])
     small_0, line_grad = table_grads([ds_0, ds_1, now(ds_2)], [line_0, line_1, line_2], maps, 0)
     then(small_0)
-    a.gather()
+    a.settle(a.across)
+    b.double(more[1:])
     c.split(1)
-    b.double(more[1:])
-    layer_out = then(ordered(half, now(out_mine), out_other, 0))
+    d_entry_low = then(entry_grad(first_right, now(last_right), qkv_weight, d_branch))
+    c.split(more[0])
+    b.back(more[0])
+    d_entry = d_entry_low.reshape(windows, length, width)
+    grad_send = then(part(now(d_entry), 1 - half, 1))
+    grad_mine, grad_other = part(d_entry, half, 1), swap_half(grad_send)
     small_1 = table_grads([ds_0, ds_1, now(ds_2)], [], maps, 1)[0]
     for w in range(2, windows):
         small_1 = small_1 + table_grads([ds_0, ds_1, ds_2], [], maps, w)[0]
     then(small_1)
-    c.double(more[:1])
-    d_entry_low = then(entry_grad(first_right, now(last_right), qkv_weight, d_sum_one))
+    c.double(more[1:])
+    b.gather()
+    then(*last[0], grad_other)
     d.core(
         *last_grads(
             place, entry_low, last_right, features, now(d_entry_low), sums_two, sums_one, sums_in, qv_0, qv_1, qv_2, line_grad, small_0, small_1
         )
     )
-    b.gather()
-    c.double(more[1:])
+    c.back(more[0])
     d.half()
-    d_entry = d_entry_low.reshape(windows, length, width)
-    grad_send = then(part(now(d_entry), 1 - half, 1))
-    grad_mine, grad_other = part(d_entry, half, 1), swap_half(grad_send)
     (ffn_out_grad,) = lay(place, a.pieces(), "long", block_rows)
     then(ffn_out_grad)
-    d.split(1)
+    d.split(more[0])
+    result = result.reshape(windows, length, width)
+    out_send = then(part(now(result), 1 - half, 1))
+    out_mine, out_other = part(result, half, 1), swap_half(out_send)
+    c.gather()
+    b.settle()
+    d.double(more[1:])
     (ffn_in_grad,) = lay(place, b.pieces(), "wide", block_rows)
     then(ffn_in_grad)
-    d.double(more[:1])
+    d.double([1])
     hidden_grad = then(ordered(half, now(grad_mine), grad_other, 0))
-    d.double(more[1:])
-    parts = [total(now(c.own[0]), c.own[1]), total(d.own[0], d.own[1])]
-    c.own = [then(jnp.concatenate(parts, 0))]
-    c.gather()
+    c.settle()
+    c_pieces = c.pieces()
+    d.gather(more[0])
     out_grad, qkv_grad, box, two, one, qv, out_sum, ffn_out_sum, ffn_in_sum, table = lay(
-        place, c.pieces(), "heads", block_rows
+        place, c_pieces + d.pieces(), "heads", block_rows
     )
+    layer_out = ordered(half, now(out_mine), out_other, 0)
     return (
         layer_out,
         hidden_grad,
@@ -1046,13 +1129,13 @@
         qkv_grad,
         qv,
         out_grad,
-        out_sum.reshape(-1),
+        out_sum,
         table,
         one,
         ffn_in_grad,
-        ffn_in_sum.reshape(-1),
+        ffn_in_sum,
         ffn_out_grad,
-        ffn_out_sum.reshape(-1),
+        ffn_out_sum,
         two,
     )
 

time: 385 us -> 347 us (0.901)
  waiting for transfers between devices: 68.8 us -> 41.3 us
  matrix products: 11.9 us -> 0 us
  Pallas kernels: 219 us -> 229 us
    ppermute x37 -> x41, waiting for transfers between devices: 56 us -> 34 us  [swap_doc(): return lax.ppermute(x, 'doc', [(i, i ^ 1 << bit) for i in range(docs)])]
    dot_general x4 -> x0, matrix products: 11.9 us -> none  [dot(): lax.dot_general(a, b, (((ca,), (cb,)), ((), ())), preferred_element_type=...]
    pallas_call x2 -> x3, Pallas kernels: 53.1 us -> 63.4 us  [the longest x1 32.6 us: feed(): pl.pallas_call(partial(feed_kernel, chunk=256), grid=(inner // tile,), in...]
    ppermute x9, waiting for transfers between devices: 12.8 us -> 7.3 us  [swap_half(): return lax.ppermute(x, 'half', [(0, 1), (1, 0)])]
    pallas_call x3 -> x0, other arithmetic: 3.86 us -> none  [lay(): pl.pallas_call(partial(lay_kernel, kind=kind, rows=rows), grid=(2,), in_s...]
    select_n x4 -> x8, other arithmetic: 6.38 us -> 10 us  [ordered(): jnp.where(index == 0, jnp.concatenate([mine, other], axis), jnp.concatena...]
    convert_element_type x20 -> x24, other arithmetic: 11.4 us -> 12.5 us  [total(): return out.astype(BF)]
    ppermute x37 -> x41, starting transfers between devices: 30.8 us -> 29.8 us  [swap_doc(): return lax.ppermute(x, 'doc', [(i, i ^ 1 << bit) for i in range(docs)])]
  transfers between devices with their start and end apart: 46 -> 50, of which waited for: 16 -> 17; matrix products, arithmetic and copies ran while one was open for 5% -> 6% of each run, Pallas kernels for 41% -> 50%
where the time goes in v2:
time: 347 us; the launch traced here: 342 us
  Pallas kernels  229 us (66%)
  waiting for transfers between devices  41.3 us (12%)
  starting transfers between devices  38.3 us (11%)
  other arithmetic  23.1 us (7%)
  local copies, waits for them, and re-layouts  8.76 us (3%)
    ppermute x41, waiting for transfers between devices, swap_doc(): return lax.ppermute(x, 'doc', [(i, i ^ 1 << bit) for i in range(docs)])  34 us
    pallas_call x1, Pallas kernels, feed(): pl.pallas_call(partial(feed_kernel, chunk=256), grid=(inner // tile,), in...  32.6 us
    pallas_call x3, Pallas kernels, attend_back(): pl.pallas_call(partial(attend_back_kernel, chunk=64), grid=(count, window...  31.5 us
    pallas_call x1, Pallas kernels, score_bias(): pl.pallas_call(partial(bias_kernel, tile=tile, rows=rows), grid=(windows,...  31.5 us
    ppermute x41, starting transfers between devices, swap_doc(): return lax.ppermute(x, 'doc', [(i, i ^ 1 << bit) for i in range(docs)])  29.8 us
    pallas_call x2, Pallas kernels, table_grads(): pl.pallas_call(partial(table_kernel, parts=parts, with_line=bool(lines)),...  26.1 us
    pallas_call x1, Pallas kernels, feed_back(): pl.pallas_call(partial(feed_back_kernel, chunk=256), grid=(inner // tile,...  22.5 us
    pallas_call x2, Pallas kernels, wide_grads(): pl.pallas_call(partial(wide_grads_kernel, counts=counts), grid_spec=pltpu...  20.2 us
  transfers between devices with their start and end apart: 50, of which 17 were waited for; matrix products, arithmetic and copies ran while one was open for 6% of the time, Pallas kernels for 50%

profile of v2, /device:TPU:1, one launch (start us, length us, event | category | flops | bytes accessed | tf_op | source)
XLA Modules:
  0.0 341.8 jit_solution(710331710501743055)
XLA Ops:
  6.9 31.5 %score_bias.1 = (bf16[2,12,512,512]{3,2,1,0:T(8,128)(2,1)}, bf16[2,2,512,512]{3,2,1,0:T(8,128)(2,1)}, bf16[1024,128]{1,0:T(8,128)(2,1)}) custom-call(s32[2]{0:T(128)} %dynamic_slice.120.len_ref, s32[4,2,512]{2,1,0:T(2,128)} %add_select_fusion.box_ref, f32[32,36]{1,0:T(8,128)} %rel_ref.1, f32[8,128]{1,0:T(8,128)} %constant.38.clone.freq_ref), custom_call_target="tpu_custom_call" | custom-call | flops 1 | bytes 1 | tf_op jit(solution)/shard_map/score_bias/pallas_call | solution.py:154
  44.7 8.3 %front.1 = (bf16[1024,768]{1,0:T(8,128)(2,1)}, bf16[1024,2304]{1,0:T(8,128)(2,1)}) custom-call(bf16[1024,768]{1,0:T(8,128)(2,1)} %bitcast.21, bf16[1024,128]{1,0:T(8,128)(2,1)} %get-tuple-element.133.f_ref, bf16[128,768]{1,0:T(8,128)(2,1)} %box_ref.3, bf16[768,2304]{1,0:T(8,128)(2,1)} %w_ref.3, f32[2,768]{1,0:T(2,128)} %qv_ref.1), custom_call_target="tpu_custom_call" | custom-call | flops 1 | bytes 1 | tf_op jit(solution)/shard_map/front/pallas_call | solution.py:449
  53.0 18.8 %attend.1 = (bf16[1024,768]{1,0:T(8,128)(2,1)}, bf16[2,12,512,512]{3,2,1,0:T(8,128)(2,1)}, f32[1024,768]{1,0:T(8,128)}) custom-call(s32[2]{0:T(128)} %dynamic_slice.120.len_ref, bf16[1024,2304]{1,0:T(8,128)(2,1)} %get-tuple-element.134.q_ref.k_ref.v_ref, bf16[1024,2304]{1,0:T(8,128)(2,1)} %get-tuple-element.134.q_ref.k_ref.v_ref, ...), custom_call_target="tpu_custom_call" | custom-call | flops 1 | bytes 1 | tf_op jit(solution)/shard_map/attend/pallas_call | solution.py:212
  74.8 32.6 %feed.1 = (bf16[1024,768]{1,0:T(8,128)(2,1)}, bf16[1024,768]{1,0:T(8,128)(2,1)}, bf16[1024,3072]{1,0:T(8,128)(2,1)}, bf16[1024,3072]{1,0:T(8,128)(2,1)}, bf16[10...) custom-call(bf16[1024,768]{1,0:T(8,128)(2,1)} %bitcast.22, ...), custom_call_target="tpu_custom_call" | custom-call | flops 1 | bytes 1 | tf_op jit(solution)/shard_map/feed/pallas_call | solution.py:511
  107.4 10.9 %long_grads.1 = (bf16[768,384]{1,0:T(8,128)(2,1)}, bf16[768,384]{1,0:T(8,128)(2,1)}, bf16[768,384]{1,0:T(8,128)(2,1)}, bf16[768,384]{1,0:T(8,128)(2,1)}, bf16[15...) custom-call(s32[4]{0:T(128)} %pad_add_fusion.place_ref, bf16[1024,3072]{1,0:T(8,128)(2,1)} %get-tuple-element.144.left_ref, ...), custom_call_target="tpu_custom_call" | custom-call | flops 1 | bytes 1 | tf_op jit(solution)/shard_map/long_grads/pallas_call | solution.py:714
  131.1 22.5 %feed_back.1 = (bf16[1024,3072]{1,0:T(8,128)(2,1)}, f32[8,3072]{1,0:T(8,128)}, bf16[1024,768]{1,0:T(8,128)(2,1)}, bf16[1024,768]{1,0:T(8,128)(2,1)}, f32[8,768]{1,0:T(8,128)}) custom-call(bf16[1024,768]{1,0:T(8,128)(2,1)} %get-tuple-element.154.send_ref.keep_ref.dlow_ref, bf16[768,3072]{1,0:T(8,128)(2,1)} %w1_ref.3, bf16[3072,768]{1,0:T(8,128)(2,1)} %w2_ref.3, ...), custom_call_target="tpu_custom_call" | custom-call | flops 1 | bytes 1 | tf_op jit(solution)/shard_map/feed_back/pallas_call | solution.py:590
  156.1 10.2 %wide_grads.2 = (bf16[1,4,192,384]{3,2,1,0:T(8,128)(2,1)}, bf16[1,4,192,384]{3,2,1,0:T(8,128)(2,1)}, bf16[1,4,192,384]{3,2,1,0:T(8,128)(2,1)}, bf16[1,4,192,384]...) custom-call(s32[4]{0:T(128)} %pad_add_fusion.place_ref, ...), custom_call_target="tpu_custom_call" | custom-call | flops 1 | bytes 1 | tf_op jit(solution)/shard_map/wide_grads/pallas_call | solution.py:676
  172.7 10.4 %attend_back.3 = (bf16[1024,1536]{1,0:T(8,128)(2,1)}, bf16[2,4,512,512]{3,2,1,0:T(8,128)(2,1)}, f32[4,128,896]{2,1,0:T(8,128)}, f32[8,768]{1,0:T(8,128)}) custom-call(bf16[1024,2304]{1,0:T(8,128)(2,1)} %get-tuple-element.134.q_ref.k_ref.v_ref, bf16[1024,2304]{1,0:T(8,128)(2,1)} %get-tuple-element.134.q_ref.k_ref.v_ref, ...), custom_call_target="tpu_custom_call" | custom-call | flops 1 | bytes 1 | tf_op jit(solution)/shard_map/attend_back/pallas_call | solution.py:285
  185.6 10.6 %attend_back.4 = (bf16[1024,1536]{1,0:T(8,128)(2,1)}, bf16[2,4,512,512]{3,2,1,0:T(8,128)(2,1)}, f32[4,128,896]{2,1,0:T(8,128)}, f32[8,768]{1,0:T(8,128)}) custom-call(bf16[1024,2304]{1,0:T(8,128)(2,1)} %get-tuple-element.134.q_ref.k_ref.v_ref, bf16[1024,2304]{1,0:T(8,128)(2,1)} %get-tuple-element.134.q_ref.k_ref.v_ref, ...), custom_call_target="tpu_custom_call", output_to_operand_aliasing={{0}: (7, {})} | custom-call | flops 1 | bytes 1 | tf_op jit(solution)/shard_map/attend_back/pallas_call | solution.py:285
  200.6 9.9 %wide_grads.3 = (bf16[1,3,192,384]{3,2,1,0:T(8,128)(2,1)}, bf16[1,3,192,384]{3,2,1,0:T(8,128)(2,1)}, bf16[1,3,192,384]{3,2,1,0:T(8,128)(2,1)}, bf16[1,3,192,384]...) custom-call(s32[4]{0:T(128)} %pad_add_fusion.place_ref, ...), custom_call_target="tpu_custom_call" | custom-call | flops 1 | bytes 1 | tf_op jit(solution)/shard_map/wide_grads/pallas_call | solution.py:676
  216.4 10.5 %attend_back.5 = (bf16[1024,768]{1,0:T(8,128)(2,1)}, bf16[2,4,512,512]{3,2,1,0:T(8,128)(2,1)}, f32[4,128,896]{2,1,0:T(8,128)}, f32[8,768]{1,0:T(8,128)}) custom-call(bf16[1024,2304]{1,0:T(8,128)(2,1)} %get-tuple-element.134.q_ref.k_ref.v_ref, bf16[1024,2304]{1,0:T(8,128)(2,1)} %get-tuple-element.134.q_ref.k_ref.v_ref, ...), custom_call_target="tpu_custom_call" | custom-call | flops 1 | bytes 1 | tf_op jit(solution)/shard_map/attend_back/pallas_call | solution.py:285
  230.6 14.4 %table_grads.2 = (f32[16,64]{1,0:T(8,128)}, f32[16,32]{1,0:T(8,128)}) custom-call(bf16[2,4,512,512]{3,2,1,0:T(8,128)(2,1)} %get-tuple-element.192.refs_0_, bf16[2,4,512,512]{3,2,1,0:T(8,128)(2,1)} %get-tuple-element.193.refs_1_, bf16[2,4,512,512]{3,2,1,0:T(8,128)(2,1)} %get-tuple-element.206.refs_2_, f32[4,128,896]{2,1,0:T(8,128)} %get-tuple-element.196.refs_3_, ...), custom_call_target="tpu_custom_call" | custom-call | flops 1 | bytes 1 | tf_op jit(solution)/shard_map/table_grads/pallas_call | solution.py:385
  249.0 8.4 %entry_grad.1.df_ref = bf16[1024,768]{1,0:T(8,128)(2,1)} custom-call(bf16[1024,1536]{1,0:T(8,128)(2,1)} %get-tuple-element.179.refs_4_.refs_5_.a_ref, bf16[1024,768]{1,0:T(8,128)(2,1)} %get-tuple-element.202.b_ref.dx_ref, bf16[768,2304]{1,0:T(8,128)(2,1)} %w_ref.3, bf16[1024,768]{1,0:T(8,128)(2,1)} %get-tuple-element.158.refs_1_.refs_2_.sum_ref), custom_call_target="tpu_custom_call" | custom-call | flops 1 | bytes 1 | tf_op jit(solution)/shard_map/entry_grad/pallas_call | solution.py:893
  257.6 5.8 %collective-permute-done.27 = bf16[384,384]{1,0:T(8,128)(2,1)S(1)} collective-permute-done((bf16[384,384]{1,0:T(8,128)(2,1)S(1)}, bf16[384,384]{1,0:T(8,128)(2,1)S(1)}, u32[]{:S(2)}, u32[]{:S(2)}) %collective-permute-start.27) | collective-permute-done | bytes 294944 | tf_op jit(solution)/shard_map/ppermute | solution.py:936
  265.9 11.8 %table_grads.3.refs_5_ = f32[16,64]{1,0:T(8,128)} custom-call(bf16[2,4,512,512]{3,2,1,0:T(8,128)(2,1)} %get-tuple-element.192.refs_0_, bf16[2,4,512,512]{3,2,1,0:T(8,128)(2,1)} %get-tuple-element.193.refs_1_, bf16[2,4,512,512]{3,2,1,0:T(8,128)(2,1)} %get-tuple-element.206.refs_2_, bf16[2,2,512,512]{3,2,1,0:T(8,128)(2,1)} %get-tuple-element.137.refs_6_.refs_3_), custom_call_target="tpu_custom_call" | custom-call | flops 1 | bytes 1 | tf_op jit(solution)/shard_map/table_grads/pallas_call | solution.py:385
  278.4 3.9 %collective-permute-done.30 = bf16[2,256,768]{2,1,0:T(8,128)(2,1)S(1)} collective-permute-done((bf16[2,256,768]{2,1,0:T(8,128)(2,1)S(1)}, bf16[2,256,768]{2,1,0:T(8,128)(2,1)S(1)}, u32[]{:S(2)}, u32[]{:S(2)}) %collective-permute-start.30) | collective-permute-done | bytes 786464 | tf_op jit(solution)/shard_map/ppermute | solution.py:933
  282.2 5.6 %last_grads.1 = (bf16[480,384]{1,0:T(8,128)(2,1)}, bf16[480,384]{1,0:T(8,128)(2,1)}, bf16[480,384]{1,0:T(8,128)(2,1)}, bf16[480,384]{1,0:T(8,128)(2,1)}) custom-call(s32[4]{0:T(128)} %pad_add_fusion.place_ref, bf16[1024,768]{1,0:T(8,128)(2,1)} %get-tuple-element.140.refs_3_.x_ref, bf16[1024,768]{1,0:T(8,128)(2,1)} %get-tuple-element.202.b_ref.dx_ref, ...), custom_call_target="tpu_custom_call" | custom-call | flops 1 | bytes 1 | tf_op jit(solution)/shard_map/last_grads/pallas_call | solution.py:787
  295.1 4.1 %lay.3 = f32[1536,768]{1,0:T(8,128)} custom-call(s32[4]{0:T(128)} %pad_add_fusion.place_ref, bf16[768,384]{1,0:T(8,128)(2,1)} %copy-done.4, bf16[768,384]{1,0:T(8,128)(2,1)} %collective-permute-done.22.refs_1_, bf16[768,384]{1,0:T(8,128)(2,1)} %collective-permute-done.23.refs_2_, bf16[768,384]{1,0:T(8,128)(2,1)} %copy-done.18), custom_call_target="tpu_custom_call" | custom-call | flops 1 | bytes 1 | tf_op jit(solution)/shard_map/lay/pallas_call | solution.py:869
  299.2 3.4 collective-permute-done.35
  303.1 5.1 %collective-permute-done.38 = bf16[240,384]{1,0:T(8,128)(2,1)S(1)} collective-permute-done((bf16[240,384]{1,0:T(8,128)(2,1)S(1)}, bf16[240,384]{1,0:T(8,128)(2,1)S(1)}, u32[]{:S(2)}, u32[]{:S(2)}) %collective-permute-start.38) | collective-permute-done | bytes 184352 | tf_op jit(solution)/shard_map/ppermute | solution.py:936
  313.5 4.0 %lay.4 = f32[384,3072]{1,0:T(8,128)} custom-call(s32[4]{0:T(128)} %pad_add_fusion.place_ref, bf16[768,384]{1,0:T(8,128)(2,1)} %copy-done.5, bf16[768,384]{1,0:T(8,128)(2,1)} %copy-done.17, bf16[768,384]{1,0:T(8,128)(2,1)} %collective-permute-done.39.refs_2_, bf16[768,384]{1,0:T(8,128)(2,1)} %copy-done.19), custom_call_target="tpu_custom_call" | custom-call | flops 1 | bytes 1 | tf_op jit(solution)/shard_map/lay/pallas_call | solution.py:869
  317.5 3.7 %collective-permute-done.41 = bf16[240,384]{1,0:T(8,128)(2,1)S(1)} collective-permute-done((bf16[240,384]{1,0:T(8,128)(2,1)S(1)}, bf16[240,384]{1,0:T(8,128)(2,1)S(1)}, u32[]{:S(2)}, u32[]{:S(2)}) %collective-permute-start.41) | collective-permute-done | bytes 184352 | tf_op jit(solution)/shard_map/ppermute | solution.py:936
  323.1 3.9 %collective-permute-done.43 = bf16[240,384]{1,0:T(8,128)(2,1)S(1)} collective-permute-done((bf16[240,384]{1,0:T(8,128)(2,1)S(1)}, bf16[240,384]{1,0:T(8,128)(2,1)S(1)}, u32[]{:S(2)}, u32[]{:S(2)}) %collective-permute-start.43) | collective-permute-done | bytes 184352 | tf_op jit(solution)/shard_map/ppermute | solution.py:936
  337.2 4.1 %lay.5 = (f32[384,768]{1,0:T(8,128)}, f32[384,2304]{1,0:T(8,128)}, f32[64,768]{1,0:T(8,128)}, f32[1,768]{1,0:T(1,128)}, f32[1,768]{1,0:T(1,128)}, /*index=5*/f32...) custom-call(s32[4]{0:T(128)} %pad_add_fusion.place_ref, bf16[576,384]{1,0:T(8,128)(2,1)} %copy-done.6, ...), custom_call_target="tpu_custom_call" | custom-call | flops 1 | bytes 1 | tf_op jit(solution)/shard_map/lay/pallas_call | solution.py:869
  (196 shorter events, 85.6 us)
Async XLA Ops:
  5.1 36.5 %collective-permute-start.1 = (bf16[2,256,768]{2,1,0:T(8,128)(2,1)S(1)}, bf16[2,256,768]{2,1,0:T(8,128)(2,1)}, u32[]{:S(2)}, u32[]{:S(2)}) collective-permute-start(bf16[2,256,768]{2,1,0:T(8,128)(2,1)S(1)} %constant_dynamic-slice_fusion.7), channel_id=1, source_target_pairs={{0,1},{1,0},{2,3},{3,2},{4,5},{5,4},{6,7},{7,6},{8,9},{9,8},{10,11... | collective-permute-start | bytes 2359304 | tf_op jit(solution)/shard_map/ppermute | solution.py:933
  39.4 32.3 %collective-permute-start.2 = (bf16[2,256,768]{2,1,0:T(8,128)(2,1)}, bf16[2,256,768]{2,1,0:T(8,128)(2,1)}, u32[]{:S(2)}, u32[]{:S(2)}) collective-permute-start(bf16[2,256,768]{2,1,0:T(8,128)(2,1)} %get-tuple-element.257), channel_id=1, source_target_pairs={{0,1},{1,0},{2,3},{3,2},{4,5},{5,4},{6,7},{7,6},{8,9},{9,8},{10,11... | collective-permute-start | bytes 2359304 | tf_op jit(solution)/shard_map/ppermute | solution.py:933
  124.3 29.4 %collective-permute-start.7 = (bf16[1536,384]{1,0:T(8,128)(2,1)S(1)}, bf16[1536,384]{1,0:T(8,128)(2,1)S(1)}, u32[]{:S(2)}, u32[]{:S(2)}) collective-permute-start(bf16[1536,384]{1,0:T(8,128)(2,1)S(1)} %add_convert_fusion.3), channel_id=1, source_target_pairs={{0,1},{1,0},{2,3},{3,2},{4,5},{5,4},{6,7},{7,6},{8,9},{9,8},{10,11... | collective-permute-start | bytes 3538952 | tf_op jit(solution)/shard_map/ppermute | solution.py:933
  154.8 14.8 %collective-permute-start.8 = (bf16[768,384]{1,0:T(8,128)(2,1)}, bf16[768,384]{1,0:T(8,128)(2,1)S(1)}, u32[]{:S(2)}, u32[]{:S(2)}) collective-permute-start(bf16[768,384]{1,0:T(8,128)(2,1)} %get-tuple-element.253), channel_id=1, source_target_pairs={{0,4},{2,6},{4,0},{6,2},{8,12},{10,14},{12,8},{14,10},{16,20},{18,... | collective-permute-start | bytes 1769480 | tf_op jit(solution)/shard_map/ppermute | solution.py:936
  169.7 13.3 %collective-permute-start.13 = (bf16[384,384]{1,0:T(8,128)(2,1)S(1)}, bf16[384,384]{1,0:T(8,128)(2,1)S(1)}, u32[]{:S(2)}, u32[]{:S(2)}) collective-permute-start(bf16[384,384]{1,0:T(8,128)(2,1)S(1)} %get-tuple-element.261), channel_id=1, source_target_pairs={{0,8},{2,10},{4,12},{6,14},{8,0},{10,2},{12,4},{14,6},{16,24},{18,... | collective-permute-start | bytes 884744 | tf_op jit(solution)/shard_map/ppermute | solution.py:936
  171.4 28.0 %collective-permute-start.15 = (bf16[1536,384]{1,0:T(8,128)(2,1)S(1)}, bf16[1536,384]{1,0:T(8,128)(2,1)S(1)}, u32[]{:S(2)}, u32[]{:S(2)}) collective-permute-start(bf16[1536,384]{1,0:T(8,128)(2,1)S(1)} %add_convert_fusion.1), channel_id=1, source_target_pairs={{0,1},{1,0},{2,3},{3,2},{4,5},{5,4},{6,7},{7,6},{8,9},{9,8},{10,11... | collective-permute-start | bytes 3538952 | tf_op jit(solution)/shard_map/ppermute | solution.py:933
  183.2 16.2 %collective-permute-start.14 = (bf16[384,384]{1,0:T(8,128)(2,1)S(1)}, bf16[384,384]{1,0:T(8,128)(2,1)S(1)}, u32[]{:S(2)}, u32[]{:S(2)}) collective-permute-start(bf16[384,384]{1,0:T(8,128)(2,1)S(1)} %add_convert_fusion.19), channel_id=1, source_target_pairs={{0,16},{2,18},{4,20},{6,22},{8,24},{10,26},{12,28},{14,30},{16,0},... | collective-permute-start | bytes 884744 | tf_op jit(solution)/shard_map/ppermute | solution.py:936
  211.2 15.7 %collective-permute-start.20 = (bf16[384,384]{1,0:T(8,128)(2,1)S(1)}, bf16[384,384]{1,0:T(8,128)(2,1)S(1)}, u32[]{:S(2)}, u32[]{:S(2)}) collective-permute-start(bf16[384,384]{1,0:T(8,128)(2,1)S(1)} %add_convert_fusion.18), channel_id=1, source_target_pairs={{0,8},{2,10},{4,12},{6,14},{8,0},{10,2},{12,4},{14,6},{16,24},{18,... | collective-permute-start | bytes 884744 | tf_op jit(solution)/shard_map/ppermute | solution.py:936
  211.2 17.8 %collective-permute-start.21 = (bf16[768,384]{1,0:T(8,128)(2,1)}, bf16[768,384]{1,0:T(8,128)(2,1)S(1)}, u32[]{:S(2)}, u32[]{:S(2)}) collective-permute-start(bf16[768,384]{1,0:T(8,128)(2,1)} %get-tuple-element.251), channel_id=1, source_target_pairs={{0,4},{2,6},{4,0},{6,2},{8,12},{10,14},{12,8},{14,10},{16,20},{18,... | collective-permute-start | bytes 1769480 | tf_op jit(solution)/shard_map/ppermute | solution.py:936
  215.8 29.3 %collective-permute-start.25 = (bf16[1152,384]{1,0:T(8,128)(2,1)}, bf16[1152,384]{1,0:T(8,128)(2,1)S(1)}, u32[]{:S(2)}, u32[]{:S(2)}) collective-permute-start(bf16[1152,384]{1,0:T(8,128)(2,1)} %add_convert_fusion.5), channel_id=1, source_target_pairs={{0,1},{1,0},{2,3},{3,2},{4,5},{5,4},{6,7},{7,6},{8,9},{9,8},{10,11... | collective-permute-start | bytes 2654216 | tf_op jit(solution)/shard_map/ppermute | solution.py:933
  227.1 17.8 %collective-permute-start.22 = (bf16[768,384]{1,0:T(8,128)(2,1)S(1)}, bf16[768,384]{1,0:T(8,128)(2,1)}, u32[]{:S(2)}, u32[]{:S(2)}) collective-permute-start(bf16[768,384]{1,0:T(8,128)(2,1)S(1)} %maximum_select_fusion.4.refs_0_), channel_id=1, source_target_pairs={{0,2},{2,0},{4,6},{6,4},{8,10},{10,8},{12,14},{14,12},{16,18},{18,... | collective-permute-start | bytes 1769480 | tf_op jit(solution)/shard_map/ppermute | solution.py:936
  227.8 17.1 %collective-permute-start.23 = (bf16[768,384]{1,0:T(8,128)(2,1)S(1)}, bf16[768,384]{1,0:T(8,128)(2,1)}, u32[]{:S(2)}, u32[]{:S(2)}) collective-permute-start(bf16[768,384]{1,0:T(8,128)(2,1)S(1)} %maximum_select_fusion.4.refs_0_), channel_id=1, source_target_pairs={{0,4},{2,6},{4,0},{6,2},{8,12},{10,14},{12,8},{14,10},{16,20},{18,... | collective-permute-start | bytes 1769480 | tf_op jit(solution)/shard_map/ppermute | solution.py:936
  229.9 15.0 %collective-permute-start.24 = (bf16[384,384]{1,0:T(8,128)(2,1)}, bf16[384,384]{1,0:T(8,128)(2,1)S(1)}, u32[]{:S(2)}, u32[]{:S(2)}) collective-permute-start(bf16[384,384]{1,0:T(8,128)(2,1)} %get-tuple-element.259), channel_id=1, source_target_pairs={{0,8},{2,10},{4,12},{6,14},{8,0},{10,2},{12,4},{14,6},{16,24},{18,... | collective-permute-start | bytes 884744 | tf_op jit(solution)/shard_map/ppermute | solution.py:936
  246.1 11.3 %collective-permute-start.26 = (bf16[576,384]{1,0:T(8,128)(2,1)}, bf16[576,384]{1,0:T(8,128)(2,1)S(1)}, u32[]{:S(2)}, u32[]{:S(2)}) collective-permute-start(bf16[576,384]{1,0:T(8,128)(2,1)} %get-tuple-element.255), channel_id=1, source_target_pairs={{0,4},{2,6},{4,0},{6,2},{8,12},{10,14},{12,8},{14,10},{16,20},{18,... | collective-permute-start | bytes 1327112 | tf_op jit(solution)/shard_map/ppermute | solution.py:936
  247.3 16.1 %collective-permute-start.27 = (bf16[384,384]{1,0:T(8,128)(2,1)S(1)}, bf16[384,384]{1,0:T(8,128)(2,1)S(1)}, u32[]{:S(2)}, u32[]{:S(2)}) collective-permute-start(bf16[384,384]{1,0:T(8,128)(2,1)S(1)} %add_convert_fusion.15), channel_id=1, source_target_pairs={{0,16},{2,18},{4,20},{6,22},{8,24},{10,26},{12,28},{14,30},{16,0},... | collective-permute-start | bytes 884744 | tf_op jit(solution)/shard_map/ppermute | solution.py:936
  263.5 18.7 %collective-permute-start.30 = (bf16[2,256,768]{2,1,0:T(8,128)(2,1)S(1)}, bf16[2,256,768]{2,1,0:T(8,128)(2,1)S(1)}, u32[]{:S(2)}, u32[]{:S(2)}) collective-permute-start(bf16[2,256,768]{2,1,0:T(8,128)(2,1)S(1)} %constant_dynamic-slice_fusion.2), channel_id=1, source_target_pairs={{0,1},{1,0},{2,3},{3,2},{4,5},{5,4},{6,7},{7,6},{8,9},{9,8},{10,11... | collective-permute-start | bytes 2359304 | tf_op jit(solution)/shard_map/ppermute | solution.py:933
  264.5 13.3 %collective-permute-start.28 = (bf16[288,384]{1,0:T(8,128)(2,1)S(1)}, bf16[288,384]{1,0:T(8,128)(2,1)S(1)}, u32[]{:S(2)}, u32[]{:S(2)}) collective-permute-start(bf16[288,384]{1,0:T(8,128)(2,1)S(1)} %get-tuple-element.263), channel_id=1, source_target_pairs={{0,8},{2,10},{4,12},{6,14},{8,0},{10,2},{12,4},{14,6},{16,24},{18,... | collective-permute-start | bytes 663560 | tf_op jit(solution)/shard_map/ppermute | solution.py:936
  264.5 13.7 %collective-permute-start.29 = (bf16[384,384]{1,0:T(8,128)(2,1)S(1)}, bf16[384,384]{1,0:T(8,128)(2,1)S(1)}, u32[]{:S(2)}, u32[]{:S(2)}) collective-permute-start(bf16[384,384]{1,0:T(8,128)(2,1)S(1)} %add_convert_fusion.14), channel_id=1, source_target_pairs={{0,8},{2,10},{4,12},{6,14},{8,0},{10,2},{12,4},{14,6},{16,24},{18,... | collective-permute-start | bytes 884744 | tf_op jit(solution)/shard_map/ppermute | solution.py:936
  277.8 12.8 %collective-permute-start.31 = (bf16[288,384]{1,0:T(8,128)(2,1)S(1)}, bf16[288,384]{1,0:T(8,128)(2,1)S(1)}, u32[]{:S(2)}, u32[]{:S(2)}) collective-permute-start(bf16[288,384]{1,0:T(8,128)(2,1)S(1)} %add_convert_fusion.23), channel_id=1, source_target_pairs={{0,16},{2,18},{4,20},{6,22},{8,24},{10,26},{12,28},{14,30},{16,0},... | collective-permute-start | bytes 663560 | tf_op jit(solution)/shard_map/ppermute | solution.py:936
  293.7 15.0 %collective-permute-start.39 = (bf16[768,384]{1,0:T(8,128)(2,1)S(1)}, bf16[768,384]{1,0:T(8,128)(2,1)}, u32[]{:S(2)}, u32[]{:S(2)}) collective-permute-start(bf16[768,384]{1,0:T(8,128)(2,1)S(1)} %maximum_select_fusion.5.refs_0_), channel_id=1, source_target_pairs={{0,4},{2,6},{4,0},{6,2},{8,12},{10,14},{12,8},{14,10},{16,20},{18,... | collective-permute-start | bytes 1769480 | tf_op jit(solution)/shard_map/ppermute | solution.py:936
  309.9 11.2 %collective-permute-start.41 = (bf16[240,384]{1,0:T(8,128)(2,1)S(1)}, bf16[240,384]{1,0:T(8,128)(2,1)S(1)}, u32[]{:S(2)}, u32[]{:S(2)}) collective-permute-start(bf16[240,384]{1,0:T(8,128)(2,1)S(1)} %add_convert_fusion.28), channel_id=1, source_target_pairs={{0,16},{2,18},{4,20},{6,22},{8,24},{10,26},{12,28},{14,30},{16,0},... | collective-permute-start | bytes 552968 | tf_op jit(solution)/shard_map/ppermute | solution.py:936
  310.8 12.3 %collective-permute-start.42 = (bf16[576,384]{1,0:T(8,128)(2,1)S(1)}, bf16[576,384]{1,0:T(8,128)(2,1)S(1)}, u32[]{:S(2)}, u32[]{:S(2)}) collective-permute-start(bf16[576,384]{1,0:T(8,128)(2,1)S(1)} %maximum_select_fusion.6.refs_0_), channel_id=1, source_target_pairs={{0,2},{2,0},{4,6},{6,4},{8,10},{10,8},{12,14},{14,12},{16,18},{18,... | collective-permute-start | bytes 1327112 | tf_op jit(solution)/shard_map/ppermute | solution.py:936
  311.2 17.2 %collective-permute-start.45 = (bf16[576,384]{1,0:T(8,128)(2,1)S(1)}, bf16[576,384]{1,0:T(8,128)(2,1)S(1)}, u32[]{:S(2)}, u32[]{:S(2)}) collective-permute-start(bf16[576,384]{1,0:T(8,128)(2,1)S(1)} %maximum_select_fusion.6.refs_0_), channel_id=1, source_target_pairs={{0,4},{2,6},{4,0},{6,2},{8,12},{10,14},{12,8},{14,10},{16,20},{18,... | collective-permute-start | bytes 1327112 | tf_op jit(solution)/shard_map/ppermute | solution.py:936
  311.9 22.4 %collective-permute-start.44 = (bf16[2,256,768]{2,1,0:T(8,128)(2,1)S(1)}, bf16[2,256,768]{2,1,0:T(8,128)(2,1)S(1)}, u32[]{:S(2)}, u32[]{:S(2)}) collective-permute-start(bf16[2,256,768]{2,1,0:T(8,128)(2,1)S(1)} %constant_dynamic-slice_fusion.1), channel_id=1, source_target_pairs={{0,1},{1,0},{2,3},{3,2},{4,5},{5,4},{6,7},{7,6},{8,9},{9,8},{10,11... | collective-permute-start | bytes 2359304 | tf_op jit(solution)/shard_map/ppermute | solution.py:933
  (55 other events, 332.8 us)

commit v3 on v2

--- a/solution.py
+++ b/solution.py
@@ -67,12 +67,26 @@
     return jnp.where((turn & 2) == 0, value, -value)
 
 
-def bias_kernel(len_ref, box_ref, rel_ref, freq_ref, out_ref, map_ref, feat_ref, line, maps, tabs, cols, *, tile, rows):
+def window_length(meta_ref, w, windows):
+    return meta_ref[4 + meta_ref[1] * windows + w]
+
+
+def position(index, half, length):
+    shifted = index + half * (length // 2)
+    return jnp.where(shifted >= length, shifted - length, shifted)
+
+
+def bias_kernel(meta_ref, own_ref, other_ref, rel_ref, freq_ref, out_ref, map_ref, feat_ref, line, maps, tabs, cols, *, rows):
     length = out_ref.shape[3]
+    windows = other_ref.shape[1]
     blocks = length // 128
     span = (2 * blocks - 1) * 128
     w = pl.program_id(0)
     it = pl.program_id(1)
+    half = meta_ref[1]
+
+    def box_row(m):
+        return jnp.concatenate([own_ref[m, pl.ds(half * windows + w, 1), :], other_ref[m, pl.ds(w, 1), :]], 1)
 
     @pl.when((w == 0) & (it == 0))
     def _():
@@ -85,25 +99,25 @@
                 first = (t[n : n + 1, :] + ROUND) - ROUND
                 tabs[3 * hp + kind : 3 * hp + kind + 1, :] = first + t[n + 1 : n + 2, :] * SMALL
 
-        mpos = lax.broadcasted_iota(jnp.int32, (8, span), 1) - (length - 128)
-        ipos = lax.broadcasted_iota(jnp.int32, (8, span), 0)
+        mpos = lax.broadcasted_iota(jnp.int32, (32, span), 1) - (length - 128)
+        ipos = lax.broadcasted_iota(jnp.int32, (32, span), 0)
 
         def body(g, carry):
-            sl = pl.ds(pl.multiple_of(g * 8, 8), 8)
-            index = bucket_of(mpos - (ipos + g * 8), 0)
-            for hp in range(H // 2):
-                table = jnp.broadcast_to(tabs[3 * hp : 3 * hp + 1, :], (8, 128))
-                for c in range(0, span, 128):
+            sl = pl.ds(pl.multiple_of(g * 32, 32), 32)
+            index = bucket_of(mpos - (ipos + g * 32), 0)
+            for c in range(0, span, 128):
+                for hp in range(H // 2):
+                    table = jnp.broadcast_to(tabs[3 * hp : 3 * hp + 1, :], (32, 128))
                     a, b = unpack(look_up(table, index[:, c : c + 128]))
                     line[2 * hp, sl, c : c + 128] = a
                     line[2 * hp + 1, sl, c : c + 128] = b
             return carry
 
-        lax.fori_loop(0, 16, body, 0)
+        lax.fori_loop(0, 4, body, 0)
 
     @pl.when(it == 0)
     def _():
-        coords = jnp.concatenate([box_ref[m, pl.ds(w, 1), :] for m in range(4)] * 2, 0).astype(F32)
+        coords = jnp.concatenate([box_row(m) for m in range(4)] * 2, 0).astype(F32)
         by_token = coords.T
         cols[:, 0:8] = by_token
         lane = lax.broadcasted_iota(jnp.int32, (1, BOXF), 1)
@@ -115,54 +129,53 @@
         )
         feat_ref[...] = sine(coord * freq_ref[0:1, :], (lane >> 4) & 1).astype(BF)
 
-    dead = lax.broadcasted_iota(jnp.int32, (1, length), 1) >= len_ref[w]
-    first = it * tile
-    line_lane = (length - 128) - (first // 128) * 128
-    line_row = first % 128
-    here = cols[pl.ds(pl.multiple_of(first, tile), tile), 0:8].astype(jnp.int32)
+    place = position(lax.broadcasted_iota(jnp.int32, (1, length), 1), half, length)
+    dead = place >= window_length(meta_ref, w, windows)
+    first = it * 128
+    here = cols[pl.ds(pl.multiple_of(first, 128), 128), 0:8].astype(jnp.int32)
     for t in range(2):
-        index = bucket_of(box_ref[t, pl.ds(w, 1), :] - here[:, t : t + 1], 2)
+        index = bucket_of(box_row(t) - here[:, t : t + 1], 2)
         map_ref[0, t] = index.astype(BF)
         maps[t] = index
 
-    def body(g, carry):
-        sl = pl.ds(pl.multiple_of(g * rows, rows), rows)
-        ls = pl.ds(pl.multiple_of(line_row + g * rows, rows), rows)
-        for hp in range(H // 2):
-            ta = jnp.broadcast_to(tabs[3 * hp + 1 : 3 * hp + 2, :], (rows, 128))
-            td = jnp.broadcast_to(tabs[3 * hp + 2 : 3 * hp + 3, :], (rows, 128))
-            for c in range(0, length, 128):
-                cs = slice(c, c + 128)
-                lc = pl.ds(pl.multiple_of(line_lane + c, 128), 128)
-                a, b = unpack(look_up(ta, maps[0, sl, cs]) + look_up(td, maps[1, sl, cs]))
-                a = jnp.where(dead[:, cs], -1e9 * LOG2E, a + line[2 * hp, ls, lc])
-                b = jnp.where(dead[:, cs], -1e9 * LOG2E, b + line[2 * hp + 1, ls, lc])
-                out_ref[0, 2 * hp, sl, cs] = a.astype(BF)
-                out_ref[0, 2 * hp + 1, sl, cs] = b.astype(BF)
-        return carry
-
-    lax.fori_loop(0, tile // rows, body, 0)
-
-
-def score_bias(lengths, boxes, rel_tables):
-    _, windows, length = boxes.shape
-    tile, rows = 64, 32
+    def block_of(n):
+        return lax.rem(n + half * (blocks // 2), blocks)
+
+    for r in range(0, 128, rows):
+        rs = slice(r, r + rows)
+        for n in range(blocks):
+            cs = slice(n * 128, (n + 1) * 128)
+            lc = pl.ds(pl.multiple_of((blocks - 1 + block_of(n) - block_of(it)) * 128, 128), 128)
+            ia, idown = maps[0, rs, cs], maps[1, rs, cs]
+            for hp in range(H // 2):
+                ta = jnp.broadcast_to(tabs[3 * hp + 1 : 3 * hp + 2, :], (rows, 128))
+                td = jnp.broadcast_to(tabs[3 * hp + 2 : 3 * hp + 3, :], (rows, 128))
+                a, b = unpack(look_up(ta, ia) + look_up(td, idown))
+                a = jnp.where(dead[:, cs], -1e9 * LOG2E, a + line[2 * hp, rs, lc])
+                b = jnp.where(dead[:, cs], -1e9 * LOG2E, b + line[2 * hp + 1, rs, lc])
+                out_ref[0, 2 * hp, rs, cs] = a.astype(BF)
+                out_ref[0, 2 * hp + 1, rs, cs] = b.astype(BF)
+
+
+def score_bias(meta, own, other, rel_tables):
+    windows, length = other.shape[1], 2 * other.shape[2]
     span = (2 * (length // 128) - 1) * 128
     freq_count = BOXF // 8
     freqs = np.float32(1000.0) ** (-np.arange(freq_count, dtype=np.float32) / np.float32(freq_count))
     freqs = jnp.asarray(np.tile(freqs.astype(np.float32), (8, 8)))
     return pl.pallas_call(
-        partial(bias_kernel, tile=tile, rows=rows),
-        grid=(windows, length // tile),
+        partial(bias_kernel, rows=128),
+        grid=(windows, length // 128),
         in_specs=[
             pl.BlockSpec(memory_space=pltpu.SMEM),
-            pl.BlockSpec((4, windows, length), lambda w, i: (0, 0, 0)),
+            pl.BlockSpec(own.shape, lambda w, i: (0, 0, 0)),
+            pl.BlockSpec(other.shape, lambda w, i: (0, 0, 0)),
             pl.BlockSpec((NB, 3 * H), lambda w, i: (0, 0)),
             pl.BlockSpec((8, BOXF), lambda w, i: (0, 0)),
         ],
         out_specs=[
-            pl.BlockSpec((1, H, tile, length), lambda w, i: (w, 0, i, 0)),
-            pl.BlockSpec((1, 2, tile, length), lambda w, i: (w, 0, i, 0)),
+            pl.BlockSpec((1, H, 128, length), lambda w, i: (w, 0, i, 0)),
+            pl.BlockSpec((1, 2, 128, length), lambda w, i: (w, 0, i, 0)),
             pl.BlockSpec((length, BOXF), lambda w, i: (w, 0)),
         ],
         out_shape=[
@@ -172,20 +185,21 @@
         ],
         scratch_shapes=[
             pltpu.VMEM((H, 128, span), F32),
-            pltpu.VMEM((2, tile, length), jnp.int32),
+            pltpu.VMEM((2, 128, length), jnp.int32),
             pltpu.VMEM((3 * H // 2 + 6, 128), F32),
             pltpu.VMEM((length, 128), F32),
         ],
         compiler_params=pltpu.CompilerParams(vmem_limit_bytes=VMEM),
         cost_estimate=SHORT,
         name="score_bias",
-    )(lengths, boxes, rel_tables, freqs)
-
-
-def attend_kernel(len_ref, q_ref, k_ref, v_ref, b_ref, o_ref, e_ref, r_ref, *, chunk):
+    )(meta, own, other, rel_tables, freqs)
+
+
+def attend_kernel(meta_ref, q_ref, k_ref, v_ref, b_ref, o_ref, e_ref, r_ref, *, chunk):
     length = q_ref.shape[0]
     lane = lax.broadcasted_iota(jnp.int32, (length, 128), 1)
-    live = lax.broadcasted_iota(jnp.int32, (length, 128), 0) < len_ref[pl.program_id(0)]
+    place = position(lax.broadcasted_iota(jnp.int32, (length, 128), 0), meta_ref[1], length)
+    live = place < window_length(meta_ref, pl.program_id(0), pl.num_programs(0))
     zero, one = jnp.zeros((), BF), jnp.ones((), BF)
     q, k, v = q_ref[...], k_ref[...], v_ref[...]
     outs = []
@@ -203,7 +217,7 @@
     o_ref[...] = (jnp.where(lane < DH, outs[0], outs[1]) * r).astype(BF)
 
 
-def attend(lengths, qkv, bias):
+def attend(meta, qkv, bias):
     windows, _, length, _ = bias.shape
     pairs = H // 2
     col = lambda off: pl.BlockSpec((length, 128), lambda w, h: (w, off + h))
@@ -222,10 +236,10 @@
         compiler_params=pltpu.CompilerParams(vmem_limit_bytes=VMEM),
         cost_estimate=SHORT,
         name="attend",
-    )(lengths, qkv, qkv, qkv, bias)
-
-
-def attend_back_kernel(q_ref, k_ref, v_ref, e_ref, r_ref, o_ref, do_ref, *refs, chunk):
+    )(meta, qkv, qkv, qkv, bias)
+
+
+def attend_back_kernel(meta_ref, q_ref, k_ref, v_ref, e_ref, r_ref, o_ref, do_ref, *refs, chunk):
     d_ref, ds_ref, line_ref, sum_ref = refs[-4:]
     length = q_ref.shape[0]
     blocks = length // 128
@@ -245,21 +259,20 @@
         for c in range(0, length, chunk):
             e = e_ref[0, h, c : c + chunk, :].astype(F32)
             ds_ref[0, h, c : c + chunk, :] = (e * (dp[c : c + chunk] - center[c : c + chunk])).astype(BF)
-        for d in range(2 * blocks - 1):
-            total = None
-            for ib in range(blocks):
-                jb = d - (blocks - 1) + ib
-                if 0 <= jb < blocks:
-                    part = ds_ref[0, h, ib * 128 : (ib + 1) * 128, jb * 128 : (jb + 1) * 128].astype(F32)
-                    total = part if total is None else total + part
-
-            @pl.when(w == 0)
+        for half in range(2):
+            at = lambda n: (n + half * blocks // 2) % blocks
+
+            @pl.when(meta_ref[1] == half)
             def _():
-                line_ref[h, :, d * 128 : (d + 1) * 128] = total
-
-            @pl.when(w != 0)
-            def _():
-                line_ref[h, :, d * 128 : (d + 1) * 128] += total
+                for d in range(2 * blocks - 1):
+                    cols = slice(d * 128, (d + 1) * 128)
+                    total = jnp.where(w == 0, 0.0, line_ref[h, :, cols])
+                    for ib in range(blocks):
+                        for jb in range(blocks):
+                            if at(jb) - at(ib) + blocks - 1 == d:
+                                rows = slice(ib * 128, (ib + 1) * 128)
+                                total = total + ds_ref[0, h, rows, jb * 128 : (jb + 1) * 128].astype(F32)
+                    line_ref[h, :, cols] = total
 
         ds = ds_ref[0, h]
         part = dot(ds, jnp.where(mine, k, zero))
@@ -275,7 +288,7 @@
         sum_ref[:, cols] = jnp.where(w == 0, sums, sum_ref[:, cols] + sums)
 
 
-def attend_back(qkv, e, r, o, do, first, count, total, at, before=None):
+def attend_back(meta, qkv, e, r, o, do, first, count, total, at, before=None):
     windows, _, length, _ = e.shape
     pairs = H // 2
     col = lambda off: pl.BlockSpec((length, 128), lambda h, w: (w, off + h))
@@ -285,7 +298,8 @@
     return pl.pallas_call(
         partial(attend_back_kernel, chunk=64),
         grid=(count, windows),
-        in_specs=[col(first), col(pairs + first), col(2 * pairs + first), sq, col(first), col(first), col(first)]
+        in_specs=[pl.BlockSpec(memory_space=pltpu.SMEM)]
+        + [col(first), col(pairs + first), col(2 * pairs + first), sq, col(first), col(first), col(first)]
         + [pl.BlockSpec(memory_space=pl.ANY)] * len(more),
         out_specs=[
             pl.BlockSpec((length, 384), lambda h, w: (w, at + h)),
@@ -299,11 +313,11 @@
             jax.ShapeDtypeStruct((2 * count, 128, span), F32),
             jax.ShapeDtypeStruct((8, count * 384), F32),
         ],
-        input_output_aliases={7: 0} if more else {},
+        input_output_aliases={8: 0} if more else {},
         compiler_params=pltpu.CompilerParams(vmem_limit_bytes=VMEM),
         cost_estimate=SHORT,
         name="attend_back",
-    )(qkv, qkv, qkv, e, r, o, do, *more)
+    )(meta, qkv, qkv, qkv, e, r, o, do, *more)
 
 
 def spread(refs, rows, stride):
@@ -428,13 +442,23 @@
     return jnp.sum(x, 0, keepdims=True)
 
 
-def front_kernel(hid_ref, f_ref, box_ref, w_ref, qv_ref, low_ref, out_ref):
+def tokens_of(own_ref, other_ref, chunk):
+    windows, local, _ = other_ref.shape
+    step = min(chunk, local)
+    for w in range(windows):
+        for n, ref in enumerate((own_ref, other_ref)):
+            for c in range(0, local, step):
+                yield slice((2 * w + n) * local + c, (2 * w + n) * local + c + step), ref[w, c : c + step, :]
+
+
+def front_kernel(meta_ref, own_ref, other_ref, f_ref, box_ref, w_ref, qv_ref, low_ref, out_ref):
     step = pl.program_id(0)
     third = pl.num_programs(0) // 3
 
     @pl.when(step == 0)
     def _():
-        low_ref[...] = (hid_ref[...].astype(F32) + dot(f_ref[...], box_ref[...])).astype(BF)
+        for cs, x in tokens_of(own_ref, other_ref, 256):
+            low_ref[cs, :] = (x.astype(F32) + dot(f_ref[cs, :], box_ref[...])).astype(BF)
 
     wide = out_ref.shape[1]
     cols = pl.ds(pl.multiple_of(lax.rem(step, third) * wide, wide), wide)
@@ -442,37 +466,44 @@
     out_ref[...] = (dot(low_ref[...], w_ref[...]) + shift).astype(BF)
 
 
-def front(hidden, features, box_weight, qkv_weight, qv_bias):
-    tokens, width = hidden.shape
+def front(meta, own, other, features, box_weight, qkv_weight, qv_bias):
+    windows, local, width = other.shape
+    tokens = 2 * windows * local
     cols = qkv_weight.shape[1]
-    whole = lambda x: pl.BlockSpec(x.shape, lambda n: (0, 0))
+    whole = lambda x: pl.BlockSpec(x.shape, lambda n, p: (0,) * len(x.shape))
     return pl.pallas_call(
         front_kernel,
-        grid=(cols // width,),
-        in_specs=[
-            whole(hidden),
-            whole(features),
-            whole(box_weight),
-            pl.BlockSpec((width, width), lambda n: (0, n)),
-            whole(qv_bias),
-        ],
-        out_specs=[whole(hidden), pl.BlockSpec((tokens, width), lambda n: (0, n))],
+        grid_spec=pltpu.PrefetchScalarGridSpec(
+            num_scalar_prefetch=1,
+            grid=(cols // width,),
+            in_specs=[
+                pl.BlockSpec(other.shape, lambda n, p: (p[1], 0, 0)),
+                whole(other),
+                whole(features),
+                whole(box_weight),
+                pl.BlockSpec((width, width), lambda n, p: (0, n)),
+                whole(qv_bias),
+            ],
+            out_specs=[
+                pl.BlockSpec((tokens, width), lambda n, p: (0, 0)),
+                pl.BlockSpec((tokens, width), lambda n, p: (0, n)),
+            ],
+        ),
         out_shape=[jax.ShapeDtypeStruct((tokens, width), BF), jax.ShapeDtypeStruct((tokens, cols), BF)],
         compiler_params=pltpu.CompilerParams(vmem_limit_bytes=VMEM),
         cost_estimate=SHORT,
         name="front",
-    )(hidden, features, box_weight, qkv_weight, qv_bias)
-
-
-def feed_kernel(hid_ref, f_ref, box_ref, att_ref, wo_ref, bo_ref, n1_ref, w1_ref, b1_ref, w2_ref, b2_ref, n2_ref, cot_ref, z_ref, low_ref, act_ref, slope_ref, out_ref, dlow_ref, sum_ref, acc, *, chunk):
+    )(meta, own, other, features, box_weight, qkv_weight, qv_bias)
+
+
+def feed_kernel(meta_ref, own_ref, other_ref, f_ref, box_ref, att_ref, wo_ref, bo_ref, n1_ref, w1_ref, b1_ref, w2_ref, b2_ref, n2_ref, cot_own_ref, cot_other_ref, z_ref, low_ref, act_ref, slope_ref, out_own_ref, out_other_ref, dlow_ref, sum_ref, acc, *, chunk):
     step = pl.program_id(0)
     tokens = low_ref.shape[0]
 
     @pl.when(step == 0)
     def _():
-        for c in range(0, tokens, chunk):
-            cs = slice(c, c + chunk)
-            entry = hid_ref[cs, :].astype(F32) + dot(f_ref[cs, :], box_ref[...])
+        for cs, x in tokens_of(own_ref, other_ref, chunk):
+            entry = x.astype(F32) + dot(f_ref[cs, :], box_ref[...])
             z = entry + (dot(att_ref[cs, :], wo_ref[...]) + bo_ref[...])
             second = norm_forward(z, n1_ref[...])[0]
             z_ref[cs, :] = z.astype(BF)
@@ -490,59 +521,68 @@
     @pl.when(step == pl.num_programs(0) - 1)
     def _():
         sums = [0.0, 0.0, 0.0]
-        for c in range(0, tokens, 128):
-            cs = slice(c, c + 128)
+        local = cot_other_ref.shape[1]
+        for cs, x in tokens_of(cot_own_ref, cot_other_ref, 128):
             result, normed, inverse = norm_forward(acc[cs, :] + b2_ref[...], n2_ref[...])
-            out_ref[cs, :] = result.astype(BF)
-            up = cot_ref[cs, :].astype(F32)
+            place = cs.start % local
+            out = (out_own_ref, out_other_ref)[cs.start // local % 2]
+            out[cs.start // local // 2, place : place + 128, :] = result.astype(BF)
+            up = x.astype(F32)
             low = norm_backward(up, normed, inverse, n2_ref[...]).astype(BF)
             dlow_ref[cs, :] = low
             sums = [sums[0] + column_sums(up * normed), sums[1] + column_sums(up), sums[2] + column_sums(low.astype(F32))]
         sum_ref[...] = jnp.concatenate(sums + [jnp.zeros((5, sums[0].shape[1]), F32)], 0)
 
 
-def feed(hidden, features, box_weight, attended, out_weight, out_bias, norm_one, w1, b1, w2, b2, norm_two, cotangent):
-    tokens, width = hidden.shape
+def feed(meta, own, other, features, box_weight, attended, out_weight, out_bias, norm_one, w1, b1, w2, b2, norm_two, cot_own, cot_other):
+    tokens, width = attended.shape
     inner = w1.shape[1]
     tile = 512
-    whole = lambda shape: pl.BlockSpec(shape, lambda n: (0, 0))
+    whole = lambda shape: pl.BlockSpec(shape, lambda n, p: (0,) * len(shape))
+    mine = pl.BlockSpec(other.shape, lambda n, p: (p[1], 0, 0))
     full = whole((tokens, width))
-    part = pl.BlockSpec((tokens, tile), lambda n: (0, n))
+    part = pl.BlockSpec((tokens, tile), lambda n, p: (0, n))
     return pl.pallas_call(
         partial(feed_kernel, chunk=256),
-        grid=(inner // tile,),
-        in_specs=[
-            full,
-            whole(features.shape),
-            whole(box_weight.shape),
-            full,
-            whole(out_weight.shape),
-            whole((1, width)),
-            whole((2, width)),
-            pl.BlockSpec((width, tile), lambda n: (0, n)),
-            pl.BlockSpec((1, tile), lambda n: (0, n)),
-            pl.BlockSpec((tile, width), lambda n: (n, 0)),
-            whole((1, width)),
-            whole((2, width)),
-            full,
-        ],
-        out_specs=[full, full, part, part, full, full, whole((8, width))],
+        grid_spec=pltpu.PrefetchScalarGridSpec(
+            num_scalar_prefetch=1,
+            grid=(inner // tile,),
+            in_specs=[
+                mine,
+                whole(other.shape),
+                whole(features.shape),
+                whole(box_weight.shape),
+                full,
+                whole(out_weight.shape),
+                whole((1, width)),
+                whole((2, width)),
+                pl.BlockSpec((width, tile), lambda n, p: (0, n)),
+                pl.BlockSpec((1, tile), lambda n, p: (0, n)),
+                pl.BlockSpec((tile, width), lambda n, p: (n, 0)),
+                whole((1, width)),
+                whole((2, width)),
+                mine,
+                whole(other.shape),
+            ],
+            out_specs=[full, full, part, part, whole(other.shape), whole(other.shape), full, whole((8, width))],
+            scratch_shapes=[pltpu.VMEM((tokens, width), F32)],
+        ),
         out_shape=[
             jax.ShapeDtypeStruct((tokens, width), BF),
             jax.ShapeDtypeStruct((tokens, width), BF),
             jax.ShapeDtypeStruct((tokens, inner), BF),
             jax.ShapeDtypeStruct((tokens, inner), BF),
-            jax.ShapeDtypeStruct((tokens, width), BF),
+            jax.ShapeDtypeStruct(other.shape, BF),
+            jax.ShapeDtypeStruct(other.shape, BF),
             jax.ShapeDtypeStruct((tokens, width), BF),
             jax.ShapeDtypeStruct((8, width), F32),
         ],
-        scratch_shapes=[pltpu.VMEM((tokens, width), F32)],
         compiler_params=pltpu.CompilerParams(vmem_limit_bytes=VMEM),
         cost_estimate=SHORT,
         name="feed",
     )(
-        hidden, features, box_weight, attended, out_weight, out_bias.reshape(1, -1), norm_one,
-        w1, b1.reshape(1, -1), w2, b2.reshape(1, -1), norm_two, cotangent,
+        meta, own, other, features, box_weight, attended, out_weight, out_bias.reshape(1, -1), norm_one,
+        w1, b1.reshape(1, -1), w2, b2.reshape(1, -1), norm_two, cot_own, cot_other,
     )
 
 
@@ -733,14 +773,15 @@
 E_ROWS = 16
 
 
-def last_kernel(place_ref, x_ref, dx_ref, f_ref, df_ref, two_ref, one_ref, in_ref, *refs):
+def last_kernel(place_ref, x_ref, dx_ref, f_ref, own_ref, other_ref, two_ref, one_ref, in_ref, *refs):
     qv_refs, (line_ref, small0_ref, small1_ref), outs = refs[:3], refs[3:6], refs[6:]
     mine = place_ref[0] == 0
     upper = place_ref[1] == 0
     width = x_ref.shape[1]
     middle = width // 2
     x = dot(x_ref[...], dx_ref[...], 0, 0).astype(BF)
-    box = dot(f_ref[...], df_ref[...], 0, 0).astype(BF)
+    entry = jnp.concatenate([ref[w] for w in range(own_ref.shape[0]) for ref in (own_ref, other_ref)], 0)
+    box = dot(f_ref[...], entry, 0, 0).astype(BF)
     tables = jnp.concatenate([line_ref[...], small0_ref[...] + small1_ref[...], jnp.zeros((16, NB), F32)], 1).T
     blocks = [ref[0:1, p : p + UNIT] for ref in qv_refs for p in range(0, ref.shape[1], UNIT)]
     qv = [jnp.concatenate([y[:, at : at + 128] for y in blocks], 1) for at in (0, 256)]
@@ -781,18 +822,18 @@
         outs[2 + m][...] = jnp.where(mine, rows[:, :middle], rows[:, middle:])
 
 
-def last_grads(place, x, dx, f, df, *sums):
+def last_grads(place, x, dx, f, own, other, *sums):
     rows = (x.shape[1] + f.shape[1]) // 4 + E_ROWS
     vmem = pl.BlockSpec(memory_space=pltpu.VMEM)
     return pl.pallas_call(
         last_kernel,
-        in_specs=[pl.BlockSpec(memory_space=pltpu.SMEM)] + [vmem] * (4 + len(sums)),
+        in_specs=[pl.BlockSpec(memory_space=pltpu.SMEM)] + [vmem] * (5 + len(sums)),
         out_specs=[vmem] * 4,
         out_shape=[jax.ShapeDtypeStruct((2 * rows, UNIT), BF)] * 4,
         compiler_params=pltpu.CompilerParams(vmem_limit_bytes=VMEM),
         cost_estimate=SHORT,
         name="last_grads",
-    )(place, x, dx, f, df, *sums)
+    )(place, x, dx, f, own, other, *sums)
 
 
 def lay_kernel(place_ref, *refs, kind, rows):
@@ -879,23 +920,27 @@
     )(place, *pieces)
 
 
-def entry_kernel(a_ref, b_ref, w_ref, sum_ref, out_ref):
+def entry_kernel(a_ref, b_ref, w_ref, sum_ref, own_ref, other_ref):
     pairs = H // 2
     weight = jnp.concatenate([w_ref[:, (m * pairs + n) * 128 : (m * pairs + n + 1) * 128] for n in range(pairs) for m in range(3)], 1)
     both = jnp.concatenate([a_ref[...], b_ref[...]], 1)
-    out_ref[...] = (sum_ref[...].astype(F32) + dot(both, weight, 1, 1)).astype(BF)
-
-
-def entry_grad(first, last, weight, base):
+    out = (sum_ref[...].astype(F32) + dot(both, weight, 1, 1)).astype(BF)
+    local = own_ref.shape[1]
+    own_ref[0] = out[:local]
+    other_ref[0] = out[local:]
+
+
+def entry_grad(first, last, weight, base, windows):
     tokens, width = base.shape
-    tile = tokens // 2
+    tile = tokens // windows
     row = lambda x: pl.BlockSpec((tile, x.shape[1]), lambda i: (i, 0))
+    out = pl.BlockSpec((1, tile // 2, width), lambda i: (i, 0, 0))
     return pl.pallas_call(
         entry_kernel,
-        grid=(tokens // tile,),
+        grid=(windows,),
         in_specs=[row(first), row(last), pl.BlockSpec(weight.shape, lambda i: (0, 0)), row(base)],
-        out_specs=row(base),
-        out_shape=jax.ShapeDtypeStruct((tokens, width), BF),
+        out_specs=[out, out],
+        out_shape=[jax.ShapeDtypeStruct((windows, tile // 2, width), BF)] * 2,
         compiler_params=pltpu.CompilerParams(vmem_limit_bytes=VMEM),
         cost_estimate=SHORT,
         name="entry_grad",
@@ -936,36 +981,28 @@
         return lax.ppermute(x, "doc", [(i, i ^ (1 << bit)) for i in range(docs)])
 
     def part(x, index, axis):
+        if isinstance(x, list):
+            return jnp.where(index == 0, *x)
         size = x.shape[axis] // 2
         return lax.dynamic_slice_in_dim(x, index * size, size, axis)
 
     def ordered(index, mine, other, axis):
         return jnp.where(index == 0, jnp.concatenate([mine, other], axis), jnp.concatenate([other, mine], axis))
 
-    def whole_windows(x, axis):
-        return ordered(half, part(x, half, axis), swap_half(part(x, 1 - half, axis)), axis + 1)
-
-    def half_positions(x):
-        return ordered(half, part(x, half, 1), swap_half(part(x, 1 - half, 1)), 0)
-
-    def add(x, y):
-        return (x.astype(F32) + y.astype(F32)).astype(BF)
-
     def tie(x, *others):
         return lax.optimization_barrier((x,) + others)[0]
 
-    box_part = swap_half(part(boxes, 1 - half, 1))
-    my_boxes = ordered(half, part(boxes, half, 1), box_part, 2)
-    my_lengths = part(lengths, half, 0)
-    hidden_send = part(tie(hidden_in, box_part), 1 - half, 0)
-    hidden = ordered(half, part(hidden_in, half, 0), swap_half(hidden_send), 1).reshape(tokens, width)
-
-    bias, maps, features = score_bias(my_lengths, my_boxes, rel_tables)
-    upstream = whole_windows(tie(cotangent, maps), 0).reshape(tokens, width)
-    entry_low, qkv = front(hidden, features, box_weight, qkv_weight, qv_bias)
-    attended, e, r = attend(my_lengths, qkv, bias)
-    z_one, second_low, active, slope, result, d_outer, sums_two = feed(
-        hidden,
+    meta = jnp.concatenate([jnp.stack([core, half, side, (doc >> 2) & 1]).astype(jnp.int32), lengths])
+    box_other = swap_half(part(boxes, 1 - half, 1))
+    hidden_other = swap_half(part(tie(hidden_in, box_other), 1 - half, 0))
+    bias, maps, features = score_bias(meta, boxes, box_other, rel_tables)
+    cot_other = swap_half(part(tie(cotangent, maps), 1 - half, 0))
+    entry_low, qkv = front(meta, hidden_in, hidden_other, features, box_weight, qkv_weight, qv_bias)
+    attended, e, r = attend(meta, qkv, bias)
+    z_one, second_low, active, slope, out_mine, out_send, d_outer, sums_two = feed(
+        meta,
+        hidden_in,
+        hidden_other,
         features,
         box_weight,
         attended,
@@ -977,14 +1014,15 @@
         ffn_out_weight,
         ffn_out_bias,
         norm_two,
-        upstream,
+        cotangent,
+        cot_other,
     )
 
     pairs, early = H // 2, H // 3
     late_pairs = pairs - early
     step = early // 2
     more = list(range(2, docs.bit_length() - 1))
-    place = jnp.stack([core, half, side, (doc >> 2) & 1]).astype(jnp.int32)
+    place = meta
     last = [None]
 
     def now(x):
@@ -1011,6 +1049,11 @@
             pieces = [swap_doc(x, 0) for x in pieces]
             self.own = [keep, pieces[:count], keep_own, pieces[count:]]
 
+        def half_later(self):
+            keep, come, keep_own, come_own = self.own
+            send = then(total(now(keep), joined(come)))
+            self.own = [keep_own, come_own, swap_half(send)]
+
         def half(self):
             keep, come, keep_own, come_own = self.own
             keep, keep_own = lax.optimization_barrier((keep, keep_own) + last[0])[:2]
@@ -1050,7 +1093,7 @@
             return [now(self.mine), self.beside, self.across, swap_doc(now(self.across), 0)]
 
     def back(first, count, total_pairs, at, before):
-        out = attend_back(qkv, e, r, attended, now(d_attended), first, count, total_pairs, at, before)
+        out = attend_back(meta, qkv, e, r, attended, now(d_attended), first, count, total_pairs, at, before)
         then(out[0])
         return out
 
@@ -1058,7 +1101,7 @@
     block_rows = width // 4
     then(d_outer)
     a.core(*long_grads(place, active, now(d_outer)))
-    a.half()
+    a.half_later()
     d_inner, sums_in, d_branch, d_attended, sums_one = feed_back(
         now(d_outer), ffn_in_weight, ffn_out_weight, slope, z_one, norm_one, out_weight
     )
@@ -1082,12 +1125,11 @@
     a.settle(a.across)
     b.double(more[1:])
     c.split(1)
-    d_entry_low = then(entry_grad(first_right, now(last_right), qkv_weight, d_branch))
+    grad_mine, grad_send = entry_grad(first_right, now(last_right), qkv_weight, d_branch, windows)
+    then(grad_send)
     c.split(more[0])
     b.back(more[0])
-    d_entry = d_entry_low.reshape(windows, length, width)
-    grad_send = then(part(now(d_entry), 1 - half, 1))
-    grad_mine, grad_other = part(d_entry, half, 1), swap_half(grad_send)
+    grad_other = swap_half(grad_send)
     small_1 = table_grads([ds_0, ds_1, now(ds_2)], [], maps, 1)[0]
     for w in range(2, windows):
         small_1 = small_1 + table_grads([ds_0, ds_1, ds_2], [], maps, w)[0]
@@ -1097,7 +1139,7 @@
     then(*last[0], grad_other)
     d.core(
         *last_grads(
-            place, entry_low, last_right, features, now(d_entry_low), sums_two, sums_one, sums_in, qv_0, qv_1, qv_2, line_grad, small_0, small_1
+            place, entry_low, last_right, features, now(grad_mine), grad_send, sums_two, sums_one, sums_in, qv_0, qv_1, qv_2, line_grad, small_0, small_1
         )
     )
     c.back(more[0])
@@ -1105,9 +1147,7 @@
     (ffn_out_grad,) = lay(place, a.pieces(), "long", block_rows)
     then(ffn_out_grad)
     d.split(more[0])
-    result = result.reshape(windows, length, width)
-    out_send = then(part(now(result), 1 - half, 1))
-    out_mine, out_other = part(result, half, 1), swap_half(out_send)
+    out_other = swap_half(now(out_send))
     c.gather()
     b.settle()
     d.double(more[1:])

time: 347 us -> 336 us (0.968)
  starting transfers between devices: 38.3 us -> 46.9 us
  other arithmetic: 23.1 us -> 15.4 us
  waiting for transfers between devices: 41.3 us -> 33.8 us
  Pallas kernels: 229 us -> 223 us
    ppermute x41, starting transfers between devices: 29.8 us -> 38.2 us  [swap_doc(): return lax.ppermute(x, 'doc', [(i, i ^ 1 << bit) for i in range(docs)])]
    ppermute x41, waiting for transfers between devices: 34 us -> 26.5 us  [swap_doc(): return lax.ppermute(x, 'doc', [(i, i ^ 1 << bit) for i in range(docs)])]
    select_n x8 -> x5, other arithmetic: 10 us -> 3.33 us  [ordered(): jnp.where(index == 0, jnp.concatenate([mine, other], axis), jnp.concatena...]
    pallas_call x4, Pallas kernels: 80.8 us -> 76.1 us  [the longest x1 33.3 us: feed(): pl.pallas_call(partial(feed_kernel, chunk=256), grid_spec=pltpu.PrefetchS...]
    convert_element_type x24 -> x23, other arithmetic: 12.5 us -> 12.1 us  [total(): return out.astype(BF)]
  transfers between devices with their start and end apart: 50 -> 50, of which waited for: 17 -> 15; matrix products, arithmetic and copies ran while one was open for 6% -> 4% of each run, Pallas kernels for 50% -> 50%
where the time goes in v3:
time: 336 us; the launch traced here: 330 us
  Pallas kernels  223 us (66%)
  starting transfers between devices  46.9 us (14%)
  waiting for transfers between devices  33.8 us (10%)
  other arithmetic  15.4 us (5%)
  local copies, waits for them, and re-layouts  8.65 us (3%)
    ppermute x41, starting transfers between devices, swap_doc(): return lax.ppermute(x, 'doc', [(i, i ^ 1 << bit) for i in range(docs)])  38.2 us
    pallas_call x1, Pallas kernels, feed(): pl.pallas_call(partial(feed_kernel, chunk=256), grid_spec=pltpu.PrefetchS...  33.3 us
    pallas_call x3, Pallas kernels, attend_back(): pl.pallas_call(partial(attend_back_kernel, chunk=64), grid=(count, window...  31.2 us
    ppermute x41, waiting for transfers between devices, swap_doc(): return lax.ppermute(x, 'doc', [(i, i ^ 1 << bit) for i in range(docs)])  26.5 us
    pallas_call x2, Pallas kernels, table_grads(): pl.pallas_call(partial(table_kernel, parts=parts, with_line=bool(lines)),...  26.1 us
    pallas_call x1, Pallas kernels, score_bias(): pl.pallas_call(partial(bias_kernel, rows=128), grid=(windows, length // 1...  25.5 us
    pallas_call x1, Pallas kernels, feed_back(): pl.pallas_call(partial(feed_back_kernel, chunk=256), grid=(inner // tile,...  22.6 us
    pallas_call x2, Pallas kernels, wide_grads(): pl.pallas_call(partial(wide_grads_kernel, counts=counts), grid_spec=pltpu...  20.2 us
  transfers between devices with their start and end apart: 50, of which 15 were waited for; matrix products, arithmetic and copies ran while one was open for 4% of the time, Pallas kernels for 50%

profile of v3, /device:TPU:1, one launch (start us, length us, event | category | flops | bytes accessed | tf_op | source)
XLA Modules:
  0.0 329.8 jit_solution(8378821070692825206)
XLA Ops:
  7.3 25.5 %score_bias.1 = (bf16[2,12,512,512]{3,2,1,0:T(8,128)(2,1)}, bf16[2,2,512,512]{3,2,1,0:T(8,128)(2,1)}, bf16[1024,128]{1,0:T(8,128)(2,1)}) custom-call(s32[8]{0:T(128)} %concatenate.48.meta_ref.place_ref, s32[4,4,256]{2,1,0:T(4,128)} %own_ref.3, s32[4,2,256]{2,1,0:T(2,128)} %copy-done.20, f32[32,36]{1,0:T(8,128)} %rel_ref.1, f32[8,128]{1,0:T(8,128)} %constant.34.clone.freq_ref), custom_call_target="tpu_custom_call" | custom-call | flops 1 | bytes 1 | tf_op jit(solution)/shard_map/score_bias/pallas_call | solution.py:166
  35.2 9.0 %front.1 = (bf16[1024,768]{1,0:T(8,128)(2,1)}, bf16[1024,2304]{1,0:T(8,128)(2,1)}) custom-call(s32[8]{0:T(128)} %concatenate.48.meta_ref.place_ref, bf16[4,256,768]{2,1,0:T(8,128)(2,1)} %own_ref.5, bf16[2,256,768]{2,1,0:T(8,128)(2,1)} %copy-done.1, bf16[1024,128]{1,0:T(8,128)(2,1)} %get-tuple-element.134.f_ref, bf16[128,768]{1,0:T(8,128)(2,1)} %box_ref.3, ...), custom_call_target="tpu_custom_call" | custom-call | flops 1 | bytes 1 | tf_op jit(solution)/shard_map/front/pallas_call | solution.py:474
  44.2 18.8 %attend.1 = (bf16[1024,768]{1,0:T(8,128)(2,1)}, bf16[2,12,512,512]{3,2,1,0:T(8,128)(2,1)}, f32[1024,768]{1,0:T(8,128)}) custom-call(s32[8]{0:T(128)} %concatenate.48.meta_ref.place_ref, bf16[1024,2304]{1,0:T(8,128)(2,1)} %get-tuple-element.135.q_ref.k_ref.v_ref, bf16[1024,2304]{1,0:T(8,128)(2,1)} %get-tuple-element.135.q_ref.k_ref.v_ref, ...), custom_call_target="tpu_custom_call" | custom-call | flops 1 | bytes 1 | tf_op jit(solution)/shard_map/attend/pallas_call | solution.py:226
  63.9 33.3 %feed.1 = (bf16[1024,768]{1,0:T(8,128)(2,1)}, bf16[1024,768]{1,0:T(8,128)(2,1)}, bf16[1024,3072]{1,0:T(8,128)(2,1)}, bf16[1024,3072]{1,0:T(8,128)(2,1)}, bf16[2,...) custom-call(s32[8]{0:T(128)} %concatenate.48.meta_ref.place_ref, ...), custom_call_target="tpu_custom_call" | custom-call | flops 1 | bytes 1 | tf_op jit(solution)/shard_map/feed/pallas_call | solution.py:545
  97.2 10.9 %long_grads.1 = (bf16[768,384]{1,0:T(8,128)(2,1)}, bf16[768,384]{1,0:T(8,128)(2,1)}, bf16[768,384]{1,0:T(8,128)(2,1)}, bf16[768,384]{1,0:T(8,128)(2,1)}, bf16[15...) custom-call(s32[8]{0:T(128)} %concatenate.48.meta_ref.place_ref, bf16[1024,3072]{1,0:T(8,128)(2,1)} %get-tuple-element.145.left_ref, ...), custom_call_target="tpu_custom_call" | custom-call | flops 1 | bytes 1 | tf_op jit(solution)/shard_map/long_grads/pallas_call | solution.py:754
  116.7 22.6 %feed_back.1 = (bf16[1024,3072]{1,0:T(8,128)(2,1)}, f32[8,3072]{1,0:T(8,128)}, bf16[1024,768]{1,0:T(8,128)(2,1)}, bf16[1024,768]{1,0:T(8,128)(2,1)}, f32[8,768]{1,0:T(8,128)}) custom-call(bf16[1024,768]{1,0:T(8,128)(2,1)} %get-tuple-element.152.send_ref.keep_ref.dlow_ref, bf16[768,3072]{1,0:T(8,128)(2,1)} %w1_ref.3, bf16[3072,768]{1,0:T(8,128)(2,1)} %w2_ref.3, ...), custom_call_target="tpu_custom_call" | custom-call | flops 1 | bytes 1 | tf_op jit(solution)/shard_map/feed_back/pallas_call | solution.py:630
  144.6 10.2 %wide_grads.2 = (bf16[1,4,192,384]{3,2,1,0:T(8,128)(2,1)}, bf16[1,4,192,384]{3,2,1,0:T(8,128)(2,1)}, bf16[1,4,192,384]{3,2,1,0:T(8,128)(2,1)}, bf16[1,4,192,384]...) custom-call(s32[8]{0:T(128)} %concatenate.48.meta_ref.place_ref, ...), custom_call_target="tpu_custom_call" | custom-call | flops 1 | bytes 1 | tf_op jit(solution)/shard_map/wide_grads/pallas_call | solution.py:716
  161.1 10.3 %attend_back.3 = (bf16[1024,1536]{1,0:T(8,128)(2,1)}, bf16[2,4,512,512]{3,2,1,0:T(8,128)(2,1)}, f32[4,128,896]{2,1,0:T(8,128)}, f32[8,768]{1,0:T(8,128)}) custom-call(s32[8]{0:T(128)} %concatenate.48.meta_ref.place_ref, bf16[1024,2304]{1,0:T(8,128)(2,1)} %get-tuple-element.135.q_ref.k_ref.v_ref, bf16[1024,2304]{1,0:T(8,128)(2,1)} %get-tuple-element.135.q_ref.k_ref.v_ref, ...), custom_call_target="tpu_custom_call" | custom-call | flops 1 | bytes 1 | tf_op jit(solution)/shard_map/attend_back/pallas_call | solution.py:298
  173.8 10.6 %attend_back.4 = (bf16[1024,1536]{1,0:T(8,128)(2,1)}, bf16[2,4,512,512]{3,2,1,0:T(8,128)(2,1)}, f32[4,128,896]{2,1,0:T(8,128)}, f32[8,768]{1,0:T(8,128)}) custom-call(s32[8]{0:T(128)} %concatenate.48.meta_ref.place_ref, bf16[1024,2304]{1,0:T(8,128)(2,1)} %get-tuple-element.135.q_ref.k_ref.v_ref, ...), custom_call_target="tpu_custom_call", output_to_operand_aliasing={{0}: (8, {})} | custom-call | flops 1 | bytes 1 | tf_op jit(solution)/shard_map/attend_back/pallas_call | solution.py:298
  187.8 9.9 %wide_grads.3 = (bf16[1,3,192,384]{3,2,1,0:T(8,128)(2,1)}, bf16[1,3,192,384]{3,2,1,0:T(8,128)(2,1)}, bf16[1,3,192,384]{3,2,1,0:T(8,128)(2,1)}, bf16[1,3,192,384]...) custom-call(s32[8]{0:T(128)} %concatenate.48.meta_ref.place_ref, ...), custom_call_target="tpu_custom_call" | custom-call | flops 1 | bytes 1 | tf_op jit(solution)/shard_map/wide_grads/pallas_call | solution.py:716
  205.5 10.3 %attend_back.5 = (bf16[1024,768]{1,0:T(8,128)(2,1)}, bf16[2,4,512,512]{3,2,1,0:T(8,128)(2,1)}, f32[4,128,896]{2,1,0:T(8,128)}, f32[8,768]{1,0:T(8,128)}) custom-call(s32[8]{0:T(128)} %concatenate.48.meta_ref.place_ref, bf16[1024,2304]{1,0:T(8,128)(2,1)} %get-tuple-element.135.q_ref.k_ref.v_ref, bf16[1024,2304]{1,0:T(8,128)(2,1)} %get-tuple-element.135.q_ref.k_ref.v_ref, ...), custom_call_target="tpu_custom_call" | custom-call | flops 1 | bytes 1 | tf_op jit(solution)/shard_map/attend_back/pallas_call | solution.py:298
  218.8 14.4 %table_grads.2 = (f32[16,64]{1,0:T(8,128)}, f32[16,32]{1,0:T(8,128)}) custom-call(bf16[2,4,512,512]{3,2,1,0:T(8,128)(2,1)} %get-tuple-element.192.refs_0_, bf16[2,4,512,512]{3,2,1,0:T(8,128)(2,1)} %get-tuple-element.193.refs_1_, bf16[2,4,512,512]{3,2,1,0:T(8,128)(2,1)} %get-tuple-element.207.refs_2_, f32[4,128,896]{2,1,0:T(8,128)} %get-tuple-element.196.refs_3_, ...), custom_call_target="tpu_custom_call" | custom-call | flops 1 | bytes 1 | tf_op jit(solution)/shard_map/table_grads/pallas_call | solution.py:399
  237.4 8.3 %entry_grad.1 = (bf16[2,256,768]{2,1,0:T(8,128)(2,1)}, bf16[2,256,768]{2,1,0:T(8,128)(2,1)}) custom-call(bf16[1024,1536]{1,0:T(8,128)(2,1)} %get-tuple-element.179.refs_4_.refs_5_.a_ref, bf16[1024,768]{1,0:T(8,128)(2,1)} %get-tuple-element.202.b_ref.dx_ref, bf16[768,2304]{1,0:T(8,128)(2,1)} %w_ref.3, bf16[1024,768]{1,0:T(8,128)(2,1)} %get-tuple-element.156.refs_1_.refs_2_.sum_ref), custom_call_target="tpu_custom_call" | custom-call | flops 1 | bytes 1 | tf_op jit(solution)/shard_map/entry_grad/pallas_call | solution.py:938
  247.0 3.7 %collective-permute-done.27 = bf16[384,384]{1,0:T(8,128)(2,1)S(1)} collective-permute-done((bf16[384,384]{1,0:T(8,128)(2,1)S(1)}, bf16[384,384]{1,0:T(8,128)(2,1)S(1)}, u32[]{:S(2)}, u32[]{:S(2)}) %collective-permute-start.27) | collective-permute-done | bytes 294944 | tf_op jit(solution)/shard_map/ppermute | solution.py:981
  251.0 11.8 %table_grads.3.refs_5_ = f32[16,64]{1,0:T(8,128)} custom-call(bf16[2,4,512,512]{3,2,1,0:T(8,128)(2,1)} %get-tuple-element.192.refs_0_, bf16[2,4,512,512]{3,2,1,0:T(8,128)(2,1)} %get-tuple-element.193.refs_1_, bf16[2,4,512,512]{3,2,1,0:T(8,128)(2,1)} %get-tuple-element.207.refs_2_, bf16[2,2,512,512]{3,2,1,0:T(8,128)(2,1)} %get-tuple-element.138.refs_6_.refs_3_), custom_call_target="tpu_custom_call" | custom-call | flops 1 | bytes 1 | tf_op jit(solution)/shard_map/table_grads/pallas_call | solution.py:399
  262.8 3.2 collective-permute-start.31
  266.2 5.5 %last_grads.1 = (bf16[480,384]{1,0:T(8,128)(2,1)}, bf16[480,384]{1,0:T(8,128)(2,1)}, bf16[480,384]{1,0:T(8,128)(2,1)}, bf16[480,384]{1,0:T(8,128)(2,1)}) custom-call(s32[8]{0:T(128)} %concatenate.48.meta_ref.place_ref, bf16[1024,768]{1,0:T(8,128)(2,1)} %get-tuple-element.141.refs_3_.x_ref, bf16[1024,768]{1,0:T(8,128)(2,1)} %get-tuple-element.202.b_ref.dx_ref, ...), custom_call_target="tpu_custom_call" | custom-call | flops 1 | bytes 1 | tf_op jit(solution)/shard_map/last_grads/pallas_call | solution.py:828
  273.4 2.8 collective-permute-done.31
  281.1 4.0 %lay.3 = f32[1536,768]{1,0:T(8,128)} custom-call(s32[8]{0:T(128)} %concatenate.48.meta_ref.place_ref, bf16[768,384]{1,0:T(8,128)(2,1)} %copy-done.3, bf16[768,384]{1,0:T(8,128)(2,1)} %collective-permute-done.22.refs_1_, bf16[768,384]{1,0:T(8,128)(2,1)} %collective-permute-done.23.refs_2_, bf16[768,384]{1,0:T(8,128)(2,1)} %collective-permute-done.34.refs_3_), custom_call_target="tpu_custom_call" | custom-call | flops 1 | bytes 1 | tf_op jit(solution)/shard_map/lay/pallas_call | solution.py:910
  285.0 4.6 %collective-permute-done.35 = bf16[480,384]{1,0:T(8,128)(2,1)S(1)} collective-permute-done((bf16[480,384]{1,0:T(8,128)(2,1)}, bf16[480,384]{1,0:T(8,128)(2,1)S(1)}, u32[]{:S(2)}, u32[]{:S(2)}) %collective-permute-start.35) | collective-permute-done | bytes 368672 | tf_op jit(solution)/shard_map/ppermute | solution.py:978
  290.0 5.3 %collective-permute-done.38 = bf16[240,384]{1,0:T(8,128)(2,1)S(1)} collective-permute-done((bf16[240,384]{1,0:T(8,128)(2,1)S(1)}, bf16[240,384]{1,0:T(8,128)(2,1)S(1)}, u32[]{:S(2)}, u32[]{:S(2)}) %collective-permute-start.38) | collective-permute-done | bytes 184352 | tf_op jit(solution)/shard_map/ppermute | solution.py:981
  300.6 4.0 %lay.4 = f32[384,3072]{1,0:T(8,128)} custom-call(s32[8]{0:T(128)} %concatenate.48.meta_ref.place_ref, bf16[768,384]{1,0:T(8,128)(2,1)} %copy-done.4, bf16[768,384]{1,0:T(8,128)(2,1)} %copy-done.13, bf16[768,384]{1,0:T(8,128)(2,1)} %collective-permute-done.39.refs_2_, bf16[768,384]{1,0:T(8,128)(2,1)} %copy-done.14), custom_call_target="tpu_custom_call" | custom-call | flops 1 | bytes 1 | tf_op jit(solution)/shard_map/lay/pallas_call | solution.py:910
  304.6 3.6 %collective-permute-done.41 = bf16[240,384]{1,0:T(8,128)(2,1)S(1)} collective-permute-done((bf16[240,384]{1,0:T(8,128)(2,1)S(1)}, bf16[240,384]{1,0:T(8,128)(2,1)S(1)}, u32[]{:S(2)}, u32[]{:S(2)}) %collective-permute-start.41) | collective-permute-done | bytes 184352 | tf_op jit(solution)/shard_map/ppermute | solution.py:981
  325.2 4.1 %lay.5 = (f32[384,768]{1,0:T(8,128)}, f32[384,2304]{1,0:T(8,128)}, f32[64,768]{1,0:T(8,128)}, f32[1,768]{1,0:T(1,128)}, f32[1,768]{1,0:T(1,128)}, /*index=5*/f32...) custom-call(s32[8]{0:T(128)} %concatenate.48.meta_ref.place_ref, ...), custom_call_target="tpu_custom_call" | custom-call | flops 1 | bytes 1 | tf_op jit(solution)/shard_map/lay/pallas_call | solution.py:910
  (174 shorter events, 81.7 us)
Async XLA Ops:
  6.0 28.3 %collective-permute-start.1 = (bf16[2,256,768]{2,1,0:T(8,128)(2,1)S(1)}, bf16[2,256,768]{2,1,0:T(8,128)(2,1)S(1)}, u32[]{:S(2)}, u32[]{:S(2)}) collective-permute-start(bf16[2,256,768]{2,1,0:T(8,128)(2,1)S(1)} %constant_dynamic-slice_fusion.1), channel_id=1, source_target_pairs={{0,1},{1,0},{2,3},{3,2},{4,5},{5,4},{6,7},{7,6},{8,9},{9,8},{10,11... | collective-permute-start | bytes 2359304 | tf_op jit(solution)/shard_map/ppermute | solution.py:978
  32.9 30.1 %collective-permute-start.2 = (bf16[2,256,768]{2,1,0:T(8,128)(2,1)S(1)}, bf16[2,256,768]{2,1,0:T(8,128)(2,1)S(1)}, u32[]{:S(2)}, u32[]{:S(2)}) collective-permute-start(bf16[2,256,768]{2,1,0:T(8,128)(2,1)S(1)} %constant_dynamic-slice_fusion), channel_id=1, source_target_pairs={{0,1},{1,0},{2,3},{3,2},{4,5},{5,4},{6,7},{7,6},{8,9},{9,8},{10,11... | collective-permute-start | bytes 2359304 | tf_op jit(solution)/shard_map/ppermute | solution.py:978
  114.3 27.7 %collective-permute-start.7 = (bf16[1536,384]{1,0:T(8,128)(2,1)S(1)}, bf16[1536,384]{1,0:T(8,128)(2,1)S(1)}, u32[]{:S(2)}, u32[]{:S(2)}) collective-permute-start(bf16[1536,384]{1,0:T(8,128)(2,1)S(1)} %add_convert_fusion.2), channel_id=1, source_target_pairs={{0,1},{1,0},{2,3},{3,2},{4,5},{5,4},{6,7},{7,6},{8,9},{9,8},{10,11... | collective-permute-start | bytes 3538952 | tf_op jit(solution)/shard_map/ppermute | solution.py:978
  116.1 23.3 %collective-permute-start.5 = (bf16[768,384]{1,0:T(8,128)(2,1)}, bf16[768,384]{1,0:T(8,128)(2,1)S(1)}, u32[]{:S(2)}, u32[]{:S(2)}) collective-permute-start(bf16[768,384]{1,0:T(8,128)(2,1)} %get-tuple-element.158), channel_id=1, source_target_pairs={{0,2},{2,0},{4,6},{6,4},{8,10},{10,8},{12,14},{14,12},{16,18},{18,... | collective-permute-start | bytes 1769480 | tf_op jit(solution)/shard_map/ppermute | solution.py:981
  116.7 22.6 %collective-permute-start.6 = (bf16[768,384]{1,0:T(8,128)(2,1)}, bf16[768,384]{1,0:T(8,128)(2,1)S(1)}, u32[]{:S(2)}, u32[]{:S(2)}) collective-permute-start(bf16[768,384]{1,0:T(8,128)(2,1)} %get-tuple-element.159), channel_id=1, source_target_pairs={{0,2},{2,0},{4,6},{6,4},{8,10},{10,8},{12,14},{14,12},{16,18},{18,... | collective-permute-start | bytes 1769480 | tf_op jit(solution)/shard_map/ppermute | solution.py:981
  143.5 14.1 %collective-permute-start.8 = (bf16[768,384]{1,0:T(8,128)(2,1)}, bf16[768,384]{1,0:T(8,128)(2,1)S(1)}, u32[]{:S(2)}, u32[]{:S(2)}) collective-permute-start(bf16[768,384]{1,0:T(8,128)(2,1)} %get-tuple-element.253), channel_id=1, source_target_pairs={{0,4},{2,6},{4,0},{6,2},{8,12},{10,14},{12,8},{14,10},{16,20},{18,... | collective-permute-start | bytes 1769480 | tf_op jit(solution)/shard_map/ppermute | solution.py:981
  157.7 13.7 %collective-permute-start.13 = (bf16[384,384]{1,0:T(8,128)(2,1)S(1)}, bf16[384,384]{1,0:T(8,128)(2,1)S(1)}, u32[]{:S(2)}, u32[]{:S(2)}) collective-permute-start(bf16[384,384]{1,0:T(8,128)(2,1)S(1)} %get-tuple-element.261), channel_id=1, source_target_pairs={{0,8},{2,10},{4,12},{6,14},{8,0},{10,2},{12,4},{14,6},{16,24},{18,... | collective-permute-start | bytes 884744 | tf_op jit(solution)/shard_map/ppermute | solution.py:981
  159.4 27.3 %collective-permute-start.15 = (bf16[1536,384]{1,0:T(8,128)(2,1)S(1)}, bf16[1536,384]{1,0:T(8,128)(2,1)S(1)}, u32[]{:S(2)}, u32[]{:S(2)}) collective-permute-start(bf16[1536,384]{1,0:T(8,128)(2,1)S(1)} %add_convert_fusion.1), channel_id=1, source_target_pairs={{0,1},{1,0},{2,3},{3,2},{4,5},{5,4},{6,7},{7,6},{8,9},{9,8},{10,11... | collective-permute-start | bytes 3538952 | tf_op jit(solution)/shard_map/ppermute | solution.py:978
  171.5 15.1 %collective-permute-start.14 = (bf16[384,384]{1,0:T(8,128)(2,1)S(1)}, bf16[384,384]{1,0:T(8,128)(2,1)S(1)}, u32[]{:S(2)}, u32[]{:S(2)}) collective-permute-start(bf16[384,384]{1,0:T(8,128)(2,1)S(1)} %add_convert_fusion.18), channel_id=1, source_target_pairs={{0,16},{2,18},{4,20},{6,22},{8,24},{10,26},{12,28},{14,30},{16,0},... | collective-permute-start | bytes 884744 | tf_op jit(solution)/shard_map/ppermute | solution.py:981
  199.5 16.3 %collective-permute-start.20 = (bf16[384,384]{1,0:T(8,128)(2,1)S(1)}, bf16[384,384]{1,0:T(8,128)(2,1)S(1)}, u32[]{:S(2)}, u32[]{:S(2)}) collective-permute-start(bf16[384,384]{1,0:T(8,128)(2,1)S(1)} %add_convert_fusion.17), channel_id=1, source_target_pairs={{0,8},{2,10},{4,12},{6,14},{8,0},{10,2},{12,4},{14,6},{16,24},{18,... | collective-permute-start | bytes 884744 | tf_op jit(solution)/shard_map/ppermute | solution.py:981
  200.3 17.7 %collective-permute-start.21 = (bf16[768,384]{1,0:T(8,128)(2,1)}, bf16[768,384]{1,0:T(8,128)(2,1)S(1)}, u32[]{:S(2)}, u32[]{:S(2)}) collective-permute-start(bf16[768,384]{1,0:T(8,128)(2,1)} %get-tuple-element.255), channel_id=1, source_target_pairs={{0,4},{2,6},{4,0},{6,2},{8,12},{10,14},{12,8},{14,10},{16,20},{18,... | collective-permute-start | bytes 1769480 | tf_op jit(solution)/shard_map/ppermute | solution.py:981
  204.0 29.4 %collective-permute-start.25 = (bf16[1152,384]{1,0:T(8,128)(2,1)}, bf16[1152,384]{1,0:T(8,128)(2,1)S(1)}, u32[]{:S(2)}, u32[]{:S(2)}) collective-permute-start(bf16[1152,384]{1,0:T(8,128)(2,1)} %add_convert_fusion.4), channel_id=1, source_target_pairs={{0,1},{1,0},{2,3},{3,2},{4,5},{5,4},{6,7},{7,6},{8,9},{9,8},{10,11... | collective-permute-start | bytes 2654216 | tf_op jit(solution)/shard_map/ppermute | solution.py:978
  216.0 17.2 %collective-permute-start.22 = (bf16[768,384]{1,0:T(8,128)(2,1)S(1)}, bf16[768,384]{1,0:T(8,128)(2,1)}, u32[]{:S(2)}, u32[]{:S(2)}) collective-permute-start(bf16[768,384]{1,0:T(8,128)(2,1)S(1)} %maximum_select_fusion.2.refs_0_), channel_id=1, source_target_pairs={{0,2},{2,0},{4,6},{6,4},{8,10},{10,8},{12,14},{14,12},{16,18},{18,... | collective-permute-start | bytes 1769480 | tf_op jit(solution)/shard_map/ppermute | solution.py:981
  216.8 16.4 %collective-permute-start.23 = (bf16[768,384]{1,0:T(8,128)(2,1)S(1)}, bf16[768,384]{1,0:T(8,128)(2,1)}, u32[]{:S(2)}, u32[]{:S(2)}) collective-permute-start(bf16[768,384]{1,0:T(8,128)(2,1)S(1)} %maximum_select_fusion.2.refs_0_), channel_id=1, source_target_pairs={{0,4},{2,6},{4,0},{6,2},{8,12},{10,14},{12,8},{14,10},{16,20},{18,... | collective-permute-start | bytes 1769480 | tf_op jit(solution)/shard_map/ppermute | solution.py:981
  218.2 15.0 %collective-permute-start.24 = (bf16[384,384]{1,0:T(8,128)(2,1)S(1)}, bf16[384,384]{1,0:T(8,128)(2,1)S(1)}, u32[]{:S(2)}, u32[]{:S(2)}) collective-permute-start(bf16[384,384]{1,0:T(8,128)(2,1)S(1)} %get-tuple-element.259), channel_id=1, source_target_pairs={{0,8},{2,10},{4,12},{6,14},{8,0},{10,2},{12,4},{14,6},{16,24},{18,... | collective-permute-start | bytes 884744 | tf_op jit(solution)/shard_map/ppermute | solution.py:981
  234.8 15.9 %collective-permute-start.27 = (bf16[384,384]{1,0:T(8,128)(2,1)S(1)}, bf16[384,384]{1,0:T(8,128)(2,1)S(1)}, u32[]{:S(2)}, u32[]{:S(2)}) collective-permute-start(bf16[384,384]{1,0:T(8,128)(2,1)S(1)} %add_convert_fusion.14), channel_id=1, source_target_pairs={{0,16},{2,18},{4,20},{6,22},{8,24},{10,26},{12,28},{14,30},{16,0},... | collective-permute-start | bytes 884744 | tf_op jit(solution)/shard_map/ppermute | solution.py:981
  245.7 20.5 %collective-permute-start.30 = (bf16[2,256,768]{2,1,0:T(8,128)(2,1)}, bf16[2,256,768]{2,1,0:T(8,128)(2,1)S(1)}, u32[]{:S(2)}, u32[]{:S(2)}) collective-permute-start(bf16[2,256,768]{2,1,0:T(8,128)(2,1)} %get-tuple-element.204.other_ref), channel_id=1, source_target_pairs={{0,1},{1,0},{2,3},{3,2},{4,5},{5,4},{6,7},{7,6},{8,9},{9,8},{10,11... | collective-permute-start | bytes 2359304 | tf_op jit(solution)/shard_map/ppermute | solution.py:978
  246.1 16.6 %collective-permute-start.28 = (bf16[288,384]{1,0:T(8,128)(2,1)S(1)}, bf16[288,384]{1,0:T(8,128)(2,1)S(1)}, u32[]{:S(2)}, u32[]{:S(2)}) collective-permute-start(bf16[288,384]{1,0:T(8,128)(2,1)S(1)} %get-tuple-element.263), channel_id=1, source_target_pairs={{0,8},{2,10},{4,12},{6,14},{8,0},{10,2},{12,4},{14,6},{16,24},{18,... | collective-permute-start | bytes 663560 | tf_op jit(solution)/shard_map/ppermute | solution.py:981
  250.8 15.2 %collective-permute-start.29 = (bf16[384,384]{1,0:T(8,128)(2,1)S(1)}, bf16[384,384]{1,0:T(8,128)(2,1)S(1)}, u32[]{:S(2)}, u32[]{:S(2)}) collective-permute-start(bf16[384,384]{1,0:T(8,128)(2,1)S(1)} %add_convert_fusion.13), channel_id=1, source_target_pairs={{0,8},{2,10},{4,12},{6,14},{8,0},{10,2},{12,4},{14,6},{16,24},{18,... | collective-permute-start | bytes 884744 | tf_op jit(solution)/shard_map/ppermute | solution.py:981
  262.8 13.4 %collective-permute-start.31 = (bf16[288,384]{1,0:T(8,128)(2,1)S(1)}, bf16[288,384]{1,0:T(8,128)(2,1)S(1)}, u32[]{:S(2)}, u32[]{:S(2)}) collective-permute-start(bf16[288,384]{1,0:T(8,128)(2,1)S(1)} %add_convert_fusion.22), channel_id=1, source_target_pairs={{0,16},{2,18},{4,20},{6,22},{8,24},{10,26},{12,28},{14,30},{16,0},... | collective-permute-start | bytes 663560 | tf_op jit(solution)/shard_map/ppermute | solution.py:981
  279.6 15.7 %collective-permute-start.39 = (bf16[768,384]{1,0:T(8,128)(2,1)S(1)}, bf16[768,384]{1,0:T(8,128)(2,1)}, u32[]{:S(2)}, u32[]{:S(2)}) collective-permute-start(bf16[768,384]{1,0:T(8,128)(2,1)S(1)} %maximum_select_fusion.3.refs_0_), channel_id=1, source_target_pairs={{0,4},{2,6},{4,0},{6,2},{8,12},{10,14},{12,8},{14,10},{16,20},{18,... | collective-permute-start | bytes 1769480 | tf_op jit(solution)/shard_map/ppermute | solution.py:981
  297.9 13.0 %collective-permute-start.42 = (bf16[576,384]{1,0:T(8,128)(2,1)S(1)}, bf16[576,384]{1,0:T(8,128)(2,1)}, u32[]{:S(2)}, u32[]{:S(2)}) collective-permute-start(bf16[576,384]{1,0:T(8,128)(2,1)S(1)} %maximum_select_fusion.4.refs_0_), channel_id=1, source_target_pairs={{0,2},{2,0},{4,6},{6,4},{8,10},{10,8},{12,14},{14,12},{16,18},{18,... | collective-permute-start | bytes 1327112 | tf_op jit(solution)/shard_map/ppermute | solution.py:981
  299.6 22.7 %collective-permute-start.44 = (bf16[2,256,768]{2,1,0:T(8,128)(2,1)}, bf16[2,256,768]{2,1,0:T(8,128)(2,1)S(1)}, u32[]{:S(2)}, u32[]{:S(2)}) collective-permute-start(bf16[2,256,768]{2,1,0:T(8,128)(2,1)} %get-tuple-element.237), channel_id=1, source_target_pairs={{0,1},{1,0},{2,3},{3,2},{4,5},{5,4},{6,7},{7,6},{8,9},{9,8},{10,11... | collective-permute-start | bytes 2359304 | tf_op jit(solution)/shard_map/ppermute | solution.py:978
  311.0 12.8 %collective-permute-start.46 = (bf16[576,384]{1,0:T(8,128)(2,1)}, bf16[576,384]{1,0:T(8,128)(2,1)S(1)}, u32[]{:S(2)}, u32[]{:S(2)}) collective-permute-start(bf16[576,384]{1,0:T(8,128)(2,1)} %collective-permute-done.45.refs_2_), channel_id=1, source_target_pairs={{0,2},{2,0},{4,6},{6,4},{8,10},{10,8},{12,14},{14,12},{16,18},{18,... | collective-permute-start | bytes 1327112 | tf_op jit(solution)/shard_map/ppermute | solution.py:981
  (49 other events, 377.2 us)
